TPU v7x, 32 devices: a whole 2x2x4 slice. The times are simulated.
32 devices in a mesh: rad: 4 (over z), ang: 8 (over y, x, core).
Axes of the slice: x: 2, y: 2, z: 4, core: 2. Of those that a mesh axis runs over, the one named last changes fastest.
Arguments:
- coarse_field: float32 [2, 4, 32, 128], P(None, 'rad', 'ang'), may hold values from -6 to 6
- excite_mid: float32 [2, 8, 4, 32, 128], P(None, None, 'rad', 'ang'), may hold values from -6 to 6
- excite_fine: float32 [2, 8, 8, 64, 256], P(None, None, 'rad', 'ang'), may hold values from -6 to 6
- kernels_mid: float32 [16, 8, 27], replicated, may hold values from -0.875 to 0.875
- noise_mid: float32 [16, 8, 8], replicated, may hold values from -1 to 1
- rows_mid: int32 [4], replicated, may hold values from 0 to 15
- kernels_fine: float32 [16, 8, 27], replicated, may hold values from -0.875 to 0.875
- noise_fine: float32 [16, 8, 8], replicated, may hold values from -1 to 1
- rows_fine: int32 [8], replicated, may hold values from 0 to 15
- emission: float32 [16, 128, 512], P('rad', 'ang'), may hold values from 0.3 to 3
- star_bins: int32 [4, 128, 512], P(None, 'ang'), may hold values from 0 to 15
- star_data: float32 [4, 128, 512], P(None, 'ang'), may hold values from -3 to 3
Outputs:
- grad_coarse: float32 [2, 4, 32, 128], P(None, 'rad', 'ang')
- grad_excite_mid: float32 [2, 8, 4, 32, 128], P(None, None, 'rad', 'ang')
- grad_excite_fine: float32 [2, 8, 8, 64, 256], P(None, None, 'rad', 'ang')
- residual: float32 [2, 4, 128, 512], P(None, None, 'ang')
All inputs are finite; a program needn't handle non-finite values.
Results may differ from a plain program's by a relative error of at most 0.0003.
Values sent between devices are 32-bit elements; how exact they have to be, the bound alone decides.
No kernel may reach another device: no remote copies, remote signals or barrier semaphores. Data moves between devices by JAX's collectives and lax.ppermute only.
A program may use at most 192 MiB of HBM per device.

v0:
```python
import functools
import typing

import jax
import jax.numpy as jnp
from jax import lax
from jax.experimental import pallas as pl
from jax.experimental.pallas import tpu as pltpu
from jax.sharding import PartitionSpec as P

F32 = jnp.float32
BF16 = jnp.bfloat16
VMEM_LIMIT = 48 * 1024 * 1024


class Plan(typing.NamedTuple):
    n: int
    m: int
    s: int
    la: int
    b: int
    stars: int
    w: int
    ra: int
    h: int


def make_plan(mesh, coarse, star_bins):
    n, m = mesh.shape["rad"], mesh.shape["ang"]
    s, rows, la, b = coarse.shape
    w = max(d for d in range(1, min(n, la) + 1) if la % d == 0)
    ra = la // w
    assert rows == 1 and m % 2 == 0 and w % 2 == 0 and (w // 2) * ra >= 2
    return Plan(n, m, s, la, b, star_bins.shape[0], w, ra, n * s)


def forward_rows(g):
    fine = 2 * 2 * g.ra * g.s * 16
    emit = fine + 16 * 4 * g.ra
    mix = emit + g.s * 4 * (2 * g.ra + 2)
    return fine, emit, mix, mix + g.s * 8 * (-(-(g.ra + 4) // 8))


def backward_rows(g):
    excite = 2 * 2 * g.ra * g.s * 16
    resid = excite + 4 * g.s * g.stars * 4 * g.ra
    mid = resid + g.s * 4 * (2 * g.ra + 2)
    coarse = mid + g.s * 8 * (-(-(g.ra + 4) // 8))
    return excite, resid, mid, coarse, coarse + g.s * 8


def pick_columns(length, ways, phase):
    src = lax.broadcasted_iota(jnp.int32, (length * ways, length), 0)
    dst = lax.broadcasted_iota(jnp.int32, (length * ways, length), 1)
    return jnp.where(src == ways * dst + phase, 1.0, 0.0).astype(BF16)


def place_columns(length, ways, phase):
    src = lax.broadcasted_iota(jnp.int32, (length, length * ways), 0)
    dst = lax.broadcasted_iota(jnp.int32, (length, length * ways), 1)
    return jnp.where(dst == ways * src + phase, 1.0, 0.0).astype(BF16)


def thirds(x):
    high = x.astype(BF16)
    rest = x - high.astype(F32)
    middle = rest.astype(BF16)
    return high, middle, (rest - middle.astype(F32)).astype(BF16)


def exact_dot(parts, choice):
    high, middle, low = [jnp.dot(part, choice, preferred_element_type=F32) for part in parts]
    return high + (middle + low)


def along_lanes(x, step):
    if step == 0:
        return x
    size = x.shape[1]
    lane = lax.broadcasted_iota(jnp.int32, x.shape, 1)
    edge = 0 if step > 0 else size - 1
    return jnp.where(lane == edge, 0.0, pltpu.roll(x, step % size, axis=1))


def along_rows(x, step):
    if step == 0:
        return x
    size = x.shape[0]
    row = lax.broadcasted_iota(jnp.int32, x.shape, 0)
    kept = row >= step if step > 0 else row < size + step
    return jnp.where(kept, pltpu.roll(x, step % size, axis=0), 0.0)


def edge_kernel(g, rows_ref, noise_ref, coarse_ref, excite_ref, mix_ref, one_ref, two_ref):
    table = rows_ref[lax.axis_index("rad")]
    even = lax.rem(lax.axis_index("ang"), 2) == 0
    for s in range(g.s):
        for c in range(8):
            total = noise_ref[table, c, 0] * excite_ref[s, 0, 0]
            for j in range(1, 8):
                total = total + noise_ref[table, c, j] * excite_ref[s, j, 0]
            mix_ref[s, c] = total
    for s in range(g.s):
        for t in range(2):
            up, down = coarse_ref[s, 0, g.la - 2 + t : g.la - 1 + t], coarse_ref[s, 0, t : t + 1]
            one_ref[2 * s + t : 2 * s + t + 1] = jnp.where(even, up, down)
            two_ref[2 * s + t : 2 * s + t + 1] = jnp.where(even, down, up)
        for cr in range(2):
            for cb in range(2):
                at = 2 * g.s + 4 * s + 2 * cr + cb
                up, down = mix_ref[s, 4 * cr + 2 + cb, g.la - 1 :], mix_ref[s, 4 * cr + cb, :1]
                one_ref[at : at + 1] = jnp.where(even, up, down)
                two_ref[at : at + 1] = jnp.where(even, down, up)


def scatter_kernel(g, rows_ref, noise_ref, fine_ref, emission_ref, coarse_ref, mix_ref, one_ref, two_ref, *rest):
    out_refs, (raw, split, lit, wide, stage) = rest[: g.n], rest[g.n :]
    me, ang = lax.axis_index("rad"), lax.axis_index("ang")
    b, s_count, la = g.b, g.s, g.la
    for i in range(2):
        table = rows_ref[2 * me + i]
        for s in range(s_count):
            for c in range(8):
                total = noise_ref[table, c, 0] * fine_ref[s, 0, i]
                for j in range(1, 8):
                    total = total + noise_ref[table, c, j] * fine_ref[s, j, i]
                at = ((s * 8 + c) * 2 + i) * 2 * la
                raw[at : at + 2 * la] = total
    parts = thirds(raw[...])
    for phase in range(2):
        split[phase] = exact_dot(parts, pick_columns(b, 2, phase))
    parts = thirds(emission_ref[...].reshape(16 * la, 4 * b))
    for phase in range(4):
        lit[:, phase * b : (phase + 1) * b] = exact_dot(parts, pick_columns(b, 4, phase))

    even = lax.rem(ang, 2) == 0
    before = jnp.where(ang > 0, jnp.where(even, two_ref[...], one_ref[...]), 0.0)
    after = jnp.where(ang < g.m - 1, jnp.where(even, one_ref[...], two_ref[...]), 0.0)
    for s in range(s_count):
        wide[s, :2] = before[2 * s : 2 * s + 2]
        wide[s, 2 : 2 + la] = coarse_ref[s, 0]
        wide[s, 2 + la :] = after[2 * s : 2 * s + 2]

    end_fine, end_emit, end_mix, _ = forward_rows(g)
    for q in range(g.w):
        for phase in range(2):
            for a in range(2 * g.ra):
                for s in range(s_count):
                    at = ((phase * 2 * g.ra + a) * s_count + s) * 16
                    rows = pl.ds(s * 32 * la + 2 * q * g.ra + a, 16, stride=2 * la)
                    stage[q, at : at + 16] = split[phase, rows, :]
        for phase in range(4):
            for f in range(4):
                at = end_fine + (phase * 4 + f) * 4 * g.ra
                rows = slice(f * 4 * la + 4 * q * g.ra, f * 4 * la + 4 * (q + 1) * g.ra)
                stage[q, at : at + 4 * g.ra] = lit[rows, phase * b : (phase + 1) * b]
        for s in range(s_count):
            for row in range(2 * g.ra + 2):
                a, ca = divmod(2 * q * g.ra - 1 + row, 2)
                for cr in range(2):
                    for cb in range(2):
                        at = end_emit + ((s * (2 * g.ra + 2) + row) * 2 + cr) * 2 + cb
                        edge = 2 * s_count + 4 * s + 2 * cr + cb
                        if a < 0:
                            value = before[edge : edge + 1]
                        elif a >= la:
                            value = after[edge : edge + 1]
                        else:
                            value = mix_ref[s, 4 * cr + 2 * ca + cb, a : a + 1]
                        stage[q, at : at + 1] = value
            at = end_mix + 8 * s
            stage[q, at : at + g.ra + 4] = wide[s, q * g.ra : q * g.ra + g.ra + 4]
    for k in range(g.n):
        out_refs[k][...] = stage[jnp.minimum(lax.rem(me + k, g.n), g.w - 1)]


def main_kernel(g, rows_mid, rows_fine, mid_table, fine_table, noise_table, bins_ref, data_ref, *rest):
    in_refs, rest = rest[: g.n], rest[g.n :]
    grad_ref, resid_ref, parent_ref, coarse_out, edge_ref = rest[:5]
    got, fine_in, emit_in, mix_in, coarse_in, weights, spread, coarse_ext, mid_ext, tall = rest[5:]
    me, ang = lax.axis_index("rad"), lax.axis_index("ang")
    n, b, s_count, ra, h = g.n, g.b, g.s, g.ra, g.h
    rows_a = 2 * ra + 2
    spacing = 1.0 / (4 * n)
    worker = jnp.minimum(me, g.w - 1)

    for k in range(n):
        got[lax.rem(me + n - k, n)] = in_refs[k][...]
    end_fine, end_emit, end_mix, _ = forward_rows(g)
    for r in range(n):
        for s in range(s_count):
            sub = r * s_count + s
            for x in range(4 * ra):
                at = (x * s_count + s) * 16
                fine_in[pl.ds(x * 16 * h + sub, 16, stride=h), :] = got[r, at : at + 16]
            emit_in[pl.ds(sub, 64 * ra, stride=h), :] = got[r, end_fine:end_emit]
            at = end_emit + s * 4 * rows_a
            mix_in[pl.ds(sub, 4 * rows_a, stride=h), :] = got[r, at : at + 4 * rows_a]
            at = end_mix + 8 * s
            coarse_in[pl.ds(sub, ra + 4, stride=h), :] = got[r, at : at + ra + 4]

    for r in range(n):
        own = slice(r * s_count, (r + 1) * s_count)
        tables = [mid_table[rows_mid[r]], fine_table[rows_fine[2 * r]], fine_table[rows_fine[2 * r + 1]]]
        for level, table in enumerate(tables):
            for c in range(8):
                weights[level, c, own] = jnp.broadcast_to(table[c : c + 1], (s_count, 27))
    for level in range(3):
        for c in range(8):
            tile = weights[level, c]
            for o in range(27):
                spread[(level * 8 + c) * 27 + o] = jnp.broadcast_to(tile[:, o : o + 1], (h, b))

    first = ang * g.la + worker * ra
    top_in = jnp.where(first > 0, 1.0, 0.0).astype(F32)
    bottom_in = jnp.where(first + ra < g.m * g.la, 1.0, 0.0).astype(F32)
    for a in range(ra + 4):
        x = coarse_in[a * h : (a + 1) * h]
        for db in range(3):
            shifted = along_lanes(x, 1 - db)
            for dr in range(3):
                coarse_ext[dr, a, db] = along_rows(shifted, (1 - dr) * s_count)
    for cr in range(2):
        for row in range(rows_a):
            a, ca = divmod(row - 1, 2)
            for cb in range(2):
                c = 4 * cr + 2 * ca + cb
                at = (row * 4 + 2 * cr + cb) * h
                total = mix_in[at : at + h]
                for dr in range(3):
                    for da in range(3):
                        for db in range(3):
                            o = 9 * dr + 3 * da + db
                            total = total + spread[c * 27 + o] * coarse_ext[dr, a + 1 + da, db]
                if row == 0:
                    total = total * top_in
                if row == rows_a - 1:
                    total = total * bottom_in
                for bi, step_b in ((1 + cb, 0), (3, -1) if cb == 0 else (0, 1)):
                    shifted = along_lanes(total, step_b)
                    for ri, step_r in ((1 + cr, 0), (3, -1) if cr == 0 else (0, 1)):
                        mid_ext[ri, row, bi] = along_rows(shifted, step_r * s_count)

    def fine_cells(c, carry):
        cr, ca, cb = c // 4, lax.rem(c // 2, 2), lax.rem(c, 2)
        for pr in range(2):
            weight = [spread[((1 + pr) * 8 + c) * 27 + o] for o in range(27)]
            for a in range(2 * ra):
                for pb in range(2):
                    at = (((pb * 2 * ra + a) * 8 + c) * 2 + pr) * h
                    total = fine_in[pl.ds(pl.multiple_of(at, 8), h), :]
                    for dr in range(3):
                        for da in range(3):
                            for db in range(3):
                                o = 9 * dr + 3 * da + db
                                total = total + weight[o] * mid_ext[pr + dr, a + da, pb + db]
                    grad_ref[2 * pr + cr, 2 * a + ca, 2 * pb + cb] = total
        return carry

    lax.fori_loop(0, 8, fine_cells, 0)

    radial = 4 * (lax.broadcasted_iota(jnp.int32, (h, b), 0) // s_count)

    def sum_before(x):
        step = s_count
        while step < h:
            x = x + along_rows(x, step)
            step *= 2
        return along_rows(x, s_count)

    def sum_all(x):
        step = s_count
        while step < h:
            x = x + pltpu.roll(x, step, axis=0)
            step *= 2
        return x

    def position(at, carry):
        a, pb = at // 4, lax.rem(at, 4)
        density = [jnp.exp(grad_ref[f, a, pb]) for f in range(4)]
        layer = [spacing * d for d in density]
        depth = sum_before(layer[0] + layer[1] + layer[2] + layer[3])
        glow = []
        for f in range(4):
            where_emit = pl.multiple_of(((pb * 4 + f) * 4 * ra + a) * h, 8)
            glow.append(spacing * emit_in[pl.ds(where_emit, h), :] * jnp.exp(-depth))
            depth = depth + layer[f]
        running = sum_before(glow[0] + glow[1] + glow[2] + glow[3])
        column = []
        for f in range(4):
            running = running + glow[f]
            column.append(running)
        total = [jnp.zeros((h, b), F32) for f in range(4)]
        for star in range(g.stars):
            row = (star * 4 * ra + a) * 4 + pb
            bins = jnp.broadcast_to(bins_ref[pl.ds(row, 1), :], (h, b))
            data = jnp.broadcast_to(data_ref[pl.ds(row, 1), :], (h, b))
            bins = bins - radial
            mine = jnp.where(bins == 0, column[0], 0.0)
            for f in range(1, 4):
                mine = jnp.where(bins == f, column[f], mine)
            predicted = sum_all(mine)
            residual = data - predicted
            resid_ref[star, a, pb] = residual
            for f in range(4):
                total[f] = total[f] + jnp.where(bins > f, residual * (predicted - column[f]), 0.0)
        for f in range(4):
            grad_ref[f, a, pb] = -density[f] * total[f]
        return carry

    lax.fori_loop(0, 16 * ra, position, 0)

    tall[...] = jnp.zeros(tall.shape, F32)
    for pr in range(2):
        def gather(c, carry, pr=pr):
            cr, ca, cb = c // 4, lax.rem(c // 2, 2), lax.rem(c, 2)
            cells = {(a, pb): grad_ref[2 * pr + cr, 2 * a + ca, 2 * pb + cb] for a in range(2 * ra) for pb in range(2)}
            for dr in range(3):
                sums = {}
                for da in range(3):
                    for db in range(3):
                        weight = spread[((1 + pr) * 8 + c) * 27 + 9 * dr + 3 * da + db]
                        for (a, pb), cell in cells.items():
                            key = (a + da, pb + db)
                            term = weight * cell
                            sums[key] = sums[key] + term if key in sums else term
                for (row, bi), value in sums.items():
                    tall[pr + dr, row, bi] += value
            return carry

        lax.fori_loop(0, 8, gather, 0)
    for row in range(rows_a):
        for pr in range(2):
            for pb in range(2):
                bi, step_b = (3, 1) if pb == 0 else (0, -1)
                ri, step_r = (3, 1) if pr == 0 else (0, -1)
                near = tall[1 + pr, row, 1 + pb] + along_lanes(tall[1 + pr, row, bi], step_b)
                far = tall[ri, row, 1 + pb] + along_lanes(tall[ri, row, bi], step_b)
                value = near + along_rows(far, step_r * s_count)
                if row == 0:
                    value = value * top_in
                if row == rows_a - 1:
                    value = value * bottom_in
                parent_ref[2 * pr + pb, row] = value

    for a in range(ra + 4):
        coarse_out[a] = jnp.zeros((h, b), F32)
    for dr in range(3):
        for db in range(3):
            sums = {}
            for cr in range(2):
                for row in range(rows_a):
                    a, ca = divmod(row - 1, 2)
                    for cb in range(2):
                        cell = parent_ref[2 * cr + cb, row]
                        for da in range(3):
                            c, o = 4 * cr + 2 * ca + cb, 9 * dr + 3 * da + db
                            term = spread[c * 27 + o] * cell
                            key = a + 1 + da
                            sums[key] = sums[key] + term if key in sums else term
            for a, value in sums.items():
                coarse_out[a] += along_lanes(along_rows(value, (dr - 1) * s_count), db - 1)

    for q in range(g.w):
        @pl.when(worker == q)
        def _(q=q):
            low = q < g.w // 2
            for x in range(4):
                if q == 0 or q == g.w - 1:
                    edge_ref[x] = parent_ref[x, 0 if low else rows_a - 1]
                else:
                    edge_ref[x] = jnp.zeros((h, b), F32)
            for t in range(2):
                a = (t - 2 if low else g.la + t) - q * ra + 2
                if 0 <= a < ra + 4:
                    edge_ref[4 + t] = coarse_out[a]
                else:
                    edge_ref[4 + t] = jnp.zeros((h, b), F32)


def gather_kernel(g, rows_fine, noise_table, grad_ref, resid_ref, parent_ref, coarse_ref, edge_ref, *rest):
    out_refs, (weights, excite, joined, seen, stage) = rest[: g.n], rest[g.n :]
    me, ang = lax.axis_index("rad"), lax.axis_index("ang")
    n, b, s_count, ra, h = g.n, g.b, g.s, g.ra, g.h
    rows_a = 2 * ra + 2
    for r in range(n):
        for i in range(2):
            table = noise_table[rows_fine[2 * r + i]]
            for c in range(8):
                weights[i, c, r * s_count : (r + 1) * s_count] = jnp.broadcast_to(table[c : c + 1], (s_count, 8))
    for i in range(2):
        tiles = [weights[i, c] for c in range(8)]
        for j in range(8):
            weight = [jnp.broadcast_to(tile[:, j : j + 1], (h, b)) for tile in tiles]
            for a in range(2 * ra):
                at = ((a * 8 + j) * 2 + i) * h
                for pb in range(2):
                    total = None
                    for c in range(8):
                        cr, ca, cb = c // 4, c // 2 % 2, c % 2
                        term = weight[c] * grad_ref[2 * i + cr, 2 * a + ca, 2 * pb + cb]
                        total = term if total is None else total + term
                    excite[at : at + h, pb * b : (pb + 1) * b] = total
    order = jnp.concatenate([place_columns(b, 2, phase) for phase in range(2)], axis=0)
    parts = thirds(excite[...])
    for half in range(2):
        joined[half] = exact_dot(parts, order[:, half * b : (half + 1) * b])
    for star in range(g.stars):
        for a in range(4 * ra):
            for pb in range(4):
                for s in range(s_count):
                    row = (s * g.stars + star) * 4 * ra + a
                    seen[row : row + 1, pb * b : (pb + 1) * b] = resid_ref[star, a, pb, s : s + 1]
    order = jnp.concatenate([place_columns(b, 4, phase) for phase in range(4)], axis=0)
    shown = exact_dot(thirds(seen[...]), order)

    live = jnp.where(worker_low(g, me), ang < g.m - 1, ang > 0)
    end_excite, end_resid, end_mid, end_coarse, _ = backward_rows(g)
    per = 4 * g.stars * ra
    parents = parent_ref.reshape(4 * rows_a * h, b)
    coarse = coarse_ref.reshape((ra + 4) * h, b)
    edges = edge_ref.reshape(6 * h, b)
    for r in range(n):
        for s in range(s_count):
            sub = r * s_count + s
            for half in range(2):
                for a in range(2 * ra):
                    at = ((half * 2 * ra + a) * s_count + s) * 16
                    rows = pl.ds(a * 16 * h + sub, 16, stride=h)
                    stage[r, at : at + 16] = joined[half, rows, :]
            for part in range(4):
                at = end_excite + (part * s_count + s) * per
                stage[r, at : at + per] = shown[s * per : (s + 1) * per, part * b : (part + 1) * b]
            at = end_resid + s * 4 * rows_a
            stage[r, at : at + 4 * rows_a] = parents[pl.ds(sub, 4 * rows_a, stride=h), :]
            at = end_mid + 8 * s
            stage[r, at : at + ra + 4] = coarse[pl.ds(sub, ra + 4, stride=h), :]
            at = end_coarse + 8 * s
            stage[r, at : at + 6] = jnp.where(live, edges[pl.ds(sub, 6, stride=h), :], 0.0)
    for k in range(n):
        out_refs[k][...] = stage[lax.rem(me + k, n)]


def worker_low(g, me):
    return jnp.minimum(me, g.w - 1) < g.w // 2


def owner_kernel(g, rows_mid, noise_mid, *rest):
    in_refs, rest = rest[: g.n], rest[g.n :]
    coarse_out, mid_out, fine_out, resid_out, got, fine, grad_mid, grad_coarse = rest
    me = lax.axis_index("rad")
    n, b, s_count, ra, la = g.n, g.b, g.s, g.ra, g.la
    rows_a = 2 * ra + 2
    end_excite, end_resid, end_mid, end_coarse, _ = backward_rows(g)
    per = 4 * g.stars * ra
    for k in range(n):
        got[lax.rem(me + n - k, n)] = in_refs[k][...]
    grad_mid[...] = jnp.zeros(grad_mid.shape, F32)
    grad_coarse[...] = jnp.zeros(grad_coarse.shape, F32)
    for q in range(g.w):
        for s in range(s_count):
            for half in range(2):
                for a in range(2 * ra):
                    at = ((half * 2 * ra + a) * s_count + s) * 16
                    rows = pl.ds(s * 32 * la + 2 * q * ra + a, 16, stride=2 * la)
                    fine[half, rows, :] = got[q, at : at + 16]
            for part in range(4):
                for star in range(g.stars):
                    at = end_excite + (part * s_count + s) * per + star * 4 * ra
                    rows = slice(4 * q * ra, 4 * (q + 1) * ra)
                    resid_out[s, star, rows, part * b : (part + 1) * b] = got[q, at : at + 4 * ra]
            for x in range(4):
                at = end_resid + s * 4 * rows_a + x * rows_a
                grad_mid[s, x, 2 * q * ra : 2 * q * ra + rows_a] += got[q, at : at + rows_a]
                at = end_coarse + 8 * s + x
                row = 2 * la if q < g.w // 2 else 1
                grad_mid[s, x, row : row + 1] += got[q, at : at + 1]
            at = end_mid + 8 * s
            grad_coarse[s, q * ra : q * ra + ra + 4] += got[q, at : at + ra + 4]
            at = end_coarse + 8 * s + 4
            row = la if q < g.w // 2 else 2
            grad_coarse[s, row : row + 2] += got[q, at : at + 2]
    for half in range(2):
        fine_out[..., half * b : (half + 1) * b] = fine[half].reshape(s_count, 8, 2, 2 * la, b)
    table = rows_mid[me]
    for s in range(s_count):
        coarse_out[s, 0] = grad_coarse[s, 2 : 2 + la]
        cells = []
        for c in range(8):
            cr, ca, cb = c // 4, c // 2 % 2, c % 2
            cells.append(grad_mid[s, 2 * cr + cb, pl.ds(1 + ca, la, stride=2), :])
        for j in range(8):
            total = noise_mid[table, 0, j] * cells[0]
            for c in range(1, 8):
                total = total + noise_mid[table, c, j] * cells[c]
            mid_out[s, j, 0] = total


def star_kernel(g, bins_ref, data_ref, bins_out, data_out, gathered):
    worker = jnp.minimum(lax.axis_index("rad"), g.w - 1)
    per, b = 4 * g.ra, g.b
    for q in range(g.w):
        @pl.when(worker == q)
        def _(q=q):
            for star in range(g.stars):
                gathered[0, star * per : (star + 1) * per] = bins_ref[star, q * per : (q + 1) * per].astype(F32)
                gathered[1, star * per : (star + 1) * per] = data_ref[star, q * per : (q + 1) * per]
    bins = gathered[0].astype(BF16)
    parts = thirds(gathered[1])
    for phase in range(4):
        choice = pick_columns(b, 4, phase)
        rows = pl.ds(phase, g.stars * per, stride=4)
        bins_out[rows, :] = jnp.dot(bins, choice, preferred_element_type=F32).astype(jnp.int32)
        data_out[rows, :] = exact_dot(parts, choice)


def call(kernel, name, outs, operands, scratch, scalars):
    smem, vmem = pl.BlockSpec(memory_space=pltpu.SMEM), pl.BlockSpec(memory_space=pltpu.VMEM)
    return pl.pallas_call(
        kernel,
        name=name,
        out_shape=[jax.ShapeDtypeStruct(shape, kind) for shape, kind in outs],
        in_specs=[smem] * scalars + [vmem] * (len(operands) - scalars),
        out_specs=[vmem] * len(outs),
        scratch_shapes=[pltpu.VMEM(shape, F32) for shape in scratch],
        compiler_params=pltpu.CompilerParams(vmem_limit_bytes=VMEM_LIMIT),
    )(*operands)


def per_device(
    g,
    coarse_field,
    excite_mid,
    excite_fine,
    kernels_mid,
    noise_mid,
    rows_mid,
    kernels_fine,
    noise_fine,
    rows_fine,
    emission,
    star_bins,
    star_data,
):
    n, m, s, la, b, stars, w, ra, h = g
    kernel = functools.partial
    pairs = [(i, i ^ 1) for i in range(m)]
    between = [(i, (i + 1) % m if i % 2 else (i - 1) % m) for i in range(m)]

    def around(k):
        return [(i, (i + k) % n) for i in range(n)]

    edge_rows = ((6 * s + 7) // 8 * 8, b)
    mixed, one, two = call(
        kernel(edge_kernel, g),
        "edges",
        [((s, 8, la, b), F32), (edge_rows, F32), (edge_rows, F32)],
        (rows_mid, noise_mid, coarse_field, excite_mid),
        [],
        2,
    )
    one, two = lax.ppermute(one, "ang", pairs), lax.ppermute(two, "ang", between)
    sent = call(
        kernel(scatter_kernel, g),
        "scatter",
        [((forward_rows(g)[-1], b), F32)] * n,
        (rows_fine, noise_fine, excite_fine, emission, coarse_field, mixed, one, two),
        [
            (32 * s * la, 2 * b),
            (2, 32 * s * la, b),
            (16 * la, 4 * b),
            (s, la + 4, b),
            (w, forward_rows(g)[-1], b),
        ],
        2,
    )
    got = [sent[0]] + [lax.ppermute(sent[k], "rad", around(k)) for k in range(1, n)]
    bins, data = call(
        kernel(star_kernel, g),
        "stars",
        [((16 * stars * ra, b), jnp.int32), ((16 * stars * ra, b), F32)],
        (star_bins, star_data),
        [(2, 4 * stars * ra, 4 * b)],
        0,
    )
    rows_a = 2 * ra + 2
    grad, resid, parent, coarse, edge = call(
        kernel(main_kernel, g),
        "main",
        [
            ((4, 4 * ra, 4, h, b), F32),
            ((stars, 4 * ra, 4, h, b), F32),
            ((4, rows_a, h, b), F32),
            ((ra + 4, h, b), F32),
            ((6, h, b), F32),
        ],
        (rows_mid, rows_fine, kernels_mid, kernels_fine, noise_fine, bins, data, *got),
        [
            (n, forward_rows(g)[-1], b),
            (64 * ra * h, b),
            (64 * ra * h, b),
            (4 * rows_a * h, b),
            ((ra + 4) * h, b),
            (3, 8, h, 27),
            (3 * 8 * 27, h, b),
            (3, ra + 4, 3, h, b),
            (4, rows_a, 4, h, b),
            (4, rows_a, 4, h, b),
        ],
        2,
    )
    sideways = [
        (r * m + a, r * m + (a - 1 if min(r, w - 1) < w // 2 else a + 1) % m) for r in range(n) for a in range(m)
    ]
    edge = lax.ppermute(edge, ("rad", "ang"), sideways)
    back = call(
        kernel(gather_kernel, g),
        "gather",
        [((backward_rows(g)[-1], b), F32)] * n,
        (rows_fine, noise_fine, grad, resid, parent, coarse, edge),
        [
            (2, 8, h, 8),
            (32 * ra * h, 2 * b),
            (2, 32 * ra * h, b),
            (4 * stars * ra * s, 4 * b),
            (n, backward_rows(g)[-1], b),
        ],
        1,
    )
    back = [back[0]] + [lax.ppermute(back[k], "rad", around(k)) for k in range(1, n)]
    return tuple(
        call(
            kernel(owner_kernel, g),
            "owner",
            [
                ((s, 1, la, b), F32),
                ((s, 8, 1, la, b), F32),
                ((s, 8, 2, 2 * la, 2 * b), F32),
                ((s, stars, 4 * la, 4 * b), F32),
            ],
            (rows_mid, noise_mid, *back),
            [(n, backward_rows(g)[-1], b), (2, 32 * s * la, b), (s, 4, 2 * la + 2, b), (s, la + 4, b)],
            2,
        )
    )


def solution(mesh):
    placed = (
        P(None, "rad", "ang", None),
        P(None, None, "rad", "ang", None),
        P(None, None, "rad", "ang", None),
        P(),
        P(),
        P(),
        P(),
        P(),
        P(),
        P("rad", "ang", None),
        P(None, "ang", None),
        P(None, "ang", None),
    )

    def local(*args):
        return per_device(make_plan(mesh, args[0], args[10]), *args)

    return jax.shard_map(
        local,
        mesh=mesh,
        in_specs=placed,
        out_specs=(
            P(None, "rad", "ang", None),
            P(None, None, "rad", "ang", None),
            P(None, None, "rad", "ang", None),
            P(None, None, "ang", None),
        ),
        check_vma=False,
    )
```

profile of v0, /device:TPU:11, one launch (start us, length us, event | category | flops | bytes accessed | tf_op | source)
XLA Modules:
  0.0 54.1 jit_solution(1401111923700683334)
XLA Ops:
  0.6 0.0 copy-start.9
  0.6 0.0 copy-start.7
  0.7 0.0 copy-start.6
  0.7 0.0 copy-start
  0.7 0.9 %copy.20.noise_ref.noise_mid = f32[16,8,8]{2,1,0:T(8,128)S(1)} copy(f32[16,8,8]{0,2,1:T(8,128)} %param.16) | data formatting | bytes 8192 | tf_op args[4]
  1.6 1.7 %edges.1 = (f32[2,8,4,128]{3,2,1,0:T(4,128)S(1)}, f32[16,128]{1,0:T(8,128)S(1)}, f32[16,128]{1,0:T(8,128)S(1)}) custom-call(s32[4]{0:T(128)S(1)} %copy-done.9, f32[16,8,8]{2,1,0:T(8,128)S(1)} %copy.20.noise_ref.noise_mid, f32[2,1,4,128]{3,2,1,0:T(4,128)S(1)} %copy-done.7, f32[2,8,1,4,128]{4,3,2,1,0:T(4,128)S(1)} %copy-done.6), custom_call_target="tpu_custom_call" | custom-call | tf_op jit(solution)/shard_map/edges/pallas_call | solution.py:519
  3.3 0.7 %collective-permute-start = (f32[16,128]{1,0:T(8,128)S(1)}, f32[16,128]{1,0:T(8,128)S(1)}, u32[]{:S(2)}, u32[]{:S(2)}) collective-permute-start(f32[16,128]{1,0:T(8,128)S(1)} %get-tuple-element.25), channel_id=1, source_target_pairs={{0,1},{1,0},{2,3},{3,2},{4,5},{5,4},{6,7},{7,6},{8,9},{9,8},{10,11... | collective-permute-start | bytes 24584 | tf_op jit(solution)/shard_map/ppermute | solution.py:562
  4.1 1.2 %collective-permute-start.1 = (f32[16,128]{1,0:T(8,128)S(1)}, f32[16,128]{1,0:T(8,128)S(1)}, u32[]{:S(2)}, u32[]{:S(2)}) collective-permute-start(f32[16,128]{1,0:T(8,128)S(1)} %get-tuple-element.26), channel_id=1, source_target_pairs={{0,7},{1,2},{2,1},{3,4},{4,3},{5,6},{6,5},{7,0},{8,15},{9,10},{10,... | collective-permute-start | bytes 24584 | tf_op jit(solution)/shard_map/ppermute | solution.py:562
  5.2 0.8 %copy.19.noise_ref.noise_table = f32[16,8,8]{2,1,0:T(8,128)S(1)} copy(f32[16,8,8]{0,2,1:T(8,128)} %param.19) | data formatting | bytes 8192 | tf_op args[7]
  6.1 0.0 copy-start.8
  6.1 0.0 collective-permute-done.one_ref
  6.1 1.9 %collective-permute-done.1.two_ref = f32[16,128]{1,0:T(8,128)S(1)} collective-permute-done((f32[16,128]{1,0:T(8,128)S(1)}, f32[16,128]{1,0:T(8,128)S(1)}, u32[]{:S(2)}, u32[]{:S(2)}) %collective-permute-start.1) | collective-permute-done | bytes 8224 | tf_op jit(solution)/shard_map/ppermute | solution.py:562
  8.0 0.9 %copy-done.1 = f32[4,16,512]{2,1,0:T(8,128)S(1)} copy-done((f32[4,16,512]{2,1,0:T(8,128)S(1)}, f32[4,16,512]{2,1,0:T(8,128)}, u32[]{:S(2)}) %copy-start.1) | copy-done | bytes 131096
  8.9 2.4 %scatter.1 = (f32[240,128]{1,0:T(8,128)S(1)}, f32[240,128]{1,0:T(8,128)S(1)}, f32[240,128]{1,0:T(8,128)S(1)}, f32[240,128]{1,0:T(8,128)S(1)}) custom-call(s32[8]{0:T(128)S(1)} %copy-done.8, f32[16,8,8]{2,1,0:T(8,128)S(1)} %copy.19.noise_ref.noise_table, f32[2,8,2,8,256]{4,3,2,1,0:T(8,128)S(1)} %copy-done, f32[4,16,512]{2,1,0:T(8,128)S(1)} %copy-done.1, ...), custom_call_target="tpu_custom_call" | custom-call | tf_op jit(solution)/shard_map/scatter/pallas_call | solution.py:519
  11.4 1.4 %collective-permute-start.2 = (f32[240,128]{1,0:T(8,128)S(1)}, f32[240,128]{1,0:T(8,128)S(1)}, u32[]{:S(2)}, u32[]{:S(2)}) collective-permute-start(f32[240,128]{1,0:T(8,128)S(1)} %get-tuple-element.28), channel_id=1, source_target_pairs={{0,8},{8,16},{16,24},{24,0},{1,9},{9,17},{17,25},{25,1},{2,10},{10... | collective-permute-start | bytes 368648 | tf_op jit(solution)/shard_map/ppermute | solution.py:577
  12.8 1.1 %collective-permute-start.3 = (f32[240,128]{1,0:T(8,128)S(1)}, f32[240,128]{1,0:T(8,128)S(1)}, u32[]{:S(2)}, u32[]{:S(2)}) collective-permute-start(f32[240,128]{1,0:T(8,128)S(1)} %get-tuple-element.29), channel_id=1, source_target_pairs={{0,16},{8,24},{16,0},{24,8},{1,17},{9,25},{17,1},{25,9},{2,18},{10... | collective-permute-start | bytes 368648 | tf_op jit(solution)/shard_map/ppermute | solution.py:577
  13.9 1.4 %collective-permute-start.4 = (f32[240,128]{1,0:T(8,128)S(1)}, f32[240,128]{1,0:T(8,128)S(1)}, u32[]{:S(2)}, u32[]{:S(2)}) collective-permute-start(f32[240,128]{1,0:T(8,128)S(1)} %get-tuple-element.30), channel_id=1, source_target_pairs={{0,24},{8,0},{16,8},{24,16},{1,25},{9,1},{17,9},{25,17},{2,26},{10... | collective-permute-start | bytes 368648 | tf_op jit(solution)/shard_map/ppermute | solution.py:577
  15.2 0.4 stars.1
  15.7 0.5 collective-permute-done.2.rest_1_
  16.2 7.3 %collective-permute-done.3.rest_2_ = f32[240,128]{1,0:T(8,128)S(1)} collective-permute-done((f32[240,128]{1,0:T(8,128)S(1)}, f32[240,128]{1,0:T(8,128)S(1)}, u32[]{:S(2)}, u32[]{:S(2)}) %collective-permute-start.3) | collective-permute-done | bytes 122912 | tf_op jit(solution)/shard_map/ppermute | solution.py:577
  23.4 1.7 %collective-permute-done.4.rest_3_ = f32[240,128]{1,0:T(8,128)S(1)} collective-permute-done((f32[240,128]{1,0:T(8,128)S(1)}, f32[240,128]{1,0:T(8,128)S(1)}, u32[]{:S(2)}, u32[]{:S(2)}) %collective-permute-start.4) | collective-permute-done | bytes 122912 | tf_op jit(solution)/shard_map/ppermute | solution.py:577
  25.1 4.7 %main.1 = (f32[4,4,4,8,128]{4,3,2,1,0:T(8,128)S(1)}, f32[4,4,4,8,128]{4,3,2,1,0:T(8,128)S(1)}, f32[4,4,8,128]{3,2,1,0:T(8,128)S(1)}, f32[5,8,128]{2,1,0:T(8,128)S(1)}, f32[6,8,128]{2,1,0:T(8,128)S(1)}) custom-call(s32[4]{0:T(128)S(1)} %copy-done.9, s32[8]{0:T(128)S(1)} %copy-done.8, f32[16,8,27]{2,1,0:T(8,128)S(1)} %copy-done.4, f32[16,8,27]{2,1,0:T(8,128)S(1)} %copy-done.5, ...), custom_call_target="tpu_custom_call" | custom-call | tf_op jit(solution)/shard_map/main/pallas_call | solution.py:519
  29.8 0.4 collective-permute-start.5
  30.2 3.8 %collective-permute-done.5.edge_ref = f32[6,8,128]{2,1,0:T(8,128)S(1)} collective-permute-done((f32[6,8,128]{2,1,0:T(8,128)S(1)}, f32[6,8,128]{2,1,0:T(8,128)S(1)}, u32[]{:S(2)}, u32[]{:S(2)}) %collective-permute-start.5) | collective-permute-done | bytes 24608 | tf_op jit(solution)/shard_map/ppermute | solution.py:615
  34.0 1.5 %gather.1 = (f32[320,128]{1,0:T(8,128)S(1)}, f32[320,128]{1,0:T(8,128)S(1)}, f32[320,128]{1,0:T(8,128)S(1)}, f32[320,128]{1,0:T(8,128)S(1)}) custom-call(s32[8]{0:T(128)S(1)} %copy-done.8, f32[16,8,8]{2,1,0:T(8,128)S(1)} %copy.19.noise_ref.noise_table, f32[4,4,4,8,128]{4,3,2,1,0:T(8,128)S(1)} %get-tuple-element.31.grad_ref, ...), custom_call_target="tpu_custom_call" | custom-call | tf_op jit(solution)/shard_map/gather/pallas_call | solution.py:519
  35.5 0.1 collective-permute-start.6
  35.6 0.7 %collective-permute-start.7 = (f32[320,128]{1,0:T(8,128)S(1)}, f32[320,128]{1,0:T(8,128)S(1)}, u32[]{:S(2)}, u32[]{:S(2)}) collective-permute-start(f32[320,128]{1,0:T(8,128)S(1)} %get-tuple-element.38), channel_id=1, source_target_pairs={{0,16},{8,24},{16,0},{24,8},{1,17},{9,25},{17,1},{25,9},{2,18},{10... | collective-permute-start | bytes 491528 | tf_op jit(solution)/shard_map/ppermute | solution.py:630
  36.2 0.8 %collective-permute-start.8 = (f32[320,128]{1,0:T(8,128)S(1)}, f32[320,128]{1,0:T(8,128)S(1)}, u32[]{:S(2)}, u32[]{:S(2)}) collective-permute-start(f32[320,128]{1,0:T(8,128)S(1)} %get-tuple-element.39), channel_id=1, source_target_pairs={{0,24},{8,0},{16,8},{24,16},{1,25},{9,1},{17,9},{25,17},{2,26},{10... | collective-permute-start | bytes 491528 | tf_op jit(solution)/shard_map/ppermute | solution.py:630
  37.0 9.4 %collective-permute-done.6.rest_1_ = f32[320,128]{1,0:T(8,128)S(1)} collective-permute-done((f32[320,128]{1,0:T(8,128)S(1)}, f32[320,128]{1,0:T(8,128)S(1)}, u32[]{:S(2)}, u32[]{:S(2)}) %collective-permute-start.6) | collective-permute-done | bytes 163872 | tf_op jit(solution)/shard_map/ppermute | solution.py:630
  46.4 2.9 %collective-permute-done.7.rest_2_ = f32[320,128]{1,0:T(8,128)S(1)} collective-permute-done((f32[320,128]{1,0:T(8,128)S(1)}, f32[320,128]{1,0:T(8,128)S(1)}, u32[]{:S(2)}, u32[]{:S(2)}) %collective-permute-start.7) | collective-permute-done | bytes 163872 | tf_op jit(solution)/shard_map/ppermute | solution.py:630
  49.3 2.1 %collective-permute-done.8.rest_3_ = f32[320,128]{1,0:T(8,128)S(1)} collective-permute-done((f32[320,128]{1,0:T(8,128)S(1)}, f32[320,128]{1,0:T(8,128)S(1)}, u32[]{:S(2)}, u32[]{:S(2)}) %collective-permute-start.8) | collective-permute-done | bytes 163872 | tf_op jit(solution)/shard_map/ppermute | solution.py:630
  51.4 2.7 %owner.1 = (f32[2,1,4,128]{3,2,1,0:T(4,128)}, f32[2,8,1,4,128]{4,3,2,1,0:T(4,128)}, f32[2,8,2,8,256]{4,3,2,1,0:T(8,128)}, f32[2,4,16,512]{3,2,1,0:T(8,128)}) custom-call(s32[4]{0:T(128)S(1)} %copy-done.9, f32[16,8,8]{2,1,0:T(8,128)S(1)} %copy.20.noise_ref.noise_mid, f32[320,128]{1,0:T(8,128)S(1)} %get-tuple-element.36.rest_0_, ...), custom_call_target="tpu_custom_call" | custom-call | tf_op jit(solution)/shard_map/owner/pallas_call | solution.py:519
  (14 shorter events, 0.0 us)
Async XLA Ops:
  0.6 0.9 %copy-start.9 = (s32[4]{0:T(128)S(1)}, s32[4]{0:T(128)}, u32[]{:S(2)}) copy-start(s32[4]{0:T(128)} %rows_mid.3) | copy-start | bytes 52
  0.6 0.9 %copy-start.7 = (f32[2,1,4,128]{3,2,1,0:T(4,128)S(1)}, f32[2,1,4,128]{3,2,1,0:T(4,128)}, u32[]{:S(2)}) copy-start(f32[2,1,4,128]{3,2,1,0:T(4,128)} %coarse_ref.3) | copy-start | bytes 12292
  0.7 0.9 %copy-start.6 = (f32[2,8,1,4,128]{4,3,2,1,0:T(4,128)S(1)}, f32[2,8,1,4,128]{4,3,2,1,0:T(4,128)}, u32[]{:S(2)}) copy-start(f32[2,8,1,4,128]{4,3,2,1,0:T(4,128)} %excite_ref.1) | copy-start | bytes 98308
  0.7 7.4 %copy-start = (f32[2,8,2,8,256]{4,3,2,1,0:T(8,128)S(1)}, f32[2,8,2,8,256]{4,3,2,1,0:T(8,128)}, u32[]{:S(2)}) copy-start(f32[2,8,2,8,256]{4,3,2,1,0:T(8,128)} %fine_ref.1) | copy-start | bytes 786436
  3.3 2.8 %collective-permute-start = (f32[16,128]{1,0:T(8,128)S(1)}, f32[16,128]{1,0:T(8,128)S(1)}, u32[]{:S(2)}, u32[]{:S(2)}) collective-permute-start(f32[16,128]{1,0:T(8,128)S(1)} %get-tuple-element.25), channel_id=1, source_target_pairs={{0,1},{1,0},{2,3},{3,2},{4,5},{5,4},{6,7},{7,6},{8,9},{9,8},{10,11... | collective-permute-start | bytes 24584 | tf_op jit(solution)/shard_map/ppermute | solution.py:562
  4.1 4.0 %collective-permute-start.1 = (f32[16,128]{1,0:T(8,128)S(1)}, f32[16,128]{1,0:T(8,128)S(1)}, u32[]{:S(2)}, u32[]{:S(2)}) collective-permute-start(f32[16,128]{1,0:T(8,128)S(1)} %get-tuple-element.26), channel_id=1, source_target_pairs={{0,7},{1,2},{2,1},{3,4},{4,3},{5,6},{6,5},{7,0},{8,15},{9,10},{10,... | collective-permute-start | bytes 24584 | tf_op jit(solution)/shard_map/ppermute | solution.py:562
  6.1 2.0 %copy-start.8 = (s32[8]{0:T(128)S(1)}, s32[8]{0:T(128)}, u32[]{:S(2)}) copy-start(s32[8]{0:T(128)} %rows_fine.3) | copy-start | bytes 100
  8.0 0.9 %copy-start.1 = (f32[4,16,512]{2,1,0:T(8,128)S(1)}, f32[4,16,512]{2,1,0:T(8,128)}, u32[]{:S(2)}) copy-start(f32[4,16,512]{2,1,0:T(8,128)} %emission_ref.1) | copy-start | bytes 393220
  8.9 6.3 %copy-start.2 = (s32[4,16,512]{2,1,0:T(8,128)S(1)}, s32[4,16,512]{2,1,0:T(8,128)}, u32[]{:S(2)}) copy-start(s32[4,16,512]{2,1,0:T(8,128)} %bins_ref.1) | copy-start | bytes 393220
  8.9 6.3 %copy-start.3 = (f32[4,16,512]{2,1,0:T(8,128)S(1)}, f32[4,16,512]{2,1,0:T(8,128)}, u32[]{:S(2)}) copy-start(f32[4,16,512]{2,1,0:T(8,128)} %data_ref.1) | copy-start | bytes 393220
  11.4 4.8 %collective-permute-start.2 = (f32[240,128]{1,0:T(8,128)S(1)}, f32[240,128]{1,0:T(8,128)S(1)}, u32[]{:S(2)}, u32[]{:S(2)}) collective-permute-start(f32[240,128]{1,0:T(8,128)S(1)} %get-tuple-element.28), channel_id=1, source_target_pairs={{0,8},{8,16},{16,24},{24,0},{1,9},{9,17},{17,25},{25,1},{2,10},{10... | collective-permute-start | bytes 368648 | tf_op jit(solution)/shard_map/ppermute | solution.py:577
  12.8 10.7 %collective-permute-start.3 = (f32[240,128]{1,0:T(8,128)S(1)}, f32[240,128]{1,0:T(8,128)S(1)}, u32[]{:S(2)}, u32[]{:S(2)}) collective-permute-start(f32[240,128]{1,0:T(8,128)S(1)} %get-tuple-element.29), channel_id=1, source_target_pairs={{0,16},{8,24},{16,0},{24,8},{1,17},{9,25},{17,1},{25,9},{2,18},{10... | collective-permute-start | bytes 368648 | tf_op jit(solution)/shard_map/ppermute | solution.py:577
  13.8 11.3 %copy-start.4 = (f32[16,8,27]{2,1,0:T(8,128)S(1)}, f32[16,8,27]{2,1,0:T(8,128)}, u32[]{:S(2)}) copy-start(f32[16,8,27]{2,1,0:T(8,128)} %mid_table.1) | copy-start | bytes 41476
  13.9 11.3 %copy-start.5 = (f32[16,8,27]{2,1,0:T(8,128)S(1)}, f32[16,8,27]{2,1,0:T(8,128)}, u32[]{:S(2)}) copy-start(f32[16,8,27]{2,1,0:T(8,128)} %fine_table.1) | copy-start | bytes 41476
  13.9 11.3 %collective-permute-start.4 = (f32[240,128]{1,0:T(8,128)S(1)}, f32[240,128]{1,0:T(8,128)S(1)}, u32[]{:S(2)}, u32[]{:S(2)}) collective-permute-start(f32[240,128]{1,0:T(8,128)S(1)} %get-tuple-element.30), channel_id=1, source_target_pairs={{0,24},{8,0},{16,8},{24,16},{1,25},{9,1},{17,9},{25,17},{2,26},{10... | collective-permute-start | bytes 368648 | tf_op jit(solution)/shard_map/ppermute | solution.py:577
  29.8 4.2 %collective-permute-start.5 = (f32[6,8,128]{2,1,0:T(8,128)S(1)}, f32[6,8,128]{2,1,0:T(8,128)S(1)}, u32[]{:S(2)}, u32[]{:S(2)}) collective-permute-start(f32[6,8,128]{2,1,0:T(8,128)S(1)} %get-tuple-element.35), channel_id=1, source_target_pairs={{0,7},{1,0},{2,1},{3,2},{4,3},{5,4},{6,5},{7,6},{8,15},{9,8},{10,9... | collective-permute-start | bytes 73736 | tf_op jit(solution)/shard_map/ppermute | solution.py:615
  35.5 10.9 %collective-permute-start.6 = (f32[320,128]{1,0:T(8,128)S(1)}, f32[320,128]{1,0:T(8,128)S(1)}, u32[]{:S(2)}, u32[]{:S(2)}) collective-permute-start(f32[320,128]{1,0:T(8,128)S(1)} %get-tuple-element.37), channel_id=1, source_target_pairs={{0,8},{8,16},{16,24},{24,0},{1,9},{9,17},{17,25},{25,1},{2,10},{10... | collective-permute-start | bytes 491528 | tf_op jit(solution)/shard_map/ppermute | solution.py:630
  35.6 13.8 %collective-permute-start.7 = (f32[320,128]{1,0:T(8,128)S(1)}, f32[320,128]{1,0:T(8,128)S(1)}, u32[]{:S(2)}, u32[]{:S(2)}) collective-permute-start(f32[320,128]{1,0:T(8,128)S(1)} %get-tuple-element.38), channel_id=1, source_target_pairs={{0,16},{8,24},{16,0},{24,8},{1,17},{9,25},{17,1},{25,9},{2,18},{10... | collective-permute-start | bytes 491528 | tf_op jit(solution)/shard_map/ppermute | solution.py:630
  36.2 15.2 %collective-permute-start.8 = (f32[320,128]{1,0:T(8,128)S(1)}, f32[320,128]{1,0:T(8,128)S(1)}, u32[]{:S(2)}, u32[]{:S(2)}) collective-permute-start(f32[320,128]{1,0:T(8,128)S(1)} %get-tuple-element.39), channel_id=1, source_target_pairs={{0,24},{8,0},{16,8},{24,16},{1,25},{9,1},{17,9},{25,17},{2,26},{10... | collective-permute-start | bytes 491528 | tf_op jit(solution)/shard_map/ppermute | solution.py:630
where the time goes:
time: 54.3 us; the launch traced here: 54.1 us
  waiting for transfers between devices  29.5 us (54%)
  Pallas kernels  13.4 us (25%)
  starting transfers between devices  7.71 us (14%)
  local copies, waits for them, and re-layouts  2.67 us (5%)
  between operations  0.76 us (1%)
    ppermute x3, waiting for transfers between devices, per_device(): lax.ppermute(back[k], 'rad', around(k))  14.4 us
    pallas_call x6, Pallas kernels, call(): pl.pallas_call(kernel, name=name, out_shape=[jax.ShapeDtypeStruct(shape,...  13.4 us
    ppermute x3, waiting for transfers between devices, per_device(): lax.ppermute(sent[k], 'rad', around(k))  9.46 us
    ppermute x3, starting transfers between devices, per_device(): lax.ppermute(sent[k], 'rad', around(k))  3.84 us
    ppermute x1, waiting for transfers between devices, per_device(): edge = lax.ppermute(edge, ('rad', 'ang'), sideways)  3.76 us
    unnamed x22, local copies, waits for them, and re-layouts  2.67 us
    ppermute x1, waiting for transfers between devices, per_device(): lax.ppermute(two, 'ang', between)  1.93 us
    ppermute x3, starting transfers between devices, per_device(): lax.ppermute(back[k], 'rad', around(k))  1.51 us
  transfers between devices with their start and end apart: 9, of which 8 were waited for; matrix products, arithmetic and copies ran while one was open for 2% of the time, Pallas kernels for 1%

commit v1 on v0

v1 whole, which is shorter than its diff:
```python
import functools
import typing

import jax
import jax.numpy as jnp
from jax import lax
from jax.experimental import pallas as pl
from jax.experimental.pallas import tpu as pltpu
from jax.sharding import PartitionSpec as P

F32 = jnp.float32
BF16 = jnp.bfloat16
VMEM_LIMIT = 24 * 1024 * 1024


class Plan(typing.NamedTuple):
    n: int
    m: int
    s: int
    la: int
    b: int
    stars: int
    w: int
    ra: int
    h: int


def make_plan(mesh, coarse, star_bins):
    n, m = mesh.shape["rad"], mesh.shape["ang"]
    s, rows, la, b = coarse.shape
    w = max(d for d in range(1, min(n, la) + 1) if la % d == 0)
    ra = la // w
    assert rows == 1 and m % 2 == 0 and w % 2 == 0 and (w // 2) * ra >= 2
    return Plan(n, m, s, la, b, star_bins.shape[0], w, ra, n * s)


def forward_rows(g):
    fine = 2 * 2 * g.ra * g.s * 16
    emit = fine + 16 * 4 * g.ra
    mix = emit + g.s * 4 * (2 * g.ra + 2)
    return fine, emit, mix, -(-(mix + g.s * (g.ra + 4)) // 8) * 8


def backward_rows(g):
    excite = 2 * 2 * g.ra * g.s * 16
    resid = excite + 4 * g.s * g.stars * 4 * g.ra
    mid = resid + g.s * 4 * (2 * g.ra + 2)
    coarse = mid + g.s * (g.ra + 4)
    return excite, resid, mid, coarse, -(-(coarse + 6 * g.s) // 8) * 8


def table_weights(table_ref, entry):
    lane = lax.broadcasted_iota(jnp.int32, table_ref.shape[1:], 1)
    columns = [
        jnp.sum(jnp.where(lane == entry, table_ref[c], 0.0), axis=1, keepdims=True) for c in range(table_ref.shape[0])
    ]
    return lambda c, j: columns[c][j : j + 1]


def fetch(pairs, sems):
    copies = [pltpu.make_async_copy(source, here, sems.at[i]) for i, (source, here) in enumerate(pairs)]
    for copy in copies:
        copy.start()
    for copy in copies:
        copy.wait()


def pick_columns(length, ways, phase):
    src = lax.broadcasted_iota(jnp.int32, (length * ways, length), 0)
    dst = lax.broadcasted_iota(jnp.int32, (length * ways, length), 1)
    return jnp.where(src == ways * dst + phase, 1.0, 0.0).astype(BF16)


def place_columns(length, ways, phase):
    src = lax.broadcasted_iota(jnp.int32, (length, length * ways), 0)
    dst = lax.broadcasted_iota(jnp.int32, (length, length * ways), 1)
    return jnp.where(dst == ways * src + phase, 1.0, 0.0).astype(BF16)


def thirds(x):
    high = x.astype(BF16)
    rest = x - high.astype(F32)
    middle = rest.astype(BF16)
    return high, middle, (rest - middle.astype(F32)).astype(BF16)


def exact_dot(parts, choice):
    high, middle, low = [jnp.dot(part, choice, preferred_element_type=F32) for part in parts]
    return high + (middle + low)


def along_lanes(x, step):
    if step == 0:
        return x
    size = x.shape[1]
    lane = lax.broadcasted_iota(jnp.int32, x.shape, 1)
    edge = 0 if step > 0 else size - 1
    return jnp.where(lane == edge, 0.0, pltpu.roll(x, step % size, axis=1))


def along_rows(x, step):
    if step == 0:
        return x
    size = x.shape[0]
    row = lax.broadcasted_iota(jnp.int32, x.shape, 0)
    kept = row >= step if step > 0 else row < size + step
    return jnp.where(kept, pltpu.roll(x, step % size, axis=0), 0.0)


def edge_kernel(g, rows_hbm, noise_hbm, coarse_hbm, excite_hbm, mix_ref, one_ref, two_ref, *rest):
    rows_ref, noise_ref, coarse_ref, excite_ref, sems = rest
    fetch(
        [(rows_hbm, rows_ref), (noise_hbm, noise_ref), (coarse_hbm, coarse_ref), (excite_hbm, excite_ref)], sems
    )
    even = lax.rem(lax.axis_index("ang"), 2) == 0
    weight = table_weights(noise_ref, rows_ref[lax.axis_index("rad")])
    for c in range(8):
        for s in range(g.s):
            total = weight(c, 0) * excite_ref[s, 0, 0]
            for j in range(1, 8):
                total = total + weight(c, j) * excite_ref[s, j, 0]
            mix_ref[s, c] = total
    for s in range(g.s):
        up, down = coarse_ref[s, 0, g.la - 2 :], coarse_ref[s, 0, :2]
        one_ref[2 * s : 2 * s + 2] = jnp.where(even, up, down)
        two_ref[2 * s : 2 * s + 2] = jnp.where(even, down, up)
        for cr in range(2):
            for cb in range(2):
                at = 2 * g.s + 4 * s + 2 * cr + cb
                up, down = mix_ref[s, 4 * cr + 2 + cb, g.la - 1 :], mix_ref[s, 4 * cr + cb, :1]
                one_ref[at : at + 1] = jnp.where(even, up, down)
                two_ref[at : at + 1] = jnp.where(even, down, up)


def scatter_kernel(g, rows_hbm, noise_hbm, fine_hbm, emission_hbm, coarse_hbm, mix_ref, one_ref, two_ref, *rest):
    out_refs, rest = rest[: g.n], rest[g.n :]
    rows_ref, noise_ref, fine_ref, emission_ref, coarse_ref, sems, raw, split, lit, wide, stage = rest
    fetch(
        [
            (rows_hbm, rows_ref),
            (noise_hbm, noise_ref),
            (coarse_hbm, coarse_ref),
            (fine_hbm, fine_ref),
            (emission_hbm, emission_ref),
        ],
        sems,
    )
    me, ang = lax.axis_index("rad"), lax.axis_index("ang")
    b, s_count, la = g.b, g.s, g.la
    for i in range(2):
        weight = table_weights(noise_ref, rows_ref[2 * me + i])
        for c in range(8):
            weights = [weight(c, j) for j in range(8)]
            for s in range(s_count):
                total = weights[0] * fine_ref[s, 0, i]
                for j in range(1, 8):
                    total = total + weights[j] * fine_ref[s, j, i]
                at = ((s * 8 + c) * 2 + i) * 2 * la
                raw[at : at + 2 * la] = total
    parts = thirds(raw[...])
    for phase in range(2):
        split[phase] = exact_dot(parts, pick_columns(b, 2, phase))
    parts = thirds(emission_ref[...].reshape(16 * la, 4 * b))
    for phase in range(4):
        lit[:, phase * b : (phase + 1) * b] = exact_dot(parts, pick_columns(b, 4, phase))

    even = lax.rem(ang, 2) == 0
    before = jnp.where(ang > 0, jnp.where(even, two_ref[...], one_ref[...]), 0.0)
    after = jnp.where(ang < g.m - 1, jnp.where(even, one_ref[...], two_ref[...]), 0.0)
    for s in range(s_count):
        wide[s, :2] = before[2 * s : 2 * s + 2]
        wide[s, 2 : 2 + la] = coarse_ref[s, 0]
        wide[s, 2 + la :] = after[2 * s : 2 * s + 2]

    end_fine, end_emit, end_mix, _ = forward_rows(g)
    for q in range(g.w):
        for phase in range(2):
            for a in range(2 * g.ra):
                for s in range(s_count):
                    at = ((phase * 2 * g.ra + a) * s_count + s) * 16
                    rows = pl.ds(s * 32 * la + 2 * q * g.ra + a, 16, stride=2 * la)
                    stage[q, at : at + 16] = split[phase, rows, :]
        for phase in range(4):
            for f in range(4):
                at = end_fine + (phase * 4 + f) * 4 * g.ra
                rows = slice(f * 4 * la + 4 * q * g.ra, f * 4 * la + 4 * (q + 1) * g.ra)
                stage[q, at : at + 4 * g.ra] = lit[rows, phase * b : (phase + 1) * b]
        for s in range(s_count):
            for row in range(2 * g.ra + 2):
                a, ca = divmod(2 * q * g.ra - 1 + row, 2)
                for cr in range(2):
                    for cb in range(2):
                        at = end_emit + ((s * (2 * g.ra + 2) + row) * 2 + cr) * 2 + cb
                        edge = 2 * s_count + 4 * s + 2 * cr + cb
                        if a < 0:
                            value = before[edge : edge + 1]
                        elif a >= la:
                            value = after[edge : edge + 1]
                        else:
                            value = mix_ref[s, 4 * cr + 2 * ca + cb, a : a + 1]
                        stage[q, at : at + 1] = value
            at = end_mix + (g.ra + 4) * s
            stage[q, at : at + g.ra + 4] = wide[s, q * g.ra : q * g.ra + g.ra + 4]
    for k in range(g.n):
        out_refs[k][...] = stage[jnp.minimum(lax.rem(me + k, g.n), g.w - 1)]


def weight_kernel(g, rows_mid, rows_fine, mid_table, fine_table, spread, weights):
    for r in range(g.n):
        own = slice(r * g.s, (r + 1) * g.s)
        tables = [mid_table[rows_mid[r]], fine_table[rows_fine[2 * r]], fine_table[rows_fine[2 * r + 1]]]
        for level, table in enumerate(tables):
            for c in range(8):
                weights[level, c, own] = jnp.broadcast_to(table[c : c + 1], (g.s, 27))
    for level in range(3):
        for c in range(8):
            tile = weights[level, c]
            for o in range(27):
                spread[(level * 8 + c) * 27 + o] = jnp.broadcast_to(tile[:, o : o + 1], (g.h, g.b))


def main_kernel(g, spread, bins_ref, data_ref, *rest):
    n, b, s_count, ra, h = g.n, g.b, g.s, g.ra, g.h
    in_refs, rest = rest[:n], rest[n:]
    cells, seen, parent, coarse_sum, edge_sum = rest[:5]
    got, fine_in, emit_in, mix_in, coarse_in, coarse_ext, mid_ext, tall = rest[5:]
    me, ang = lax.axis_index("rad"), lax.axis_index("ang")
    rows_a = 2 * ra + 2
    spacing = 1.0 / (4 * n)
    worker = jnp.minimum(me, g.w - 1)

    for k in range(n):
        source = lax.rem(me + n - k, n)
        got[source] = in_refs[k][...]
    end_fine, end_emit, end_mix, _ = forward_rows(g)
    for r in range(n):
        for s in range(s_count):
            sub = r * s_count + s
            for x in range(4 * ra):
                at = (x * s_count + s) * 16
                fine_in[pl.ds(x * 16 * h + sub, 16, stride=h), :] = got[r, at : at + 16]
            emit_in[pl.ds(sub, 64 * ra, stride=h), :] = got[r, end_fine:end_emit]
            at = end_emit + s * 4 * rows_a
            mix_in[pl.ds(sub, 4 * rows_a, stride=h), :] = got[r, at : at + 4 * rows_a]
            at = end_mix + (ra + 4) * s
            coarse_in[pl.ds(sub, ra + 4, stride=h), :] = got[r, at : at + ra + 4]

    first = ang * g.la + worker * ra
    top_in = jnp.where(first > 0, 1.0, 0.0).astype(F32)
    bottom_in = jnp.where(first + ra < g.m * g.la, 1.0, 0.0).astype(F32)
    for a in range(ra + 4):
        x = coarse_in[a * h : (a + 1) * h]
        for db in range(3):
            shifted = along_lanes(x, 1 - db)
            for dr in range(3):
                coarse_ext[dr, a, db] = along_rows(shifted, (1 - dr) * s_count)
    for cr in range(2):
        for row in range(rows_a):
            a, ca = divmod(row - 1, 2)
            for cb in range(2):
                c = 4 * cr + 2 * ca + cb
                at = (row * 4 + 2 * cr + cb) * h
                total = mix_in[at : at + h]
                for dr in range(3):
                    for da in range(3):
                        for db in range(3):
                            o = 9 * dr + 3 * da + db
                            total = total + spread[c * 27 + o] * coarse_ext[dr, a + 1 + da, db]
                if row == 0:
                    total = total * top_in
                if row == rows_a - 1:
                    total = total * bottom_in
                for bi, step_b in ((1 + cb, 0), (3, -1) if cb == 0 else (0, 1)):
                    shifted = along_lanes(total, step_b)
                    for ri, step_r in ((1 + cr, 0), (3, -1) if cr == 0 else (0, 1)):
                        mid_ext[ri, row, bi] = along_rows(shifted, step_r * s_count)

    def cell_rows(a, c, pr):
        return pl.ds(pl.multiple_of(((a * 8 + c) * 2 + pr) * h, 8), h)

    def fine_cells(c, carry):
        for pr in range(2):
            weight = [spread[((1 + pr) * 8 + c) * 27 + o] for o in range(27)]
            for a in range(2 * ra):
                for pb in range(2):
                    at = (((pb * 2 * ra + a) * 8 + c) * 2 + pr) * h
                    total = fine_in[pl.ds(pl.multiple_of(at, 8), h), :]
                    for dr in range(3):
                        for da in range(3):
                            for db in range(3):
                                o = 9 * dr + 3 * da + db
                                total = total + weight[o] * mid_ext[pr + dr, a + da, pb + db]
                    cells[pb, cell_rows(a, c, pr), :] = total
        return carry

    lax.fori_loop(0, 8, fine_cells, 0)

    radial = 4 * (lax.broadcasted_iota(jnp.int32, (h, b), 0) // s_count)

    def sum_before(x):
        step = s_count
        while step < h:
            x = x + along_rows(x, step)
            step *= 2
        return along_rows(x, s_count)

    def sum_all(x):
        step = s_count
        while step < h:
            x = x + pltpu.roll(x, step, axis=0)
            step *= 2
        return x

    def position(at, carry):
        a, pb = at // 4, lax.rem(at, 4)
        half = pb // 2
        rows = [cell_rows(a // 2, 4 * (f % 2) + 2 * lax.rem(a, 2) + lax.rem(pb, 2), f // 2) for f in range(4)]
        density = [jnp.exp(cells[half, rows[f], :]) for f in range(4)]
        layer = [spacing * d for d in density]
        depth = sum_before(layer[0] + layer[1] + layer[2] + layer[3])
        glow = []
        for f in range(4):
            where_emit = pl.multiple_of(((pb * 4 + f) * 4 * ra + a) * h, 8)
            glow.append(spacing * emit_in[pl.ds(where_emit, h), :] * jnp.exp(-depth))
            depth = depth + layer[f]
        running = sum_before(glow[0] + glow[1] + glow[2] + glow[3])
        column = []
        for f in range(4):
            running = running + glow[f]
            column.append(running)
        total = [jnp.zeros((h, b), F32) for f in range(4)]
        for star in range(g.stars):
            row = (star * 4 * ra + a) * 4 + pb
            bins = jnp.broadcast_to(bins_ref[pl.ds(row, 1), :], (h, b))
            data = jnp.broadcast_to(data_ref[pl.ds(row, 1), :], (h, b))
            bins = bins - radial
            mine = jnp.where(bins == 0, column[0], 0.0)
            for f in range(1, 4):
                mine = jnp.where(bins == f, column[f], mine)
            predicted = sum_all(mine)
            residual = data - predicted
            for s in range(s_count):
                seen[pb, pl.ds((s * g.stars + star) * 4 * ra + a, 1), :] = residual[s : s + 1]
            for f in range(4):
                total[f] = total[f] + jnp.where(bins > f, residual * (predicted - column[f]), 0.0)
        for f in range(4):
            cells[half, rows[f], :] = -density[f] * total[f]
        return carry

    lax.fori_loop(0, 16 * ra, position, 0)

    tall[...] = jnp.zeros(tall.shape, F32)
    for pr in range(2):
        def gather(c, carry, pr=pr):
            values = {(a, pb): cells[pb, cell_rows(a, c, pr), :] for a in range(2 * ra) for pb in range(2)}
            for dr in range(3):
                sums = {}
                for da in range(3):
                    for db in range(3):
                        weight = spread[((1 + pr) * 8 + c) * 27 + 9 * dr + 3 * da + db]
                        for (a, pb), value in values.items():
                            key = (a + da, pb + db)
                            term = weight * value
                            sums[key] = sums[key] + term if key in sums else term
                for (row, bi), value in sums.items():
                    tall[pr + dr, row, bi] += value
            return carry

        lax.fori_loop(0, 8, gather, 0)
    for row in range(rows_a):
        for pr in range(2):
            for pb in range(2):
                bi, step_b = (3, 1) if pb == 0 else (0, -1)
                ri, step_r = (3, 1) if pr == 0 else (0, -1)
                close = tall[1 + pr, row, 1 + pb] + along_lanes(tall[1 + pr, row, bi], step_b)
                far = tall[ri, row, 1 + pb] + along_lanes(tall[ri, row, bi], step_b)
                value = close + along_rows(far, step_r * s_count)
                if row == 0:
                    value = value * top_in
                if row == rows_a - 1:
                    value = value * bottom_in
                at = ((2 * pr + pb) * rows_a + row) * h
                parent[at : at + h] = value

    coarse_sum[...] = jnp.zeros(coarse_sum.shape, F32)
    for dr in range(3):
        for db in range(3):
            sums = {}
            for cr in range(2):
                for row in range(rows_a):
                    a, ca = divmod(row - 1, 2)
                    for cb in range(2):
                        at = ((2 * cr + cb) * rows_a + row) * h
                        cell = parent[at : at + h]
                        for da in range(3):
                            c, o = 4 * cr + 2 * ca + cb, 9 * dr + 3 * da + db
                            term = spread[c * 27 + o] * cell
                            key = a + 1 + da
                            sums[key] = sums[key] + term if key in sums else term
            for a, value in sums.items():
                coarse_sum[a * h : (a + 1) * h] += along_lanes(along_rows(value, (dr - 1) * s_count), db - 1)

    edge_sum[...] = jnp.zeros(edge_sum.shape, F32)
    for q in range(g.w):
        @pl.when(worker == q)
        def _(q=q):
            low = q < g.w // 2
            if q == 0 or q == g.w - 1:
                for x in range(4):
                    at = (x * rows_a + (0 if low else rows_a - 1)) * h
                    edge_sum[x * h : (x + 1) * h] = parent[at : at + h]
            for t in range(2):
                a = (t - 2 if low else g.la + t) - q * ra + 2
                if 0 <= a < ra + 4:
                    edge_sum[(4 + t) * h : (5 + t) * h] = coarse_sum[a * h : (a + 1) * h]


def gather_kernel(g, cells, seen, parent, coarse_sum, edge_ref, *rest):
    out_refs, (joined, stage) = rest[: g.n], rest[g.n :]
    me, ang = lax.axis_index("rad"), lax.axis_index("ang")
    n, b, s_count, ra, h = g.n, g.b, g.s, g.ra, g.h
    rows_a = 2 * ra + 2
    parts = [thirds(cells[phase]) for phase in range(2)]
    order = [place_columns(b, 2, phase) for phase in range(2)]
    for half in range(2):
        lanes = slice(half * b, (half + 1) * b)
        joined[half] = exact_dot(parts[0], order[0][:, lanes]) + exact_dot(parts[1], order[1][:, lanes])
    shown = None
    for phase in range(4):
        value = exact_dot(thirds(seen[phase]), place_columns(b, 4, phase))
        shown = value if shown is None else shown + value
    live = jnp.where(jnp.minimum(me, g.w - 1) < g.w // 2, ang < g.m - 1, ang > 0)
    end_excite, end_resid, end_mid, end_coarse, _ = backward_rows(g)
    per = 4 * g.stars * ra
    for r in range(n):
        for s in range(s_count):
            sub = r * s_count + s
            for half in range(2):
                for a in range(2 * ra):
                    at = ((half * 2 * ra + a) * s_count + s) * 16
                    stage[r, at : at + 16] = joined[half, pl.ds(a * 16 * h + sub, 16, stride=h), :]
            for part in range(4):
                at = end_excite + (part * s_count + s) * per
                stage[r, at : at + per] = shown[s * per : (s + 1) * per, part * b : (part + 1) * b]
            at = end_resid + s * 4 * rows_a
            stage[r, at : at + 4 * rows_a] = parent[pl.ds(sub, 4 * rows_a, stride=h), :]
            at = end_mid + (ra + 4) * s
            stage[r, at : at + ra + 4] = coarse_sum[pl.ds(sub, ra + 4, stride=h), :]
            at = end_coarse + 6 * s
            stage[r, at : at + 6] = jnp.where(live, edge_ref[pl.ds(sub, 6, stride=h), :], 0.0)
    for k in range(n):
        out_refs[k][...] = stage[lax.rem(me + k, n)]


def mixing_kernel(g, rows_mid, rows_fine, noise_mid, noise_fine, mid_out, fine_out):
    me = lax.axis_index("rad")
    entries = [(mid_out, noise_mid, rows_mid[me])]
    entries += [(fine_out.at[i], noise_fine, rows_fine[2 * me + i]) for i in range(2)]
    for out, table, entry in entries:
        lane = lax.broadcasted_iota(jnp.int32, table.shape[1:], 1)
        for c in range(8):
            column = jnp.sum(jnp.where(lane == entry, table[c], 0.0), axis=1, keepdims=True)
            out[c] = jnp.broadcast_to(column, (8, g.b))


def owner_kernel(g, mid_weights, fine_weights, *rest):
    in_refs, rest = rest[: g.n], rest[g.n :]
    coarse_out, mid_out, fine_out, resid_out, got, fine, grad_mid, grad_coarse = rest
    me = lax.axis_index("rad")
    n, b, s_count, ra, la = g.n, g.b, g.s, g.ra, g.la
    rows_a = 2 * ra + 2
    end_excite, end_resid, end_mid, end_coarse, _ = backward_rows(g)
    per = 4 * g.stars * ra
    for k in range(n):
        got[lax.rem(me + n - k, n)] = in_refs[k][...]
    grad_mid[...] = jnp.zeros(grad_mid.shape, F32)
    grad_coarse[...] = jnp.zeros(grad_coarse.shape, F32)
    for q in range(g.w):
        low = q < g.w // 2
        for s in range(s_count):
            for half in range(2):
                for a in range(2 * ra):
                    at = ((half * 2 * ra + a) * s_count + s) * 16
                    rows = pl.ds(s * 32 * la + 2 * q * ra + a, 16, stride=2 * la)
                    fine[half, rows, :] = got[q, at : at + 16]
            for part in range(4):
                for star in range(g.stars):
                    at = end_excite + (part * s_count + s) * per + star * 4 * ra
                    rows = slice(4 * q * ra, 4 * (q + 1) * ra)
                    resid_out[s, star, rows, part * b : (part + 1) * b] = got[q, at : at + 4 * ra]
            edge = got[q, end_coarse + 6 * s : end_coarse + 6 * s + 6]
            for x in range(4):
                at = end_resid + s * 4 * rows_a + x * rows_a
                grad_mid[s, x, 2 * q * ra : 2 * q * ra + rows_a] += got[q, at : at + rows_a]
                row = 2 * la if low else 1
                grad_mid[s, x, row : row + 1] += edge[x : x + 1]
            at = end_mid + (ra + 4) * s
            grad_coarse[s, q * ra : q * ra + ra + 4] += got[q, at : at + ra + 4]
            row = la if low else 2
            grad_coarse[s, row : row + 2] += edge[4:6]
    for i in range(2):
        for j in range(8):
            weight = [fine_weights[i, c, j : j + 1] for c in range(8)]
            for s in range(s_count):
                for half in range(2):
                    total = None
                    for c in range(8):
                        at = ((s * 8 + c) * 2 + i) * 2 * la
                        term = weight[c] * fine[half, at : at + 2 * la]
                        total = term if total is None else total + term
                    fine_out[s, j, i, :, half * b : (half + 1) * b] = total
    for s in range(s_count):
        coarse_out[s, 0] = grad_coarse[s, 2 : 2 + la]
        cells = []
        for c in range(8):
            cr, ca, cb = c // 4, c // 2 % 2, c % 2
            cells.append(grad_mid[s, 2 * cr + cb, pl.ds(1 + ca, la, stride=2), :])
        for j in range(8):
            total = mid_weights[0, j : j + 1] * cells[0]
            for c in range(1, 8):
                total = total + mid_weights[c, j : j + 1] * cells[c]
            mid_out[s, j, 0] = total


def star_kernel(g, bins_ref, data_ref, bins_out, data_out, gathered):
    worker = jnp.minimum(lax.axis_index("rad"), g.w - 1)
    per, b = 4 * g.ra, g.b
    for q in range(g.w):
        @pl.when(worker == q)
        def _(q=q):
            for star in range(g.stars):
                gathered[0, star * per : (star + 1) * per] = bins_ref[star, q * per : (q + 1) * per].astype(F32)
                gathered[1, star * per : (star + 1) * per] = data_ref[star, q * per : (q + 1) * per]
    bins = gathered[0].astype(BF16)
    parts = thirds(gathered[1])
    for phase in range(4):
        choice = pick_columns(b, 4, phase)
        rows = pl.ds(phase, g.stars * per, stride=4)
        bins_out[rows, :] = jnp.dot(bins, choice, preferred_element_type=F32).astype(jnp.int32)
        data_out[rows, :] = exact_dot(parts, choice)


def call(kernel, name, outs, operands, scratch, scalars=0, unmoved=0):
    smem, vmem = pl.BlockSpec(memory_space=pltpu.SMEM), pl.BlockSpec(memory_space=pltpu.VMEM)
    placed = pl.BlockSpec(memory_space=pl.ANY)
    limit = None if unmoved else VMEM_LIMIT
    return pl.pallas_call(
        kernel,
        name=name,
        out_shape=[jax.ShapeDtypeStruct(shape, kind) for shape, kind in outs],
        in_specs=[placed] * unmoved + [smem] * scalars + [vmem] * (len(operands) - scalars - unmoved),
        out_specs=[vmem] * len(outs),
        scratch_shapes=[pltpu.VMEM(shape, F32) if isinstance(shape, tuple) else shape for shape in scratch],
        compiler_params=pltpu.CompilerParams(vmem_limit_bytes=limit),
    )(*operands)


def per_device(
    g,
    coarse_field,
    excite_mid,
    excite_fine,
    kernels_mid,
    noise_mid,
    rows_mid,
    kernels_fine,
    noise_fine,
    rows_fine,
    emission,
    star_bins,
    star_data,
):
    n, m, s, la, b, stars, w, ra, h = g
    kernel = functools.partial
    rows_a = 2 * ra + 2
    there, back = forward_rows(g)[-1], backward_rows(g)[-1]
    pairs = [(i, i ^ 1) for i in range(m)]
    between = [(i, (i + 1) % m if i % 2 else (i - 1) % m) for i in range(m)]
    workers = [(r, a, 1 if min(r, w - 1) < w // 2 else -1) for r in range(n) for a in range(m)]
    sideways = [(r * m + a, r * m + (a - step) % m) for r, a, step in workers]

    def exchange(blocks):
        return [blocks[0]] + [lax.ppermute(blocks[k], "rad", [(i, (i + k) % n) for i in range(n)]) for k in range(1, n)]

    noise_mid, noise_fine = noise_mid.transpose(1, 2, 0), noise_fine.transpose(1, 2, 0)
    edge_rows = (-(-6 * s // 8) * 8, b)
    mixed, one, two = call(
        kernel(edge_kernel, g),
        "edges",
        [((s, 8, la, b), F32), (edge_rows, F32), (edge_rows, F32)],
        (rows_mid, noise_mid, coarse_field, excite_mid),
        [
            pltpu.SMEM(rows_mid.shape, jnp.int32),
            noise_mid.shape,
            coarse_field.shape,
            excite_mid.shape,
            pltpu.SemaphoreType.DMA((4,)),
        ],
        unmoved=4,
    )
    one, two = lax.ppermute(one, "ang", pairs), lax.ppermute(two, "ang", between)
    sent = call(
        kernel(scatter_kernel, g),
        "scatter",
        [((there, b), F32)] * n,
        (rows_fine, noise_fine, excite_fine, emission, coarse_field, mixed, one, two),
        [
            pltpu.SMEM(rows_fine.shape, jnp.int32),
            noise_fine.shape,
            excite_fine.shape,
            emission.shape,
            coarse_field.shape,
            pltpu.SemaphoreType.DMA((5,)),
            (32 * s * la, 2 * b),
            (2, 32 * s * la, b),
            (16 * la, 4 * b),
            (s, la + 4, b),
            (w, there, b),
        ],
        unmoved=5,
    )
    got = exchange(sent)
    bins, data = call(
        kernel(star_kernel, g),
        "stars",
        [((16 * stars * ra, b), jnp.int32), ((16 * stars * ra, b), F32)],
        (star_bins, star_data),
        [(2, 4 * stars * ra, 4 * b)],
    )
    (spread,) = call(
        kernel(weight_kernel, g),
        "weights",
        [((3 * 8 * 27, h, b), F32)],
        (rows_mid, rows_fine, kernels_mid, kernels_fine),
        [(3, 8, h, 27)],
        scalars=2,
    )
    cells, seen, parent, coarse_sum, edge = call(
        kernel(main_kernel, g),
        "main",
        [
            ((2, 32 * ra * h, b), F32),
            ((4, 4 * stars * ra * s, b), F32),
            ((4 * rows_a * h, b), F32),
            (((ra + 4) * h, b), F32),
            ((6 * h, b), F32),
        ],
        (spread, bins, data, *got),
        [
            (n, there, b),
            (64 * ra * h, b),
            (64 * ra * h, b),
            (4 * rows_a * h, b),
            ((ra + 4) * h, b),
            (3, ra + 4, 3, h, b),
            (4, rows_a, 4, h, b),
            (4, rows_a, 4, h, b),
        ],
    )
    edge = lax.ppermute(edge, ("rad", "ang"), sideways)
    done = call(
        kernel(gather_kernel, g),
        "gather",
        [((back, b), F32)] * n,
        (cells, seen, parent, coarse_sum, edge),
        [(2, 32 * ra * h, b), (n, back, b)],
    )
    got = exchange(done)
    mid_weights, fine_weights = call(
        kernel(mixing_kernel, g),
        "mixing",
        [((8, 8, b), F32), ((2, 8, 8, b), F32)],
        (rows_mid, rows_fine, noise_mid, noise_fine),
        [],
        scalars=2,
    )
    return tuple(
        call(
            kernel(owner_kernel, g),
            "owner",
            [
                ((s, 1, la, b), F32),
                ((s, 8, 1, la, b), F32),
                ((s, 8, 2, 2 * la, 2 * b), F32),
                ((s, stars, 4 * la, 4 * b), F32),
            ],
            (mid_weights, fine_weights, *got),
            [(n, back, b), (2, 32 * s * la, b), (s, 4, 2 * la + 2, b), (s, la + 4, b)],
        )
    )


def solution(mesh):
    placed = (
        P(None, "rad", "ang", None),
        P(None, None, "rad", "ang", None),
        P(None, None, "rad", "ang", None),
        P(),
        P(),
        P(),
        P(),
        P(),
        P(),
        P("rad", "ang", None),
        P(None, "ang", None),
        P(None, "ang", None),
    )

    def local(*args):
        return per_device(make_plan(mesh, args[0], args[10]), *args)

    return jax.shard_map(
        local,
        mesh=mesh,
        in_specs=placed,
        out_specs=(
            P(None, "rad", "ang", None),
            P(None, None, "rad", "ang", None),
            P(None, None, "rad", "ang", None),
            P(None, None, "ang", None),
        ),
        check_vma=False,
    )
```

time: 54.3 us -> 50.3 us (0.926)
  waiting for transfers between devices: 29.5 us -> 23.2 us
  local copies, waits for them, and re-layouts: 2.67 us -> 5.42 us
  Pallas kernels: 13.4 us -> 12.8 us
    ppermute x6, waiting for transfers between devices: 23.9 us -> 16.5 us  [exchange(): lax.ppermute(blocks[k], 'rad', [(i, (i + k) % n) for i in range(n)])]
    unnamed x22 -> x26, local copies, waits for them, and re-layouts: 2.67 us -> 5.42 us
    ppermute x1, waiting for transfers between devices: 1.93 us -> 3.01 us  [per_device(): lax.ppermute(two, 'ang', between)]
    pallas_call x6 -> x8, Pallas kernels: 13.4 us -> 12.8 us  [call(): pl.pallas_call(kernel, name=name, out_shape=[jax.ShapeDtypeStruct(shape,...]
  transfers between devices with their start and end apart: 9 -> 9, of which waited for: 8 -> 7; matrix products, arithmetic and copies ran while one was open for 2% -> 0% of each run, Pallas kernels for 1% -> 6%
where the time goes in v1:
time: 50.3 us; the launch traced here: 49.9 us
  waiting for transfers between devices  23.2 us (46%)
  Pallas kernels  12.8 us (25%)
  starting transfers between devices  7.71 us (15%)
  local copies, waits for them, and re-layouts  5.42 us (11%)
  between operations  0.71 us (1%)
    ppermute x6, waiting for transfers between devices, exchange(): lax.ppermute(blocks[k], 'rad', [(i, (i + k) % n) for i in range(n)])  16.5 us
    pallas_call x8, Pallas kernels, call(): pl.pallas_call(kernel, name=name, out_shape=[jax.ShapeDtypeStruct(shape,...  12.8 us
    unnamed x26, local copies, waits for them, and re-layouts  5.42 us
    ppermute x6, starting transfers between devices, exchange(): lax.ppermute(blocks[k], 'rad', [(i, (i + k) % n) for i in range(n)])  5.35 us
    ppermute x1, waiting for transfers between devices, per_device(): edge = lax.ppermute(edge, ('rad', 'ang'), sideways)  3.76 us
    ppermute x1, waiting for transfers between devices, per_device(): lax.ppermute(two, 'ang', between)  3.01 us
    ppermute x1, starting transfers between devices, per_device(): lax.ppermute(two, 'ang', between)  1.17 us
  transfers between devices with their start and end apart: 9, of which 7 were waited for; matrix products, arithmetic and copies ran while one was open for 0% of the time, Pallas kernels for 6%

profile of v1, /device:TPU:11, one launch (start us, length us, event | category | flops | bytes accessed | tf_op | source)
XLA Modules:
  0.0 49.9 jit_solution(11456769831076196070)
XLA Ops:
  0.6 1.6 %edges.1 = (f32[2,8,4,128]{3,2,1,0:T(4,128)}, f32[16,128]{1,0:T(8,128)}, f32[16,128]{1,0:T(8,128)}) custom-call(s32[4]{0:T(128)} %rows_hbm.2, f32[8,8,16]{2,1,0:T(8,128)} %bitcast.4, f32[2,1,4,128]{3,2,1,0:T(4,128)} %coarse_hbm.3, f32[2,8,1,4,128]{4,3,2,1,0:T(4,128)} %excite_hbm.1), custom_call_target="tpu_custom_call" | custom-call | tf_op jit(solution)/shard_map/edges/pallas_call | solution.py:547
  2.2 0.7 %collective-permute-start = (f32[16,128]{1,0:T(8,128)}, f32[16,128]{1,0:T(8,128)S(1)}, u32[]{:S(2)}, u32[]{:S(2)}) collective-permute-start(f32[16,128]{1,0:T(8,128)} %get-tuple-element.29), channel_id=1, source_target_pairs={{0,1},{1,0},{2,3},{3,2},{4,5},{5,4},{6,7},{7,6},{8,9},{9,8},{10,11... | collective-permute-start | bytes 24584 | tf_op jit(solution)/shard_map/ppermute | solution.py:601
  3.0 1.2 %collective-permute-start.1 = (f32[16,128]{1,0:T(8,128)}, f32[16,128]{1,0:T(8,128)S(1)}, u32[]{:S(2)}, u32[]{:S(2)}) collective-permute-start(f32[16,128]{1,0:T(8,128)} %get-tuple-element.30), channel_id=1, source_target_pairs={{0,7},{1,2},{2,1},{3,4},{4,3},{5,6},{6,5},{7,0},{8,15},{9,10},{10,... | collective-permute-start | bytes 24584 | tf_op jit(solution)/shard_map/ppermute | solution.py:601
  4.1 0.0 collective-permute-done.one_ref
  4.1 3.0 %collective-permute-done.1.two_ref = f32[16,128]{1,0:T(8,128)S(1)} collective-permute-done((f32[16,128]{1,0:T(8,128)}, f32[16,128]{1,0:T(8,128)S(1)}, u32[]{:S(2)}, u32[]{:S(2)}) %collective-permute-start.1) | collective-permute-done | bytes 8224 | tf_op jit(solution)/shard_map/ppermute | solution.py:601
  7.1 0.6 %copy-done.12 = f32[16,128]{1,0:T(8,128)} copy-done((f32[16,128]{1,0:T(8,128)}, f32[16,128]{1,0:T(8,128)S(1)}, u32[]{:S(2)}) %copy-start.12) | copy-done | bytes 8216
  7.7 3.5 %scatter.1 = (f32[240,128]{1,0:T(8,128)}, f32[240,128]{1,0:T(8,128)}, f32[240,128]{1,0:T(8,128)}, f32[240,128]{1,0:T(8,128)}) custom-call(s32[8]{0:T(128)} %rows_hbm.3, f32[8,8,16]{2,1,0:T(8,128)} %bitcast.2, f32[2,8,2,8,256]{4,3,2,1,0:T(8,128)} %fine_hbm.1, f32[4,16,512]{2,1,0:T(8,128)} %emission_hbm.1, f32[2,1,4,128]{3,2,1,0:T(4,128)} %coarse_hbm.3, ...), custom_call_target="tpu_custom_call" | custom-call | tf_op jit(solution)/shard_map/scatter/pallas_call | solution.py:547
  11.2 1.4 %collective-permute-start.2 = (f32[240,128]{1,0:T(8,128)}, f32[240,128]{1,0:T(8,128)S(1)}, u32[]{:S(2)}, u32[]{:S(2)}) collective-permute-start(f32[240,128]{1,0:T(8,128)} %get-tuple-element.32), channel_id=1, source_target_pairs={{0,8},{8,16},{16,24},{24,0},{1,9},{9,17},{17,25},{25,1},{2,10},{10... | collective-permute-start | bytes 368648 | tf_op jit(solution)/shard_map/ppermute | solution.py:583
  12.6 1.1 %collective-permute-start.3 = (f32[240,128]{1,0:T(8,128)}, f32[240,128]{1,0:T(8,128)S(1)}, u32[]{:S(2)}, u32[]{:S(2)}) collective-permute-start(f32[240,128]{1,0:T(8,128)} %get-tuple-element.33), channel_id=1, source_target_pairs={{0,16},{8,24},{16,0},{24,8},{1,17},{9,25},{17,1},{25,9},{2,18},{10... | collective-permute-start | bytes 368648 | tf_op jit(solution)/shard_map/ppermute | solution.py:583
  13.7 1.4 %collective-permute-start.4 = (f32[240,128]{1,0:T(8,128)}, f32[240,128]{1,0:T(8,128)S(1)}, u32[]{:S(2)}, u32[]{:S(2)}) collective-permute-start(f32[240,128]{1,0:T(8,128)} %get-tuple-element.34), channel_id=1, source_target_pairs={{0,24},{8,0},{16,8},{24,16},{1,25},{9,1},{17,9},{25,17},{2,26},{10... | collective-permute-start | bytes 368648 | tf_op jit(solution)/shard_map/ppermute | solution.py:583
  15.1 0.9 %copy-done.1 = s32[4,16,512]{2,1,0:T(8,128)S(1)} copy-done((s32[4,16,512]{2,1,0:T(8,128)S(1)}, s32[4,16,512]{2,1,0:T(8,128)}, u32[]{:S(2)}) %copy-start.1) | copy-done | bytes 131096
  16.0 0.9 %copy-done.2 = f32[4,16,512]{2,1,0:T(8,128)S(1)} copy-done((f32[4,16,512]{2,1,0:T(8,128)S(1)}, f32[4,16,512]{2,1,0:T(8,128)}, u32[]{:S(2)}) %copy-start.2) | copy-done | bytes 131096
  16.9 0.4 stars.1
  17.3 0.8 %copy-done.5 = f32[16,8,27]{2,1,0:T(8,128)S(1)} copy-done((f32[16,8,27]{2,1,0:T(8,128)S(1)}, f32[16,8,27]{2,1,0:T(8,128)}, u32[]{:S(2)}) %copy-start.5) | copy-done | bytes 13848
  18.2 0.8 %copy-done.6 = f32[16,8,27]{2,1,0:T(8,128)S(1)} copy-done((f32[16,8,27]{2,1,0:T(8,128)S(1)}, f32[16,8,27]{2,1,0:T(8,128)}, u32[]{:S(2)}) %copy-start.6) | copy-done | bytes 13848
  19.0 0.7 %copy-done.7 = s32[4]{0:T(128)S(1)} copy-done((s32[4]{0:T(128)S(1)}, s32[4]{0:T(128)}, u32[]{:S(2)}) %copy-start.7) | copy-done | bytes 40
  19.7 0.7 %copy-done.9 = s32[8]{0:T(128)S(1)} copy-done((s32[8]{0:T(128)S(1)}, s32[8]{0:T(128)}, u32[]{:S(2)}) %copy-start.9) | copy-done | bytes 56
  20.3 1.8 %weights.1.spread = f32[648,8,128]{2,1,0:T(8,128)S(1)} custom-call(s32[4]{0:T(128)S(1)} %copy-done.7, s32[8]{0:T(128)S(1)} %copy-done.9, f32[16,8,27]{2,1,0:T(8,128)S(1)} %copy-done.5, f32[16,8,27]{2,1,0:T(8,128)S(1)} %copy-done.6), custom_call_target="tpu_custom_call" | custom-call | tf_op jit(solution)/shard_map/weights/pallas_call | solution.py:547
  22.1 1.5 %collective-permute-done.3.rest_2_ = f32[240,128]{1,0:T(8,128)S(1)} collective-permute-done((f32[240,128]{1,0:T(8,128)}, f32[240,128]{1,0:T(8,128)S(1)}, u32[]{:S(2)}, u32[]{:S(2)}) %collective-permute-start.3) | collective-permute-done | bytes 122912 | tf_op jit(solution)/shard_map/ppermute | solution.py:583
  23.6 1.6 %collective-permute-done.4.rest_3_ = f32[240,128]{1,0:T(8,128)S(1)} collective-permute-done((f32[240,128]{1,0:T(8,128)}, f32[240,128]{1,0:T(8,128)S(1)}, u32[]{:S(2)}, u32[]{:S(2)}) %collective-permute-start.4) | collective-permute-done | bytes 122912 | tf_op jit(solution)/shard_map/ppermute | solution.py:583
  25.2 3.1 %main.1 = (f32[2,256,128]{2,1,0:T(8,128)S(1)}, f32[4,32,128]{2,1,0:T(8,128)S(1)}, f32[128,128]{1,0:T(8,128)S(1)}, f32[40,128]{1,0:T(8,128)S(1)}, f32[48,128]{1,0:T(8,128)S(1)}) custom-call(f32[648,8,128]{2,1,0:T(8,128)S(1)} %weights.1.spread, s32[64,128]{1,0:T(8,128)S(1)} %get-tuple-element.26.bins_ref, f32[64,128]{1,0:T(8,128)S(1)} %get-tuple-element.27.data_ref, ...), custom_call_target="tpu_custom_call" | custom-call | tf_op jit(solution)/shard_map/main/pallas_call | solution.py:547
  28.3 0.4 collective-permute-start.5
  28.8 3.8 %collective-permute-done.5.edge_ref = f32[48,128]{1,0:T(8,128)S(1)} collective-permute-done((f32[48,128]{1,0:T(8,128)S(1)}, f32[48,128]{1,0:T(8,128)S(1)}, u32[]{:S(2)}, u32[]{:S(2)}) %collective-permute-start.5) | collective-permute-done | bytes 24608 | tf_op jit(solution)/shard_map/ppermute | solution.py:660
  32.5 0.6 %gather.1 = (f32[312,128]{1,0:T(8,128)S(1)}, f32[312,128]{1,0:T(8,128)S(1)}, f32[312,128]{1,0:T(8,128)S(1)}, f32[312,128]{1,0:T(8,128)S(1)}) custom-call(f32[2,256,128]{2,1,0:T(8,128)S(1)} %get-tuple-element.35.cells, f32[4,32,128]{2,1,0:T(8,128)S(1)} %get-tuple-element.36.seen, f32[128,128]{1,0:T(8,128)S(1)} %get-tuple-element.37.parent, ...), custom_call_target="tpu_custom_call" | custom-call | tf_op jit(solution)/shard_map/gather/pallas_call | solution.py:547
  33.2 0.1 collective-permute-start.6
  33.2 0.6 %collective-permute-start.7 = (f32[312,128]{1,0:T(8,128)S(1)}, f32[312,128]{1,0:T(8,128)S(1)}, u32[]{:S(2)}, u32[]{:S(2)}) collective-permute-start(f32[312,128]{1,0:T(8,128)S(1)} %get-tuple-element.42), channel_id=1, source_target_pairs={{0,16},{8,24},{16,0},{24,8},{1,17},{9,25},{17,1},{25,9},{2,18},{10... | collective-permute-start | bytes 479240 | tf_op jit(solution)/shard_map/ppermute | solution.py:583
  33.9 0.8 %collective-permute-start.8 = (f32[312,128]{1,0:T(8,128)S(1)}, f32[312,128]{1,0:T(8,128)S(1)}, u32[]{:S(2)}, u32[]{:S(2)}) collective-permute-start(f32[312,128]{1,0:T(8,128)S(1)} %get-tuple-element.43), channel_id=1, source_target_pairs={{0,24},{8,0},{16,8},{24,16},{1,25},{9,1},{17,9},{25,17},{2,26},{10... | collective-permute-start | bytes 479240 | tf_op jit(solution)/shard_map/ppermute | solution.py:583
  34.7 0.6 %mixing.1 = (f32[8,8,128]{2,1,0:T(8,128)S(1)}, f32[2,8,8,128]{3,2,1,0:T(8,128)S(1)}) custom-call(s32[4]{0:T(128)S(1)} %copy-done.8, s32[8]{0:T(128)S(1)} %copy-done.10, f32[8,8,16]{2,1,0:T(8,128)S(1)} %bitcast.5, f32[8,8,16]{2,1,0:T(8,128)S(1)} %bitcast.3), custom_call_target="tpu_custom_call" | custom-call | tf_op jit(solution)/shard_map/mixing/pallas_call | solution.py:547
  35.4 8.5 %collective-permute-done.6.rest_1_ = f32[312,128]{1,0:T(8,128)S(1)} collective-permute-done((f32[312,128]{1,0:T(8,128)S(1)}, f32[312,128]{1,0:T(8,128)S(1)}, u32[]{:S(2)}, u32[]{:S(2)}) %collective-permute-start.6) | collective-permute-done | bytes 159776 | tf_op jit(solution)/shard_map/ppermute | solution.py:583
  43.8 2.9 %collective-permute-done.7.rest_2_ = f32[312,128]{1,0:T(8,128)S(1)} collective-permute-done((f32[312,128]{1,0:T(8,128)S(1)}, f32[312,128]{1,0:T(8,128)S(1)}, u32[]{:S(2)}, u32[]{:S(2)}) %collective-permute-start.7) | collective-permute-done | bytes 159776 | tf_op jit(solution)/shard_map/ppermute | solution.py:583
  46.8 2.0 %collective-permute-done.8.rest_3_ = f32[312,128]{1,0:T(8,128)S(1)} collective-permute-done((f32[312,128]{1,0:T(8,128)S(1)}, f32[312,128]{1,0:T(8,128)S(1)}, u32[]{:S(2)}, u32[]{:S(2)}) %collective-permute-start.8) | collective-permute-done | bytes 159776 | tf_op jit(solution)/shard_map/ppermute | solution.py:583
  48.8 1.1 %owner.1 = (f32[2,1,4,128]{3,2,1,0:T(4,128)}, f32[2,8,1,4,128]{4,3,2,1,0:T(4,128)}, f32[2,8,2,8,256]{4,3,2,1,0:T(8,128)}, f32[2,4,16,512]{3,2,1,0:T(8,128)}) custom-call(f32[8,8,128]{2,1,0:T(8,128)S(1)} %get-tuple-element.24.mid_weights, f32[2,8,8,128]{3,2,1,0:T(8,128)S(1)} %get-tuple-element.25.fine_weights, f32[312,128]{1,0:T(8,128)S(1)} %get-tuple-element.40.rest_0_, ...), custom_call_target="tpu_custom_call" | custom-call | tf_op jit(solution)/shard_map/owner/pallas_call | solution.py:547
  (20 shorter events, 0.0 us)
Async XLA Ops:
  2.2 1.9 %collective-permute-start = (f32[16,128]{1,0:T(8,128)}, f32[16,128]{1,0:T(8,128)S(1)}, u32[]{:S(2)}, u32[]{:S(2)}) collective-permute-start(f32[16,128]{1,0:T(8,128)} %get-tuple-element.29), channel_id=1, source_target_pairs={{0,1},{1,0},{2,3},{3,2},{4,5},{5,4},{6,7},{7,6},{8,9},{9,8},{10,11... | collective-permute-start | bytes 24584 | tf_op jit(solution)/shard_map/ppermute | solution.py:601
  3.0 4.2 %collective-permute-start.1 = (f32[16,128]{1,0:T(8,128)}, f32[16,128]{1,0:T(8,128)S(1)}, u32[]{:S(2)}, u32[]{:S(2)}) collective-permute-start(f32[16,128]{1,0:T(8,128)} %get-tuple-element.30), channel_id=1, source_target_pairs={{0,7},{1,2},{2,1},{3,4},{4,3},{5,6},{6,5},{7,0},{8,15},{9,10},{10,... | collective-permute-start | bytes 24584 | tf_op jit(solution)/shard_map/ppermute | solution.py:601
  4.1 3.0 %copy-start.11 = (f32[16,128]{1,0:T(8,128)}, f32[16,128]{1,0:T(8,128)S(1)}, u32[]{:S(2)}) copy-start(f32[16,128]{1,0:T(8,128)S(1)} %collective-permute-done.one_ref) | copy-start | bytes 24580
  7.1 0.6 %copy-start.12 = (f32[16,128]{1,0:T(8,128)}, f32[16,128]{1,0:T(8,128)S(1)}, u32[]{:S(2)}) copy-start(f32[16,128]{1,0:T(8,128)S(1)} %collective-permute-done.1.two_ref) | copy-start | bytes 24580
  11.2 10.8 %collective-permute-start.2 = (f32[240,128]{1,0:T(8,128)}, f32[240,128]{1,0:T(8,128)S(1)}, u32[]{:S(2)}, u32[]{:S(2)}) collective-permute-start(f32[240,128]{1,0:T(8,128)} %get-tuple-element.32), channel_id=1, source_target_pairs={{0,8},{8,16},{16,24},{24,0},{1,9},{9,17},{17,25},{25,1},{2,10},{10... | collective-permute-start | bytes 368648 | tf_op jit(solution)/shard_map/ppermute | solution.py:583
  12.6 11.0 %collective-permute-start.3 = (f32[240,128]{1,0:T(8,128)}, f32[240,128]{1,0:T(8,128)S(1)}, u32[]{:S(2)}, u32[]{:S(2)}) collective-permute-start(f32[240,128]{1,0:T(8,128)} %get-tuple-element.33), channel_id=1, source_target_pairs={{0,16},{8,24},{16,0},{24,8},{1,17},{9,25},{17,1},{25,9},{2,18},{10... | collective-permute-start | bytes 368648 | tf_op jit(solution)/shard_map/ppermute | solution.py:583
  13.7 11.5 %collective-permute-start.4 = (f32[240,128]{1,0:T(8,128)}, f32[240,128]{1,0:T(8,128)S(1)}, u32[]{:S(2)}, u32[]{:S(2)}) collective-permute-start(f32[240,128]{1,0:T(8,128)} %get-tuple-element.34), channel_id=1, source_target_pairs={{0,24},{8,0},{16,8},{24,16},{1,25},{9,1},{17,9},{25,17},{2,26},{10... | collective-permute-start | bytes 368648 | tf_op jit(solution)/shard_map/ppermute | solution.py:583
  15.1 0.9 %copy-start.1 = (s32[4,16,512]{2,1,0:T(8,128)S(1)}, s32[4,16,512]{2,1,0:T(8,128)}, u32[]{:S(2)}) copy-start(s32[4,16,512]{2,1,0:T(8,128)} %bins_ref.1) | copy-start | bytes 393220
  16.0 0.9 %copy-start.2 = (f32[4,16,512]{2,1,0:T(8,128)S(1)}, f32[4,16,512]{2,1,0:T(8,128)}, u32[]{:S(2)}) copy-start(f32[4,16,512]{2,1,0:T(8,128)} %data_ref.1) | copy-start | bytes 393220
  16.9 8.3 %copy-start.4 = (f32[240,128]{1,0:T(8,128)S(1)}, f32[240,128]{1,0:T(8,128)}, u32[]{:S(2)}) copy-start(f32[240,128]{1,0:T(8,128)} %get-tuple-element.31.rest_0_) | copy-start | bytes 368644
  17.3 0.9 %copy-start.5 = (f32[16,8,27]{2,1,0:T(8,128)S(1)}, f32[16,8,27]{2,1,0:T(8,128)}, u32[]{:S(2)}) copy-start(f32[16,8,27]{2,1,0:T(8,128)} %mid_table.1) | copy-start | bytes 41476
  18.2 0.8 %copy-start.6 = (f32[16,8,27]{2,1,0:T(8,128)S(1)}, f32[16,8,27]{2,1,0:T(8,128)}, u32[]{:S(2)}) copy-start(f32[16,8,27]{2,1,0:T(8,128)} %fine_table.1) | copy-start | bytes 41476
  19.0 0.7 %copy-start.7 = (s32[4]{0:T(128)S(1)}, s32[4]{0:T(128)}, u32[]{:S(2)}) copy-start(s32[4]{0:T(128)} %rows_hbm.2) | copy-start | bytes 52
  19.6 0.7 %copy-start.9 = (s32[8]{0:T(128)S(1)}, s32[8]{0:T(128)}, u32[]{:S(2)}) copy-start(s32[8]{0:T(128)} %rows_hbm.3) | copy-start | bytes 100
  20.3 14.4 %copy-start = (f32[16,8,8]{0,2,1:T(8,128)S(1)}, f32[16,8,8]{0,2,1:T(8,128)}, u32[]{:S(2)}) copy-start(f32[16,8,8]{0,2,1:T(8,128)} %param.19) | copy-start | bytes 12292
  20.3 14.4 %copy-start.3 = (f32[16,8,8]{0,2,1:T(8,128)S(1)}, f32[16,8,8]{0,2,1:T(8,128)}, u32[]{:S(2)}) copy-start(f32[16,8,8]{0,2,1:T(8,128)} %param.16) | copy-start | bytes 12292
  20.3 14.4 %copy-start.8 = (s32[4]{0:T(128)S(1)}, s32[4]{0:T(128)}, u32[]{:S(2)}) copy-start(s32[4]{0:T(128)} %rows_hbm.2) | copy-start | bytes 52
  20.3 14.4 %copy-start.10 = (s32[8]{0:T(128)S(1)}, s32[8]{0:T(128)}, u32[]{:S(2)}) copy-start(s32[8]{0:T(128)} %rows_hbm.3) | copy-start | bytes 100
  28.3 4.2 %collective-permute-start.5 = (f32[48,128]{1,0:T(8,128)S(1)}, f32[48,128]{1,0:T(8,128)S(1)}, u32[]{:S(2)}, u32[]{:S(2)}) collective-permute-start(f32[48,128]{1,0:T(8,128)S(1)} %get-tuple-element.39), channel_id=1, source_target_pairs={{0,7},{1,0},{2,1},{3,2},{4,3},{5,4},{6,5},{7,6},{8,15},{9,8},{10,9... | collective-permute-start | bytes 73736 | tf_op jit(solution)/shard_map/ppermute | solution.py:660
  33.2 10.6 %collective-permute-start.6 = (f32[312,128]{1,0:T(8,128)S(1)}, f32[312,128]{1,0:T(8,128)S(1)}, u32[]{:S(2)}, u32[]{:S(2)}) collective-permute-start(f32[312,128]{1,0:T(8,128)S(1)} %get-tuple-element.41), channel_id=1, source_target_pairs={{0,8},{8,16},{16,24},{24,0},{1,9},{9,17},{17,25},{25,1},{2,10},{10... | collective-permute-start | bytes 479240 | tf_op jit(solution)/shard_map/ppermute | solution.py:583
  33.2 13.5 %collective-permute-start.7 = (f32[312,128]{1,0:T(8,128)S(1)}, f32[312,128]{1,0:T(8,128)S(1)}, u32[]{:S(2)}, u32[]{:S(2)}) collective-permute-start(f32[312,128]{1,0:T(8,128)S(1)} %get-tuple-element.42), channel_id=1, source_target_pairs={{0,16},{8,24},{16,0},{24,8},{1,17},{9,25},{17,1},{25,9},{2,18},{10... | collective-permute-start | bytes 479240 | tf_op jit(solution)/shard_map/ppermute | solution.py:583
  33.9 14.9 %collective-permute-start.8 = (f32[312,128]{1,0:T(8,128)S(1)}, f32[312,128]{1,0:T(8,128)S(1)}, u32[]{:S(2)}, u32[]{:S(2)}) collective-permute-start(f32[312,128]{1,0:T(8,128)S(1)} %get-tuple-element.43), channel_id=1, source_target_pairs={{0,24},{8,0},{16,8},{24,16},{1,25},{9,1},{17,9},{25,17},{2,26},{10... | collective-permute-start | bytes 479240 | tf_op jit(solution)/shard_map/ppermute | solution.py:583

commit v2 on v1

v2 whole, which is shorter than its diff:
```python
import functools
import typing

import jax
import jax.numpy as jnp
from jax import lax
from jax.experimental import pallas as pl
from jax.experimental.pallas import tpu as pltpu
from jax.sharding import PartitionSpec as P

F32 = jnp.float32
BF16 = jnp.bfloat16
VMEM_LIMIT = 24 * 1024 * 1024


class Plan(typing.NamedTuple):
    n: int
    m: int
    s: int
    la: int
    b: int
    stars: int
    w: int
    ra: int
    h: int


def make_plan(mesh, coarse, star_bins):
    n, m = mesh.shape["rad"], mesh.shape["ang"]
    s, rows, la, b = coarse.shape
    w = max(d for d in range(1, min(n, la) + 1) if la % d == 0)
    ra = la // w
    assert rows == 1 and m % 2 == 0 and w % 2 == 0 and (w // 2) * ra >= 2
    return Plan(n, m, s, la, b, star_bins.shape[0], w, ra, n * s)


def eights(rows):
    return -(-rows // 8) * 8


def large_there(g):
    fine = 2 * 2 * g.ra * g.s * 16
    return fine, fine + 16 * 4 * g.ra


def small_there(g):
    mix = g.s * 4 * (2 * g.ra + 2)
    return mix, eights(mix + g.s * (g.ra + 4))


def large_back(g):
    field = 2 * 2 * g.ra * g.s * 16
    return field, field + 4 * g.s * g.stars * 4 * g.ra


def small_back(g):
    mid = g.s * 4 * (2 * g.ra + 2)
    coarse = mid + g.s * (g.ra + 4)
    return mid, coarse, eights(coarse + 6 * g.s)


def prepared_rows(g):
    sizes = dict(
        mixed=8 * g.s * g.la,
        coarse=eights(g.s * g.la),
        stencil=24 * g.h,
        bins=16 * g.stars * g.ra,
        data=16 * g.stars * g.ra,
        mid=64,
        fine=128,
    )
    begins, at = {}, 0
    for part, size in sizes.items():
        begins[part] = at
        at += size
    return begins, at


def table_weights(table_ref, entry):
    lane = lax.broadcasted_iota(jnp.int32, table_ref.shape[1:], 1)
    columns = [
        jnp.sum(jnp.where(lane == entry, table_ref[c], 0.0), axis=1, keepdims=True) for c in range(table_ref.shape[0])
    ]
    return lambda c, j: columns[c][j : j + 1]


def start_all(pairs, sems, first=0):
    copies = [pltpu.make_async_copy(source, here, sems.at[first + i]) for i, (source, here) in enumerate(pairs)]
    for copy in copies:
        copy.start()
    return copies


def wait_all(copies):
    for copy in copies:
        copy.wait()


def pick_columns(length, ways, phase):
    src = lax.broadcasted_iota(jnp.int32, (length * ways, length), 0)
    dst = lax.broadcasted_iota(jnp.int32, (length * ways, length), 1)
    return jnp.where(src == ways * dst + phase, 1.0, 0.0).astype(BF16)


def place_columns(length, ways, phase):
    src = lax.broadcasted_iota(jnp.int32, (length, length * ways), 0)
    dst = lax.broadcasted_iota(jnp.int32, (length, length * ways), 1)
    return jnp.where(dst == ways * src + phase, 1.0, 0.0).astype(BF16)


def thirds(x):
    high = x.astype(BF16)
    rest = x - high.astype(F32)
    middle = rest.astype(BF16)
    return high, middle, (rest - middle.astype(F32)).astype(BF16)


def exact_dot(parts, choice):
    high, middle, low = [jnp.dot(part, choice, preferred_element_type=F32) for part in parts]
    return high + (middle + low)


def along_lanes(x, step):
    if step == 0:
        return x
    size = x.shape[1]
    lane = lax.broadcasted_iota(jnp.int32, x.shape, 1)
    edge = 0 if step > 0 else size - 1
    return jnp.where(lane == edge, 0.0, pltpu.roll(x, step % size, axis=1))


def along_rows(x, step):
    if step == 0:
        return x
    size = x.shape[0]
    row = lax.broadcasted_iota(jnp.int32, x.shape, 0)
    kept = row >= step if step > 0 else row < size + step
    return jnp.where(kept, pltpu.roll(x, step % size, axis=0), 0.0)


def prepare_kernel(g, *rest):
    sources, (one_ref, two_ref, block), rest = rest[:10], rest[11:14], rest[14:]
    held, (sems, gathered) = rest[:10], rest[10:]
    copies = start_all(list(zip(sources, held)), sems)
    rows_mid, rows_fine, noise_mid, noise_fine, mid_table, fine_table = held[:6]
    coarse_ref, excite_ref, bins_ref, data_ref = held[6:]
    begins, _ = prepared_rows(g)
    me = lax.axis_index("rad")
    even = lax.rem(lax.axis_index("ang"), 2) == 0
    worker = jnp.minimum(me, g.w - 1)
    per, b = 4 * g.ra, g.b
    choices = [pick_columns(b, 4, phase) for phase in range(4)]
    wait_all(copies)
    weight = table_weights(noise_mid, rows_mid[me])
    for c in range(8):
        for s in range(g.s):
            total = weight(c, 0) * excite_ref[s, 0, 0]
            for j in range(1, 8):
                total = total + weight(c, j) * excite_ref[s, j, 0]
            at = begins["mixed"] + (s * 8 + c) * g.la
            block[at : at + g.la] = total
    for s in range(g.s):
        up, down = coarse_ref[s, 0, g.la - 2 :], coarse_ref[s, 0, :2]
        one_ref[2 * s : 2 * s + 2] = jnp.where(even, up, down)
        two_ref[2 * s : 2 * s + 2] = jnp.where(even, down, up)
        for cr in range(2):
            for cb in range(2):
                at = 2 * g.s + 4 * s + 2 * cr + cb
                last = begins["mixed"] + (s * 8 + 4 * cr + 2 + cb) * g.la + g.la - 1
                leading = begins["mixed"] + (s * 8 + 4 * cr + cb) * g.la
                up, down = block[last : last + 1], block[leading : leading + 1]
                one_ref[at : at + 1] = jnp.where(even, up, down)
                two_ref[at : at + 1] = jnp.where(even, down, up)
        at = begins["coarse"] + s * g.la
        block[at : at + g.la] = coarse_ref[s, 0]
    for r in range(g.n):
        tables = [mid_table[rows_mid[r]], fine_table[rows_fine[2 * r]], fine_table[rows_fine[2 * r + 1]]]
        for level, table in enumerate(tables):
            for c in range(8):
                at = begins["stencil"] + (level * 8 + c) * g.h + r * g.s
                block[at : at + g.s, :27] = jnp.broadcast_to(table[c : c + 1], (g.s, 27))
    entries = [(begins["mid"], noise_mid, rows_mid[me])]
    entries += [(begins["fine"] + 64 * i, noise_fine, rows_fine[2 * me + i]) for i in range(2)]
    for at, table, entry in entries:
        lane = lax.broadcasted_iota(jnp.int32, table.shape[1:], 1)
        for c in range(8):
            column = jnp.sum(jnp.where(lane == entry, table[c], 0.0), axis=1, keepdims=True)
            block[at + 8 * c : at + 8 * c + 8] = jnp.broadcast_to(column, (8, b))
    for q in range(g.w):
        @pl.when(worker == q)
        def _(q=q):
            for star in range(g.stars):
                gathered[0, star * per : (star + 1) * per] = bins_ref[star, q * per : (q + 1) * per].astype(F32)
                gathered[1, star * per : (star + 1) * per] = data_ref[star, q * per : (q + 1) * per]
    bins = gathered[0].astype(BF16)
    parts = thirds(gathered[1])
    for phase in range(4):
        rows = pl.ds(begins["bins"] + phase, g.stars * per, stride=4)
        block[rows, :] = jnp.dot(bins, choices[phase], preferred_element_type=F32)
        rows = pl.ds(begins["data"] + phase, g.stars * per, stride=4)
        block[rows, :] = exact_dot(parts, choices[phase])


def scatter_kernel(g, rows_hbm, noise_hbm, fine_hbm, emission_hbm, *rest):
    out_refs, rest = rest[: g.n], rest[g.n :]
    rows_ref, noise_ref, fine_ref, emission_ref, sems, out_sems, raw, split, lit, stage = rest
    operands = [(emission_hbm, emission_ref), (rows_hbm, rows_ref), (noise_hbm, noise_ref), (fine_hbm, fine_ref)]
    copies = start_all(operands, sems)
    me = lax.axis_index("rad")
    b, s_count, la = g.b, g.s, g.la
    end_fine, _ = large_there(g)
    choices = [pick_columns(b, 4, phase) for phase in range(4)]
    copies[0].wait()
    parts = thirds(emission_ref[...].reshape(16 * la, 4 * b))
    for phase in range(4):
        lit[phase] = exact_dot(parts, choices[phase])
    for q in range(g.w):
        for phase in range(4):
            for f in range(4):
                at = end_fine + (phase * 4 + f) * 4 * g.ra
                rows = slice(f * 4 * la + 4 * q * g.ra, f * 4 * la + 4 * (q + 1) * g.ra)
                stage[q, at : at + 4 * g.ra] = lit[phase, rows]
    wait_all(copies[1:])
    for i in range(2):
        weight = table_weights(noise_ref, rows_ref[2 * me + i])
        for c in range(8):
            weights = [weight(c, j) for j in range(8)]
            for s in range(s_count):
                total = weights[0] * fine_ref[s, 0, i]
                for j in range(1, 8):
                    total = total + weights[j] * fine_ref[s, j, i]
                at = ((s * 8 + c) * 2 + i) * 2 * la
                raw[at : at + 2 * la] = total
    parts = thirds(raw[...])
    for phase in range(2):
        split[phase] = exact_dot(parts, pick_columns(b, 2, phase))
    for q in range(g.w):
        for phase in range(2):
            for a in range(2 * g.ra):
                for s in range(s_count):
                    at = ((phase * 2 * g.ra + a) * s_count + s) * 16
                    rows = pl.ds(s * 32 * la + 2 * q * g.ra + a, 16, stride=2 * la)
                    stage[q, at : at + 16] = split[phase, rows, :]
    workers = [jnp.minimum(lax.rem(me + k, g.n), g.w - 1) for k in range(g.n)]
    wait_all(start_all([(stage.at[worker], out) for worker, out in zip(workers, out_refs)], out_sems))


def halo_kernel(g, block, one_ref, two_ref, *rest):
    out_refs, (wide, stage) = rest[: g.n], rest[g.n :]
    begins, _ = prepared_rows(g)
    me, ang = lax.axis_index("rad"), lax.axis_index("ang")
    even = lax.rem(ang, 2) == 0
    before = jnp.where(ang > 0, jnp.where(even, two_ref[...], one_ref[...]), 0.0)
    after = jnp.where(ang < g.m - 1, jnp.where(even, one_ref[...], two_ref[...]), 0.0)
    for s in range(g.s):
        wide[s, :2] = before[2 * s : 2 * s + 2]
        at = begins["coarse"] + s * g.la
        wide[s, 2 : 2 + g.la] = block[at : at + g.la]
        wide[s, 2 + g.la :] = after[2 * s : 2 * s + 2]
    end_mix, _ = small_there(g)
    for q in range(g.w):
        for s in range(g.s):
            for row in range(2 * g.ra + 2):
                a, ca = divmod(2 * q * g.ra - 1 + row, 2)
                for cr in range(2):
                    for cb in range(2):
                        at = ((s * (2 * g.ra + 2) + row) * 2 + cr) * 2 + cb
                        edge = 2 * g.s + 4 * s + 2 * cr + cb
                        if a < 0:
                            value = before[edge : edge + 1]
                        elif a >= g.la:
                            value = after[edge : edge + 1]
                        else:
                            own = begins["mixed"] + (s * 8 + 4 * cr + 2 * ca + cb) * g.la + a
                            value = block[own : own + 1]
                        stage[q, at : at + 1] = value
            at = end_mix + (g.ra + 4) * s
            stage[q, at : at + g.ra + 4] = wide[s, q * g.ra : q * g.ra + g.ra + 4]
    for k in range(g.n):
        out_refs[k][...] = stage[jnp.minimum(lax.rem(me + k, g.n), g.w - 1)]


def weight_kernel(g, block, spread):
    begins, _ = prepared_rows(g)
    for x in range(24):
        at = begins["stencil"] + x * g.h
        tile = block[at : at + g.h]
        for o in range(27):
            spread[x * 27 + o] = jnp.broadcast_to(tile[:, o : o + 1], (g.h, g.b))


def main_kernel(g, block, spread, *rest):
    n, b, s_count, ra, h = g.n, g.b, g.s, g.ra, g.h
    large_refs, small_refs, out_refs, rest = rest[:n], rest[n : 2 * n], rest[2 * n : 3 * n], rest[3 * n :]
    parent, coarse_sum, edge_sum = rest[:3]
    got, near, fine_in, emit_in, mix_in, coarse_in, coarse_ext, mid_ext, tall, cells, seen, joined, stage = rest[3:]
    me, ang = lax.axis_index("rad"), lax.axis_index("ang")
    rows_a = 2 * ra + 2
    spacing = 1.0 / (4 * n)
    worker = jnp.minimum(me, g.w - 1)
    begins, _ = prepared_rows(g)

    def weight_at(level, c, o):
        return spread[(level * 8 + c) * 27 + o]

    for k in range(n):
        source = lax.rem(me + n - k, n)
        got[source] = large_refs[k][...]
        near[source] = small_refs[k][...]
    end_fine, end_emit = large_there(g)
    end_mix, _ = small_there(g)
    for r in range(n):
        for s in range(s_count):
            sub = r * s_count + s
            at = s * 4 * rows_a
            mix_in[pl.ds(sub, 4 * rows_a, stride=h), :] = near[r, at : at + 4 * rows_a]
            at = end_mix + (ra + 4) * s
            coarse_in[pl.ds(sub, ra + 4, stride=h), :] = near[r, at : at + ra + 4]

    first = ang * g.la + worker * ra
    top_in = jnp.where(first > 0, 1.0, 0.0).astype(F32)
    bottom_in = jnp.where(first + ra < g.m * g.la, 1.0, 0.0).astype(F32)
    for a in range(ra + 4):
        x = coarse_in[a * h : (a + 1) * h]
        for db in range(3):
            shifted = along_lanes(x, 1 - db)
            for dr in range(3):
                coarse_ext[dr, a, db] = along_rows(shifted, (1 - dr) * s_count)
    for c in range(8):
        cr, ca, cb = c // 4, c // 2 % 2, c % 2
        weight = [weight_at(0, c, o) for o in range(27)]
        for row in range(1 - ca, rows_a, 2):
            a = (row - 1) // 2
            at = (row * 4 + 2 * cr + cb) * h
            total = mix_in[at : at + h]
            for dr in range(3):
                for da in range(3):
                    for db in range(3):
                        total = total + weight[9 * dr + 3 * da + db] * coarse_ext[dr, a + 1 + da, db]
            if row == 0:
                total = total * top_in
            if row == rows_a - 1:
                total = total * bottom_in
            for bi, step_b in ((1 + cb, 0), (3, -1) if cb == 0 else (0, 1)):
                shifted = along_lanes(total, step_b)
                for ri, step_r in ((1 + cr, 0), (3, -1) if cr == 0 else (0, 1)):
                    mid_ext[ri, row, bi] = along_rows(shifted, step_r * s_count)

    for r in range(n):
        for s in range(s_count):
            sub = r * s_count + s
            for x in range(4 * ra):
                at = (x * s_count + s) * 16
                fine_in[pl.ds(x * 16 * h + sub, 16, stride=h), :] = got[r, at : at + 16]
            emit_in[pl.ds(sub, 64 * ra, stride=h), :] = got[r, end_fine:end_emit]

    def cell_rows(a, c, pr):
        return pl.ds(pl.multiple_of(((a * 8 + c) * 2 + pr) * h, 8), h)

    def fine_cells(c, carry):
        for pr in range(2):
            weight = [weight_at(1 + pr, c, o) for o in range(27)]
            for a in range(2 * ra):
                for pb in range(2):
                    at = (((pb * 2 * ra + a) * 8 + c) * 2 + pr) * h
                    total = fine_in[pl.ds(pl.multiple_of(at, 8), h), :]
                    for dr in range(3):
                        for da in range(3):
                            for db in range(3):
                                o = 9 * dr + 3 * da + db
                                total = total + weight[o] * mid_ext[pr + dr, a + da, pb + db]
                    cells[pb, cell_rows(a, c, pr), :] = total
        return carry

    lax.fori_loop(0, 8, fine_cells, 0)

    radial = (4 * (lax.broadcasted_iota(jnp.int32, (h, b), 0) // s_count)).astype(F32)

    def sum_before(x):
        step = s_count
        while step < h:
            x = x + along_rows(x, step)
            step *= 2
        return along_rows(x, s_count)

    def sum_all(x):
        step = s_count
        while step < h:
            x = x + pltpu.roll(x, step, axis=0)
            step *= 2
        return x

    def position(at, carry):
        a, pb = at // 4, lax.rem(at, 4)
        half = pb // 2
        rows = [cell_rows(a // 2, 4 * (f % 2) + 2 * lax.rem(a, 2) + lax.rem(pb, 2), f // 2) for f in range(4)]
        density = [jnp.exp(cells[half, rows[f], :]) for f in range(4)]
        layer = [spacing * d for d in density]
        depth = sum_before(layer[0] + layer[1] + layer[2] + layer[3])
        glow = []
        for f in range(4):
            where_emit = pl.multiple_of(((pb * 4 + f) * 4 * ra + a) * h, 8)
            glow.append(spacing * emit_in[pl.ds(where_emit, h), :] * jnp.exp(-depth))
            depth = depth + layer[f]
        running = sum_before(glow[0] + glow[1] + glow[2] + glow[3])
        column = []
        for f in range(4):
            running = running + glow[f]
            column.append(running)
        total = [jnp.zeros((h, b), F32) for f in range(4)]
        for star in range(g.stars):
            row = (star * 4 * ra + a) * 4 + pb
            bins = jnp.broadcast_to(block[pl.ds(begins["bins"] + row, 1), :], (h, b)) - radial
            data = jnp.broadcast_to(block[pl.ds(begins["data"] + row, 1), :], (h, b))
            mine = jnp.where(bins == 0, column[0], 0.0)
            for f in range(1, 4):
                mine = jnp.where(bins == f, column[f], mine)
            predicted = sum_all(mine)
            residual = data - predicted
            for s in range(s_count):
                seen[pb, pl.ds((s * g.stars + star) * 4 * ra + a, 1), :] = residual[s : s + 1]
            for f in range(4):
                total[f] = total[f] + jnp.where(bins > f, residual * (predicted - column[f]), 0.0)
        for f in range(4):
            cells[half, rows[f], :] = -density[f] * total[f]
        return carry

    lax.fori_loop(0, 16 * ra, position, 0)

    parts = [thirds(cells[phase]) for phase in range(2)]
    order = [place_columns(b, 2, phase) for phase in range(2)]
    for half in range(2):
        lanes = slice(half * b, (half + 1) * b)
        joined[half] = exact_dot(parts[0], order[0][:, lanes]) + exact_dot(parts[1], order[1][:, lanes])
    shown = None
    for phase in range(4):
        value = exact_dot(thirds(seen[phase]), place_columns(b, 4, phase))
        shown = value if shown is None else shown + value
    end_field, _ = large_back(g)
    per = 4 * g.stars * ra
    for r in range(n):
        for s in range(s_count):
            sub = r * s_count + s
            for half in range(2):
                for a in range(2 * ra):
                    at = ((half * 2 * ra + a) * s_count + s) * 16
                    stage[r, at : at + 16] = joined[half, pl.ds(a * 16 * h + sub, 16, stride=h), :]
            for part in range(4):
                at = end_field + (part * s_count + s) * per
                stage[r, at : at + per] = shown[s * per : (s + 1) * per, part * b : (part + 1) * b]
    for k in range(n):
        out_refs[k][...] = stage[lax.rem(me + k, n)]

    tall[...] = jnp.zeros(tall.shape, F32)
    for pr in range(2):
        def gather(c, carry, pr=pr):
            values = {(a, pb): cells[pb, cell_rows(a, c, pr), :] for a in range(2 * ra) for pb in range(2)}
            for dr in range(3):
                sums = {}
                for da in range(3):
                    for db in range(3):
                        weight = weight_at(1 + pr, c, 9 * dr + 3 * da + db)
                        for (a, pb), value in values.items():
                            key = (a + da, pb + db)
                            term = weight * value
                            sums[key] = sums[key] + term if key in sums else term
                for (row, bi), value in sums.items():
                    tall[pr + dr, row, bi] += value
            return carry

        lax.fori_loop(0, 8, gather, 0)
    for row in range(rows_a):
        for pr in range(2):
            for pb in range(2):
                bi, step_b = (3, 1) if pb == 0 else (0, -1)
                ri, step_r = (3, 1) if pr == 0 else (0, -1)
                close = tall[1 + pr, row, 1 + pb] + along_lanes(tall[1 + pr, row, bi], step_b)
                far = tall[ri, row, 1 + pb] + along_lanes(tall[ri, row, bi], step_b)
                value = close + along_rows(far, step_r * s_count)
                if row == 0:
                    value = value * top_in
                if row == rows_a - 1:
                    value = value * bottom_in
                at = ((2 * pr + pb) * rows_a + row) * h
                parent[at : at + h] = value

    coarse_sum[...] = jnp.zeros(coarse_sum.shape, F32)
    for dr in range(3):
        for db in range(3):
            sums = {}
            for c in range(8):
                cr, ca, cb = c // 4, c // 2 % 2, c % 2
                for da in range(3):
                    weight = weight_at(0, c, 9 * dr + 3 * da + db)
                    for row in range(1 - ca, rows_a, 2):
                        at = ((2 * cr + cb) * rows_a + row) * h
                        term = weight * parent[at : at + h]
                        key = (row - 1) // 2 + 1 + da
                        sums[key] = sums[key] + term if key in sums else term
            for a, value in sums.items():
                coarse_sum[a * h : (a + 1) * h] += along_lanes(along_rows(value, (dr - 1) * s_count), db - 1)

    edge_sum[...] = jnp.zeros(edge_sum.shape, F32)
    for q in range(g.w):
        @pl.when(worker == q)
        def _(q=q):
            low = q < g.w // 2
            if q == 0 or q == g.w - 1:
                for x in range(4):
                    at = (x * rows_a + (0 if low else rows_a - 1)) * h
                    edge_sum[x * h : (x + 1) * h] = parent[at : at + h]
            for t in range(2):
                a = (t - 2 if low else g.la + t) - q * ra + 2
                if 0 <= a < ra + 4:
                    edge_sum[(4 + t) * h : (5 + t) * h] = coarse_sum[a * h : (a + 1) * h]


def sums_kernel(g, parent, coarse_sum, edge_ref, *rest):
    out_refs, (stage,) = rest[: g.n], rest[g.n :]
    me, ang = lax.axis_index("rad"), lax.axis_index("ang")
    n, s_count, ra, h = g.n, g.s, g.ra, g.h
    rows_a = 2 * ra + 2
    live = jnp.where(jnp.minimum(me, g.w - 1) < g.w // 2, ang < g.m - 1, ang > 0)
    end_mid, end_coarse, _ = small_back(g)
    for r in range(n):
        for s in range(s_count):
            sub = r * s_count + s
            at = s * 4 * rows_a
            stage[r, at : at + 4 * rows_a] = parent[pl.ds(sub, 4 * rows_a, stride=h), :]
            at = end_mid + (ra + 4) * s
            stage[r, at : at + ra + 4] = coarse_sum[pl.ds(sub, ra + 4, stride=h), :]
            at = end_coarse + 6 * s
            stage[r, at : at + 6] = jnp.where(live, edge_ref[pl.ds(sub, 6, stride=h), :], 0.0)
    for k in range(n):
        out_refs[k][...] = stage[lax.rem(me + k, n)]


def owner_kernel(g, block, *rest):
    large_refs, small_refs, rest = rest[: g.n], rest[g.n : 2 * g.n], rest[2 * g.n :]
    coarse_out, mid_out, fine_out, resid_out, got, near, fine, grad_mid, grad_coarse = rest
    me = lax.axis_index("rad")
    n, b, s_count, ra, la = g.n, g.b, g.s, g.ra, g.la
    rows_a = 2 * ra + 2
    begins, _ = prepared_rows(g)
    end_field, _ = large_back(g)
    end_mid, end_coarse, _ = small_back(g)
    per = 4 * g.stars * ra
    for k in range(n):
        source = lax.rem(me + n - k, n)
        got[source] = large_refs[k][...]
        near[source] = small_refs[k][...]
    grad_mid[...] = jnp.zeros(grad_mid.shape, F32)
    grad_coarse[...] = jnp.zeros(grad_coarse.shape, F32)
    for q in range(g.w):
        low = q < g.w // 2
        for s in range(s_count):
            for half in range(2):
                for a in range(2 * ra):
                    at = ((half * 2 * ra + a) * s_count + s) * 16
                    rows = pl.ds(s * 32 * la + 2 * q * ra + a, 16, stride=2 * la)
                    fine[half, rows, :] = got[q, at : at + 16]
            for part in range(4):
                for star in range(g.stars):
                    at = end_field + (part * s_count + s) * per + star * 4 * ra
                    rows = slice(4 * q * ra, 4 * (q + 1) * ra)
                    resid_out[s, star, rows, part * b : (part + 1) * b] = got[q, at : at + 4 * ra]
            edge = near[q, end_coarse + 6 * s : end_coarse + 6 * s + 6]
            for x in range(4):
                at = s * 4 * rows_a + x * rows_a
                grad_mid[s, x, 2 * q * ra : 2 * q * ra + rows_a] += near[q, at : at + rows_a]
                row = 2 * la if low else 1
                grad_mid[s, x, row : row + 1] += edge[x : x + 1]
            at = end_mid + (ra + 4) * s
            grad_coarse[s, q * ra : q * ra + ra + 4] += near[q, at : at + ra + 4]
            row = la if low else 2
            grad_coarse[s, row : row + 2] += edge[4:6]
    for i in range(2):
        for j in range(8):
            rows = [begins["fine"] + 64 * i + 8 * c + j for c in range(8)]
            weight = [block[row : row + 1] for row in rows]
            for s in range(s_count):
                for half in range(2):
                    total = None
                    for c in range(8):
                        at = ((s * 8 + c) * 2 + i) * 2 * la
                        term = weight[c] * fine[half, at : at + 2 * la]
                        total = term if total is None else total + term
                    fine_out[s, j, i, :, half * b : (half + 1) * b] = total
    for s in range(s_count):
        coarse_out[s, 0] = grad_coarse[s, 2 : 2 + la]
        cells = []
        for c in range(8):
            cr, ca, cb = c // 4, c // 2 % 2, c % 2
            cells.append(grad_mid[s, 2 * cr + cb, pl.ds(1 + ca, la, stride=2), :])
        for j in range(8):
            row = begins["mid"] + j
            total = block[row : row + 1] * cells[0]
            for c in range(1, 8):
                total = total + block[row + 8 * c : row + 8 * c + 1] * cells[c]
            mid_out[s, j, 0] = total


def call(kernel, name, outs, operands, scratch, unmoved=0, written=0):
    vmem = pl.BlockSpec(memory_space=pltpu.VMEM)
    placed = pl.BlockSpec(memory_space=pl.ANY)
    limit = None if unmoved else VMEM_LIMIT
    return pl.pallas_call(
        kernel,
        name=name,
        out_shape=[jax.ShapeDtypeStruct(shape, kind) for shape, kind in outs],
        in_specs=[placed] * unmoved + [vmem] * (len(operands) - unmoved),
        out_specs=[placed] * written + [vmem] * (len(outs) - written),
        scratch_shapes=[pltpu.VMEM(shape, F32) if isinstance(shape, tuple) else shape for shape in scratch],
        compiler_params=pltpu.CompilerParams(vmem_limit_bytes=limit),
    )(*operands)


def per_device(
    g,
    coarse_field,
    excite_mid,
    excite_fine,
    kernels_mid,
    noise_mid,
    rows_mid,
    kernels_fine,
    noise_fine,
    rows_fine,
    emission,
    star_bins,
    star_data,
):
    n, m, s, la, b, stars, w, ra, h = g
    kernel = functools.partial
    rows_a = 2 * ra + 2
    pairs = [(i, i ^ 1) for i in range(m)]
    between = [(i, (i + 1) % m if i % 2 else (i - 1) % m) for i in range(m)]
    workers = [(r, a, 1 if min(r, w - 1) < w // 2 else -1) for r in range(n) for a in range(m)]
    sideways = [(r * m + a, r * m + (a - step) % m) for r, a, step in workers]

    def exchange(blocks):
        return [blocks[0]] + [lax.ppermute(blocks[k], "rad", [(i, (i + k) % n) for i in range(n)]) for k in range(1, n)]

    noise_mid, noise_fine = noise_mid.transpose(1, 2, 0), noise_fine.transpose(1, 2, 0)
    edge_rows = (eights(6 * s), b)
    large, small = (large_there(g)[-1], b), (small_there(g)[-1], b)
    sent = call(
        kernel(scatter_kernel, g),
        "scatter",
        [(large, F32)] * n,
        (rows_fine, noise_fine, excite_fine, emission),
        [
            pltpu.SMEM(rows_fine.shape, jnp.int32),
            noise_fine.shape,
            excite_fine.shape,
            emission.shape,
            pltpu.SemaphoreType.DMA((4,)),
            pltpu.SemaphoreType.DMA((n,)),
            (32 * s * la, 2 * b),
            (2, 32 * s * la, b),
            (4, 16 * la, b),
            (w, *large),
        ],
        unmoved=4,
        written=n,
    )
    got = exchange(sent)
    operands = (rows_mid, rows_fine, noise_mid, noise_fine, kernels_mid, kernels_fine)
    operands += (coarse_field, excite_mid, star_bins, star_data)
    one, two, block = call(
        kernel(prepare_kernel, g),
        "prepare",
        [(edge_rows, F32), (edge_rows, F32), ((prepared_rows(g)[1], b), F32)],
        (*operands, sent[0]),
        [
            *[(pltpu.SMEM if len(x.shape) == 1 else pltpu.VMEM)(x.shape, x.dtype) for x in operands],
            pltpu.SemaphoreType.DMA((10,)),
            (2, 4 * stars * ra, 4 * b),
        ],
        unmoved=11,
    )
    one, two = lax.ppermute(one, "ang", pairs), lax.ppermute(two, "ang", between)
    got += exchange(
        call(
            kernel(halo_kernel, g),
            "halos",
            [(small, F32)] * n,
            (block, one, two),
            [(s, la + 4, b), (w, *small)],
        )
    )
    (spread,) = call(kernel(weight_kernel, g), "weights", [((24 * 27, h, b), F32)], (block,), [])
    large_out = (large_back(g)[-1], b)
    *done, parent, coarse_sum, edge = call(
        kernel(main_kernel, g),
        "main",
        [(large_out, F32)] * n + [((4 * rows_a * h, b), F32), (((ra + 4) * h, b), F32), ((6 * h, b), F32)],
        (block, spread, *got),
        [
            (n, *large),
            (n, *small),
            (64 * ra * h, b),
            (64 * ra * h, b),
            (4 * rows_a * h, b),
            ((ra + 4) * h, b),
            (3, ra + 4, 3, h, b),
            (4, rows_a, 4, h, b),
            (4, rows_a, 4, h, b),
            (2, 32 * ra * h, b),
            (4, 4 * stars * ra * s, b),
            (2, 32 * ra * h, b),
            (n, *large_out),
        ],
    )
    large, small = (large_back(g)[-1], b), (small_back(g)[-1], b)
    got = exchange(done)
    edge = lax.ppermute(edge, ("rad", "ang"), sideways)
    got += exchange(
        call(
            kernel(sums_kernel, g),
            "sums",
            [(small, F32)] * n,
            (parent, coarse_sum, edge),
            [(n, *small)],
        )
    )
    return tuple(
        call(
            kernel(owner_kernel, g),
            "owner",
            [
                ((s, 1, la, b), F32),
                ((s, 8, 1, la, b), F32),
                ((s, 8, 2, 2 * la, 2 * b), F32),
                ((s, stars, 4 * la, 4 * b), F32),
            ],
            (block, *got),
            [(n, *large), (n, *small), (2, 32 * s * la, b), (s, 4, 2 * la + 2, b), (s, la + 4, b)],
        )
    )


def solution(mesh):
    placed = (
        P(None, "rad", "ang", None),
        P(None, None, "rad", "ang", None),
        P(None, None, "rad", "ang", None),
        P(),
        P(),
        P(),
        P(),
        P(),
        P(),
        P("rad", "ang", None),
        P(None, "ang", None),
        P(None, "ang", None),
    )

    def local(*args):
        return per_device(make_plan(mesh, args[0], args[10]), *args)

    return jax.shard_map(
        local,
        mesh=mesh,
        in_specs=placed,
        out_specs=(
            P(None, "rad", "ang", None),
            P(None, None, "rad", "ang", None),
            P(None, None, "rad", "ang", None),
            P(None, None, "ang", None),
        ),
        check_vma=False,
    )
```

time: 50.3 us -> 48.6 us (0.966)
  the two profiles are of different devices: /device:TPU:11 before, /device:TPU:0 now
where the time goes in v2:
time: 48.6 us; the launch traced here: 48.4 us
  starting transfers between devices  21.9 us (45%)
  waiting for transfers between devices  13.4 us (28%)
  Pallas kernels  11.4 us (23%)
  local copies, waits for them, and re-layouts  0.97 us (2%)
  between operations  0.73 us (2%)
    ppermute x12, starting transfers between devices, exchange(): lax.ppermute(blocks[k], 'rad', [(i, (i + k) % n) for i in range(n)])  19.3 us
    pallas_call x7, Pallas kernels, call(): pl.pallas_call(kernel, name=name, out_shape=[jax.ShapeDtypeStruct(shape,...  11.4 us
    ppermute x12, waiting for transfers between devices, exchange(): lax.ppermute(blocks[k], 'rad', [(i, (i + k) % n) for i in range(n)])  10.2 us
    ppermute x1, starting transfers between devices, per_device(): lax.ppermute(two, 'ang', between)  2.55 us
    ppermute x1, waiting for transfers between devices, per_device(): lax.ppermute(two, 'ang', between)  1.7 us
    ppermute x1, waiting for transfers between devices, per_device(): edge = lax.ppermute(edge, ('rad', 'ang'), sideways)  1.52 us
    unnamed x6, local copies, waits for them, and re-layouts  0.97 us
  transfers between devices with their start and end apart: 15, of which 7 were waited for; matrix products, arithmetic and copies ran while one was open for 0% of the time, Pallas kernels for 8%

profile of v2, /device:TPU:0, one launch (start us, length us, event | category | flops | bytes accessed | tf_op | source)
XLA Modules:
  0.0 48.4 jit_solution(823348738978988973)
XLA Ops:
  0.6 2.7 %scatter.1 = (f32[192,128]{1,0:T(8,128)}, f32[192,128]{1,0:T(8,128)}, f32[192,128]{1,0:T(8,128)}, f32[192,128]{1,0:T(8,128)}) custom-call(s32[8]{0:T(128)} %rest_1_.1, f32[8,8,16]{2,1,0:T(8,128)} %bitcast.2, f32[2,8,2,8,256]{4,3,2,1,0:T(8,128)} %fine_hbm.1, f32[4,16,512]{2,1,0:T(8,128)} %emission_hbm.1), custom_call_target="tpu_custom_call" | custom-call | tf_op jit(solution)/shard_map/scatter/pallas_call | solution.py:607
  3.4 0.0 copy-start.2
  3.4 3.1 %collective-permute-start = (f32[192,128]{1,0:T(8,128)}, f32[192,128]{1,0:T(8,128)S(1)}, u32[]{:S(2)}, u32[]{:S(2)}) collective-permute-start(f32[192,128]{1,0:T(8,128)} %get-tuple-element.28), channel_id=1, source_target_pairs={{0,8},{8,16},{16,24},{24,0},{1,9},{9,17},{17,25},{25,1},{2,10},{10... | collective-permute-start | bytes 294920 | tf_op jit(solution)/shard_map/ppermute | solution.py:642
  6.4 2.6 %collective-permute-start.1 = (f32[192,128]{1,0:T(8,128)}, f32[192,128]{1,0:T(8,128)S(1)}, u32[]{:S(2)}, u32[]{:S(2)}) collective-permute-start(f32[192,128]{1,0:T(8,128)} %get-tuple-element.29), channel_id=1, source_target_pairs={{0,16},{8,24},{16,0},{24,8},{1,17},{9,25},{17,1},{25,9},{2,18},{10... | collective-permute-start | bytes 294920 | tf_op jit(solution)/shard_map/ppermute | solution.py:642
  9.0 1.4 %collective-permute-start.2 = (f32[192,128]{1,0:T(8,128)}, f32[192,128]{1,0:T(8,128)S(1)}, u32[]{:S(2)}, u32[]{:S(2)}) collective-permute-start(f32[192,128]{1,0:T(8,128)} %get-tuple-element.30), channel_id=1, source_target_pairs={{0,24},{8,0},{16,8},{24,16},{1,25},{9,1},{17,9},{25,17},{2,26},{10... | collective-permute-start | bytes 294920 | tf_op jit(solution)/shard_map/ppermute | solution.py:642
  10.4 2.5 %prepare.1 = (f32[16,128]{1,0:T(8,128)}, f32[16,128]{1,0:T(8,128)}, f32[584,128]{1,0:T(8,128)}) custom-call(s32[4]{0:T(128)} %rest_0_.1, s32[8]{0:T(128)} %rest_1_.1, f32[8,8,16]{2,1,0:T(8,128)} %bitcast.4, f32[8,8,16]{2,1,0:T(8,128)} %bitcast.3, f32[16,8,27]{2,1,0:T(8,128)} %rest_4_.1, f32[16,8,27]{2,1,0:T(8,128)} %rest_5_.1, f32[2,1,4,128]{3,2,1,0:T(4,128)} %rest_6_.1, ...), custom_call_target="tpu_custom_call" | custom-call | tf_op jit(solution)/shard_map/prepare/pallas_call | solution.py:607
  12.9 0.1 collective-permute-start.3
  13.0 2.5 %collective-permute-start.4 = (f32[16,128]{1,0:T(8,128)}, f32[16,128]{1,0:T(8,128)S(1)}, u32[]{:S(2)}, u32[]{:S(2)}) collective-permute-start(f32[16,128]{1,0:T(8,128)} %get-tuple-element.32), channel_id=1, source_target_pairs={{0,7},{1,2},{2,1},{3,4},{4,3},{5,6},{6,5},{7,0},{8,15},{9,10},{10,... | collective-permute-start | bytes 24584 | tf_op jit(solution)/shard_map/ppermute | solution.py:682
  15.5 0.0 collective-permute-done.3.one_ref
  15.5 1.7 %collective-permute-done.4.two_ref = f32[16,128]{1,0:T(8,128)S(1)} collective-permute-done((f32[16,128]{1,0:T(8,128)}, f32[16,128]{1,0:T(8,128)S(1)}, u32[]{:S(2)}, u32[]{:S(2)}) %collective-permute-start.4) | collective-permute-done | bytes 8224 | tf_op jit(solution)/shard_map/ppermute | solution.py:682
  17.2 1.0 %copy-done = f32[584,128]{1,0:T(8,128)S(1)} copy-done((f32[584,128]{1,0:T(8,128)S(1)}, f32[584,128]{1,0:T(8,128)}, u32[]{:S(2)}) %copy-start) | copy-done | bytes 299032
  18.2 0.1 halos.1
  18.2 0.7 %collective-permute-start.5 = (f32[48,128]{1,0:T(8,128)S(1)}, f32[48,128]{1,0:T(8,128)S(1)}, u32[]{:S(2)}, u32[]{:S(2)}) collective-permute-start(f32[48,128]{1,0:T(8,128)S(1)} %get-tuple-element.34), channel_id=1, source_target_pairs={{0,8},{8,16},{16,24},{24,0},{1,9},{9,17},{17,25},{25,1},{2,10},{10... | collective-permute-start | bytes 73736 | tf_op jit(solution)/shard_map/ppermute | solution.py:642
  19.0 0.3 collective-permute-start.6
  19.3 4.7 %collective-permute-done.5.rest_5_ = f32[48,128]{1,0:T(8,128)S(1)} collective-permute-done((f32[48,128]{1,0:T(8,128)S(1)}, f32[48,128]{1,0:T(8,128)S(1)}, u32[]{:S(2)}, u32[]{:S(2)}) %collective-permute-start.5) | collective-permute-done | bytes 24608 | tf_op jit(solution)/shard_map/ppermute | solution.py:642
  24.0 0.0 collective-permute-start.7
  24.0 1.2 %weights.1.spread = f32[648,8,128]{2,1,0:T(8,128)S(1)} custom-call(f32[584,128]{1,0:T(8,128)S(1)} %copy-done), custom_call_target="tpu_custom_call" | custom-call | tf_op jit(solution)/shard_map/weights/pallas_call | solution.py:607
  25.2 0.0 collective-permute-done.6.rest_6_
  25.2 2.6 %collective-permute-done.7.rest_7_ = f32[48,128]{1,0:T(8,128)S(1)} collective-permute-done((f32[48,128]{1,0:T(8,128)S(1)}, f32[48,128]{1,0:T(8,128)S(1)}, u32[]{:S(2)}, u32[]{:S(2)}) %collective-permute-start.7) | collective-permute-done | bytes 24608 | tf_op jit(solution)/shard_map/ppermute | solution.py:642
  27.8 0.0 collective-permute-done.rest_1_
  27.8 3.8 %main.1 = (f32[256,128]{1,0:T(8,128)S(1)}, f32[256,128]{1,0:T(8,128)S(1)}, f32[256,128]{1,0:T(8,128)S(1)}, f32[256,128]{1,0:T(8,128)S(1)}, f32[128,128]{1,0:T(8,...) custom-call(f32[584,128]{1,0:T(8,128)S(1)} %copy-done.1, f32[648,8,128]{2,1,0:T(8,128)S(1)} %weights.1.spread, ...), custom_call_target="tpu_custom_call" | custom-call | tf_op jit(solution)/shard_map/main/pallas_call | solution.py:607
  31.7 0.1 collective-permute-start.8
  31.7 2.4 %collective-permute-start.9 = (f32[256,128]{1,0:T(8,128)S(1)}, f32[256,128]{1,0:T(8,128)S(1)}, u32[]{:S(2)}, u32[]{:S(2)}) collective-permute-start(f32[256,128]{1,0:T(8,128)S(1)} %get-tuple-element.39), channel_id=1, source_target_pairs={{0,16},{8,24},{16,0},{24,8},{1,17},{9,25},{17,1},{25,9},{2,18},{10... | collective-permute-start | bytes 393224 | tf_op jit(solution)/shard_map/ppermute | solution.py:642
  34.1 1.5 %collective-permute-start.10 = (f32[256,128]{1,0:T(8,128)S(1)}, f32[256,128]{1,0:T(8,128)S(1)}, u32[]{:S(2)}, u32[]{:S(2)}) collective-permute-start(f32[256,128]{1,0:T(8,128)S(1)} %get-tuple-element.40), channel_id=1, source_target_pairs={{0,24},{8,0},{16,8},{24,16},{1,25},{9,1},{17,9},{25,17},{2,26},{10... | collective-permute-start | bytes 393224 | tf_op jit(solution)/shard_map/ppermute | solution.py:642
  35.5 1.5 %collective-permute-done.11.edge_ref = f32[48,128]{1,0:T(8,128)S(1)} collective-permute-done((f32[48,128]{1,0:T(8,128)S(1)}, f32[48,128]{1,0:T(8,128)S(1)}, u32[]{:S(2)}, u32[]{:S(2)}) %collective-permute-start.11) | collective-permute-done | bytes 24608 | tf_op jit(solution)/shard_map/ppermute | solution.py:717
  37.1 0.6 %collective-permute-start.12 = (f32[56,128]{1,0:T(8,128)S(1)}, f32[56,128]{1,0:T(8,128)S(1)}, u32[]{:S(2)}, u32[]{:S(2)}) collective-permute-start(f32[56,128]{1,0:T(8,128)S(1)} %get-tuple-element.45), channel_id=1, source_target_pairs={{0,8},{8,16},{16,24},{24,0},{1,9},{9,17},{17,25},{25,1},{2,10},{10... | collective-permute-start | bytes 86024 | tf_op jit(solution)/shard_map/ppermute | solution.py:642
  37.7 4.2 %collective-permute-start.13 = (f32[56,128]{1,0:T(8,128)S(1)}, f32[56,128]{1,0:T(8,128)S(1)}, u32[]{:S(2)}, u32[]{:S(2)}) collective-permute-start(f32[56,128]{1,0:T(8,128)S(1)} %get-tuple-element.46), channel_id=1, source_target_pairs={{0,16},{8,24},{16,0},{24,8},{1,17},{9,25},{17,1},{25,9},{2,18},{10... | collective-permute-start | bytes 86024 | tf_op jit(solution)/shard_map/ppermute | solution.py:642
  41.9 1.3 %collective-permute-done.12.rest_5_ = f32[56,128]{1,0:T(8,128)S(1)} collective-permute-done((f32[56,128]{1,0:T(8,128)S(1)}, f32[56,128]{1,0:T(8,128)S(1)}, u32[]{:S(2)}, u32[]{:S(2)}) %collective-permute-start.12) | collective-permute-done | bytes 28704 | tf_op jit(solution)/shard_map/ppermute | solution.py:642
  43.2 2.5 %collective-permute-start.14 = (f32[56,128]{1,0:T(8,128)S(1)}, f32[56,128]{1,0:T(8,128)S(1)}, u32[]{:S(2)}, u32[]{:S(2)}) collective-permute-start(f32[56,128]{1,0:T(8,128)S(1)} %get-tuple-element.47), channel_id=1, source_target_pairs={{0,24},{8,0},{16,8},{24,16},{1,25},{9,1},{17,9},{25,17},{2,26},{10... | collective-permute-start | bytes 86024 | tf_op jit(solution)/shard_map/ppermute | solution.py:642
  45.7 0.2 collective-permute-done.13.rest_6_
  45.9 1.4 %collective-permute-done.14.rest_7_ = f32[56,128]{1,0:T(8,128)S(1)} collective-permute-done((f32[56,128]{1,0:T(8,128)S(1)}, f32[56,128]{1,0:T(8,128)S(1)}, u32[]{:S(2)}, u32[]{:S(2)}) %collective-permute-start.14) | collective-permute-done | bytes 28704 | tf_op jit(solution)/shard_map/ppermute | solution.py:642
  47.3 1.1 %owner.1 = (f32[2,1,4,128]{3,2,1,0:T(4,128)}, f32[2,8,1,4,128]{4,3,2,1,0:T(4,128)}, f32[2,8,2,8,256]{4,3,2,1,0:T(8,128)}, f32[2,4,16,512]{3,2,1,0:T(8,128)}) custom-call(f32[584,128]{1,0:T(8,128)S(1)} %copy-done.1, f32[256,128]{1,0:T(8,128)S(1)} %get-tuple-element.37.rest_0_, f32[256,128]{1,0:T(8,128)S(1)} %collective-permute-done.8.rest_1_, ...), custom_call_target="tpu_custom_call" | custom-call | tf_op jit(solution)/shard_map/owner/pallas_call | solution.py:607
  (11 shorter events, 0.1 us)
Async XLA Ops:
  3.4 24.5 %copy-start.2 = (f32[192,128]{1,0:T(8,128)S(1)}, f32[192,128]{1,0:T(8,128)}, u32[]{:S(2)}) copy-start(f32[192,128]{1,0:T(8,128)} %get-tuple-element.26.rest_10_.rest_0_) | copy-start | bytes 294916
  3.4 24.4 %collective-permute-start = (f32[192,128]{1,0:T(8,128)}, f32[192,128]{1,0:T(8,128)S(1)}, u32[]{:S(2)}, u32[]{:S(2)}) collective-permute-start(f32[192,128]{1,0:T(8,128)} %get-tuple-element.28), channel_id=1, source_target_pairs={{0,8},{8,16},{16,24},{24,0},{1,9},{9,17},{17,25},{25,1},{2,10},{10... | collective-permute-start | bytes 294920 | tf_op jit(solution)/shard_map/ppermute | solution.py:642
  6.4 21.4 %collective-permute-start.1 = (f32[192,128]{1,0:T(8,128)}, f32[192,128]{1,0:T(8,128)S(1)}, u32[]{:S(2)}, u32[]{:S(2)}) collective-permute-start(f32[192,128]{1,0:T(8,128)} %get-tuple-element.29), channel_id=1, source_target_pairs={{0,16},{8,24},{16,0},{24,8},{1,17},{9,25},{17,1},{25,9},{2,18},{10... | collective-permute-start | bytes 294920 | tf_op jit(solution)/shard_map/ppermute | solution.py:642
  9.0 18.8 %collective-permute-start.2 = (f32[192,128]{1,0:T(8,128)}, f32[192,128]{1,0:T(8,128)S(1)}, u32[]{:S(2)}, u32[]{:S(2)}) collective-permute-start(f32[192,128]{1,0:T(8,128)} %get-tuple-element.30), channel_id=1, source_target_pairs={{0,24},{8,0},{16,8},{24,16},{1,25},{9,1},{17,9},{25,17},{2,26},{10... | collective-permute-start | bytes 294920 | tf_op jit(solution)/shard_map/ppermute | solution.py:642
  12.9 2.6 %collective-permute-start.3 = (f32[16,128]{1,0:T(8,128)}, f32[16,128]{1,0:T(8,128)S(1)}, u32[]{:S(2)}, u32[]{:S(2)}) collective-permute-start(f32[16,128]{1,0:T(8,128)} %get-tuple-element.31), channel_id=1, source_target_pairs={{0,1},{1,0},{2,3},{3,2},{4,5},{5,4},{6,7},{7,6},{8,9},{9,8},{10,11... | collective-permute-start | bytes 24584 | tf_op jit(solution)/shard_map/ppermute | solution.py:682
  13.0 4.3 %collective-permute-start.4 = (f32[16,128]{1,0:T(8,128)}, f32[16,128]{1,0:T(8,128)S(1)}, u32[]{:S(2)}, u32[]{:S(2)}) collective-permute-start(f32[16,128]{1,0:T(8,128)} %get-tuple-element.32), channel_id=1, source_target_pairs={{0,7},{1,2},{2,1},{3,4},{4,3},{5,6},{6,5},{7,0},{8,15},{9,10},{10,... | collective-permute-start | bytes 24584 | tf_op jit(solution)/shard_map/ppermute | solution.py:682
  17.2 1.0 %copy-start = (f32[584,128]{1,0:T(8,128)S(1)}, f32[584,128]{1,0:T(8,128)}, u32[]{:S(2)}) copy-start(f32[584,128]{1,0:T(8,128)} %get-tuple-element.27.block) | copy-start | bytes 897028
  18.2 9.7 %copy-start.1 = (f32[584,128]{1,0:T(8,128)S(1)}, f32[584,128]{1,0:T(8,128)}, u32[]{:S(2)}) copy-start(f32[584,128]{1,0:T(8,128)} %get-tuple-element.27.block) | copy-start | bytes 897028
  18.2 5.7 %collective-permute-start.5 = (f32[48,128]{1,0:T(8,128)S(1)}, f32[48,128]{1,0:T(8,128)S(1)}, u32[]{:S(2)}, u32[]{:S(2)}) collective-permute-start(f32[48,128]{1,0:T(8,128)S(1)} %get-tuple-element.34), channel_id=1, source_target_pairs={{0,8},{8,16},{16,24},{24,0},{1,9},{9,17},{17,25},{25,1},{2,10},{10... | collective-permute-start | bytes 73736 | tf_op jit(solution)/shard_map/ppermute | solution.py:642
  19.0 6.2 %collective-permute-start.6 = (f32[48,128]{1,0:T(8,128)S(1)}, f32[48,128]{1,0:T(8,128)S(1)}, u32[]{:S(2)}, u32[]{:S(2)}) collective-permute-start(f32[48,128]{1,0:T(8,128)S(1)} %get-tuple-element.35), channel_id=1, source_target_pairs={{0,16},{8,24},{16,0},{24,8},{1,17},{9,25},{17,1},{25,9},{2,18},{10... | collective-permute-start | bytes 73736 | tf_op jit(solution)/shard_map/ppermute | solution.py:642
  24.0 3.8 %collective-permute-start.7 = (f32[48,128]{1,0:T(8,128)S(1)}, f32[48,128]{1,0:T(8,128)S(1)}, u32[]{:S(2)}, u32[]{:S(2)}) collective-permute-start(f32[48,128]{1,0:T(8,128)S(1)} %get-tuple-element.36), channel_id=1, source_target_pairs={{0,24},{8,0},{16,8},{24,16},{1,25},{9,1},{17,9},{25,17},{2,26},{10... | collective-permute-start | bytes 73736 | tf_op jit(solution)/shard_map/ppermute | solution.py:642
  31.7 15.6 %collective-permute-start.8 = (f32[256,128]{1,0:T(8,128)S(1)}, f32[256,128]{1,0:T(8,128)S(1)}, u32[]{:S(2)}, u32[]{:S(2)}) collective-permute-start(f32[256,128]{1,0:T(8,128)S(1)} %get-tuple-element.38), channel_id=1, source_target_pairs={{0,8},{8,16},{16,24},{24,0},{1,9},{9,17},{17,25},{25,1},{2,10},{10... | collective-permute-start | bytes 393224 | tf_op jit(solution)/shard_map/ppermute | solution.py:642
  31.7 15.6 %collective-permute-start.9 = (f32[256,128]{1,0:T(8,128)S(1)}, f32[256,128]{1,0:T(8,128)S(1)}, u32[]{:S(2)}, u32[]{:S(2)}) collective-permute-start(f32[256,128]{1,0:T(8,128)S(1)} %get-tuple-element.39), channel_id=1, source_target_pairs={{0,16},{8,24},{16,0},{24,8},{1,17},{9,25},{17,1},{25,9},{2,18},{10... | collective-permute-start | bytes 393224 | tf_op jit(solution)/shard_map/ppermute | solution.py:642
  34.1 13.2 %collective-permute-start.10 = (f32[256,128]{1,0:T(8,128)S(1)}, f32[256,128]{1,0:T(8,128)S(1)}, u32[]{:S(2)}, u32[]{:S(2)}) collective-permute-start(f32[256,128]{1,0:T(8,128)S(1)} %get-tuple-element.40), channel_id=1, source_target_pairs={{0,24},{8,0},{16,8},{24,16},{1,25},{9,1},{17,9},{25,17},{2,26},{10... | collective-permute-start | bytes 393224 | tf_op jit(solution)/shard_map/ppermute | solution.py:642
  35.5 1.5 %collective-permute-start.11 = (f32[48,128]{1,0:T(8,128)S(1)}, f32[48,128]{1,0:T(8,128)S(1)}, u32[]{:S(2)}, u32[]{:S(2)}) collective-permute-start(f32[48,128]{1,0:T(8,128)S(1)} %get-tuple-element.43), channel_id=1, source_target_pairs={{0,7},{1,0},{2,1},{3,2},{4,3},{5,4},{6,5},{7,6},{8,15},{9,8},{10,9... | collective-permute-start | bytes 73736 | tf_op jit(solution)/shard_map/ppermute | solution.py:717
  37.1 6.1 %collective-permute-start.12 = (f32[56,128]{1,0:T(8,128)S(1)}, f32[56,128]{1,0:T(8,128)S(1)}, u32[]{:S(2)}, u32[]{:S(2)}) collective-permute-start(f32[56,128]{1,0:T(8,128)S(1)} %get-tuple-element.45), channel_id=1, source_target_pairs={{0,8},{8,16},{16,24},{24,0},{1,9},{9,17},{17,25},{25,1},{2,10},{10... | collective-permute-start | bytes 86024 | tf_op jit(solution)/shard_map/ppermute | solution.py:642
  37.7 8.2 %collective-permute-start.13 = (f32[56,128]{1,0:T(8,128)S(1)}, f32[56,128]{1,0:T(8,128)S(1)}, u32[]{:S(2)}, u32[]{:S(2)}) collective-permute-start(f32[56,128]{1,0:T(8,128)S(1)} %get-tuple-element.46), channel_id=1, source_target_pairs={{0,16},{8,24},{16,0},{24,8},{1,17},{9,25},{17,1},{25,9},{2,18},{10... | collective-permute-start | bytes 86024 | tf_op jit(solution)/shard_map/ppermute | solution.py:642
  43.2 4.1 %collective-permute-start.14 = (f32[56,128]{1,0:T(8,128)S(1)}, f32[56,128]{1,0:T(8,128)S(1)}, u32[]{:S(2)}, u32[]{:S(2)}) collective-permute-start(f32[56,128]{1,0:T(8,128)S(1)} %get-tuple-element.47), channel_id=1, source_target_pairs={{0,24},{8,0},{16,8},{24,16},{1,25},{9,1},{17,9},{25,17},{2,26},{10... | collective-permute-start | bytes 86024 | tf_op jit(solution)/shard_map/ppermute | solution.py:642

commit v3 on v2

--- a/solution.py
+++ b/solution.py
@@ -30,7 +30,7 @@
     s, rows, la, b = coarse.shape
     w = max(d for d in range(1, min(n, la) + 1) if la % d == 0)
     ra = la // w
-    assert rows == 1 and m % 2 == 0 and w % 2 == 0 and (w // 2) * ra >= 2
+    assert rows == 1 and n & (n - 1) == 0 and w % 2 == 0 and (w // 2) * ra >= 2
     return Plan(n, m, s, la, b, star_bins.shape[0], w, ra, n * s)
 
 
@@ -40,17 +40,14 @@
 
 def large_there(g):
     fine = 2 * 2 * g.ra * g.s * 16
-    return fine, fine + 16 * 4 * g.ra
-
-
-def small_there(g):
-    mix = g.s * 4 * (2 * g.ra + 2)
-    return mix, eights(mix + g.s * (g.ra + 4))
+    emit = fine + 16 * 4 * g.ra
+    mix = emit + g.s * 4 * (2 * g.ra + 2)
+    coarse = mix + g.s * (g.ra + 4)
+    return fine, emit, mix, coarse, eights(coarse + 6 * g.s)
 
 
 def large_back(g):
-    field = 2 * 2 * g.ra * g.s * 16
-    return field, field + 4 * g.s * g.stars * 4 * g.ra
+    return 2 * 2 * g.ra * g.s * 16, 4 * g.s * 4 * g.stars * g.ra
 
 
 def small_back(g):
@@ -61,8 +58,6 @@
 
 def prepared_rows(g):
     sizes = dict(
-        mixed=8 * g.s * g.la,
-        coarse=eights(g.s * g.la),
         stencil=24 * g.h,
         bins=16 * g.stars * g.ra,
         data=16 * g.stars * g.ra,
@@ -139,40 +134,16 @@
 
 
 def prepare_kernel(g, *rest):
-    sources, (one_ref, two_ref, block), rest = rest[:10], rest[11:14], rest[14:]
-    held, (sems, gathered) = rest[:10], rest[10:]
+    sources, block, rest = rest[:8], rest[9], rest[10:]
+    held, (sems, gathered) = rest[:8], rest[8:]
     copies = start_all(list(zip(sources, held)), sems)
-    rows_mid, rows_fine, noise_mid, noise_fine, mid_table, fine_table = held[:6]
-    coarse_ref, excite_ref, bins_ref, data_ref = held[6:]
+    rows_mid, rows_fine, noise_mid, noise_fine, mid_table, fine_table, bins_ref, data_ref = held
     begins, _ = prepared_rows(g)
     me = lax.axis_index("rad")
-    even = lax.rem(lax.axis_index("ang"), 2) == 0
     worker = jnp.minimum(me, g.w - 1)
     per, b = 4 * g.ra, g.b
     choices = [pick_columns(b, 4, phase) for phase in range(4)]
     wait_all(copies)
-    weight = table_weights(noise_mid, rows_mid[me])
-    for c in range(8):
-        for s in range(g.s):
-            total = weight(c, 0) * excite_ref[s, 0, 0]
-            for j in range(1, 8):
-                total = total + weight(c, j) * excite_ref[s, j, 0]
-            at = begins["mixed"] + (s * 8 + c) * g.la
-            block[at : at + g.la] = total
-    for s in range(g.s):
-        up, down = coarse_ref[s, 0, g.la - 2 :], coarse_ref[s, 0, :2]
-        one_ref[2 * s : 2 * s + 2] = jnp.where(even, up, down)
-        two_ref[2 * s : 2 * s + 2] = jnp.where(even, down, up)
-        for cr in range(2):
-            for cb in range(2):
-                at = 2 * g.s + 4 * s + 2 * cr + cb
-                last = begins["mixed"] + (s * 8 + 4 * cr + 2 + cb) * g.la + g.la - 1
-                leading = begins["mixed"] + (s * 8 + 4 * cr + cb) * g.la
-                up, down = block[last : last + 1], block[leading : leading + 1]
-                one_ref[at : at + 1] = jnp.where(even, up, down)
-                two_ref[at : at + 1] = jnp.where(even, down, up)
-        at = begins["coarse"] + s * g.la
-        block[at : at + g.la] = coarse_ref[s, 0]
     for r in range(g.n):
         tables = [mid_table[rows_mid[r]], fine_table[rows_fine[2 * r]], fine_table[rows_fine[2 * r + 1]]]
         for level, table in enumerate(tables):
@@ -201,14 +172,14 @@
         block[rows, :] = exact_dot(parts, choices[phase])
 
 
-def scatter_kernel(g, rows_hbm, noise_hbm, fine_hbm, emission_hbm, *rest):
-    out_refs, rest = rest[: g.n], rest[g.n :]
-    rows_ref, noise_ref, fine_ref, emission_ref, sems, out_sems, raw, split, lit, stage = rest
-    operands = [(emission_hbm, emission_ref), (rows_hbm, rows_ref), (noise_hbm, noise_ref), (fine_hbm, fine_ref)]
-    copies = start_all(operands, sems)
+def scatter_kernel(g, *rest):
+    sources, out_refs, rest = rest[:8], rest[8 : 8 + g.n], rest[8 + g.n :]
+    held, (sems, out_sems, raw, split, lit, stage, mixed, wide) = rest[:8], rest[8:]
+    copies = start_all(list(zip(sources, held)), sems)
+    emission_ref, rows_mid, noise_mid, coarse_ref, excite_ref, rows_ref, noise_ref, fine_ref = held
     me = lax.axis_index("rad")
     b, s_count, la = g.b, g.s, g.la
-    end_fine, _ = large_there(g)
+    end_fine, end_emit, end_mix, end_coarse, _ = large_there(g)
     choices = [pick_columns(b, 4, phase) for phase in range(4)]
     copies[0].wait()
     parts = thirds(emission_ref[...].reshape(16 * la, 4 * b))
@@ -220,7 +191,40 @@
                 at = end_fine + (phase * 4 + f) * 4 * g.ra
                 rows = slice(f * 4 * la + 4 * q * g.ra, f * 4 * la + 4 * (q + 1) * g.ra)
                 stage[q, at : at + 4 * g.ra] = lit[phase, rows]
-    wait_all(copies[1:])
+    wait_all(copies[1:5])
+    weight = table_weights(noise_mid, rows_mid[me])
+    for c in range(8):
+        for s in range(s_count):
+            total = weight(c, 0) * excite_ref[s, 0, 0]
+            for j in range(1, 8):
+                total = total + weight(c, j) * excite_ref[s, j, 0]
+            mixed[s, c] = total
+    wide[...] = jnp.zeros(wide.shape, F32)
+    for s in range(s_count):
+        wide[s, 2 : 2 + la] = coarse_ref[s, 0]
+    for q in range(g.w):
+        low = q < g.w // 2
+        for s in range(s_count):
+            for row in range(2 * g.ra + 2):
+                a, ca = divmod(2 * q * g.ra - 1 + row, 2)
+                for cr in range(2):
+                    for cb in range(2):
+                        at = end_emit + ((s * (2 * g.ra + 2) + row) * 2 + cr) * 2 + cb
+                        if 0 <= a < la:
+                            stage[q, at : at + 1] = mixed[s, 4 * cr + 2 * ca + cb, a : a + 1]
+                        else:
+                            stage[q, at : at + 1] = jnp.zeros((1, b), F32)
+            at = end_mix + (g.ra + 4) * s
+            stage[q, at : at + g.ra + 4] = wide[s, q * g.ra : q * g.ra + g.ra + 4]
+            at = end_coarse + 6 * s
+            row = la - 1 if low else 0
+            for cr in range(2):
+                for cb in range(2):
+                    c = 4 * cr + (2 if low else 0) + cb
+                    stage[q, at + 2 * cr + cb : at + 2 * cr + cb + 1] = mixed[s, c, row : row + 1]
+            row = la - 2 if low else 0
+            stage[q, at + 4 : at + 6] = coarse_ref[s, 0, row : row + 2]
+    wait_all(copies[5:])
     for i in range(2):
         weight = table_weights(noise_ref, rows_ref[2 * me + i])
         for c in range(8):
@@ -245,42 +249,40 @@
     wait_all(start_all([(stage.at[worker], out) for worker, out in zip(workers, out_refs)], out_sems))
 
 
-def halo_kernel(g, block, one_ref, two_ref, *rest):
-    out_refs, (wide, stage) = rest[: g.n], rest[g.n :]
-    begins, _ = prepared_rows(g)
-    me, ang = lax.axis_index("rad"), lax.axis_index("ang")
-    even = lax.rem(ang, 2) == 0
-    before = jnp.where(ang > 0, jnp.where(even, two_ref[...], one_ref[...]), 0.0)
-    after = jnp.where(ang < g.m - 1, jnp.where(even, one_ref[...], two_ref[...]), 0.0)
-    for s in range(g.s):
-        wide[s, :2] = before[2 * s : 2 * s + 2]
-        at = begins["coarse"] + s * g.la
-        wide[s, 2 : 2 + g.la] = block[at : at + g.la]
-        wide[s, 2 + g.la :] = after[2 * s : 2 * s + 2]
-    end_mix, _ = small_there(g)
-    for q in range(g.w):
+def relay_kernel(g, *rest):
+    in_refs, (edge_out,) = rest[: g.n], rest[g.n :]
+    me = lax.axis_index("rad")
+    _, _, _, end_coarse, _ = large_there(g)
+    for k in range(g.n):
+        source = lax.rem(me + g.n - k, g.n)
         for s in range(g.s):
-            for row in range(2 * g.ra + 2):
-                a, ca = divmod(2 * q * g.ra - 1 + row, 2)
-                for cr in range(2):
-                    for cb in range(2):
-                        at = ((s * (2 * g.ra + 2) + row) * 2 + cr) * 2 + cb
-                        edge = 2 * g.s + 4 * s + 2 * cr + cb
-                        if a < 0:
-                            value = before[edge : edge + 1]
-                        elif a >= g.la:
-                            value = after[edge : edge + 1]
-                        else:
-                            own = begins["mixed"] + (s * 8 + 4 * cr + 2 * ca + cb) * g.la + a
-                            value = block[own : own + 1]
-                        stage[q, at : at + 1] = value
-            at = end_mix + (g.ra + 4) * s
-            stage[q, at : at + g.ra + 4] = wide[s, q * g.ra : q * g.ra + g.ra + 4]
+            rows = pl.ds(source * g.s + s, 6, stride=g.h)
+            edge_out[rows, :] = in_refs[k][end_coarse + 6 * s : end_coarse + 6 * s + 6]
+
+
+def unpack_kernel(g, *rest):
+    in_refs, (fine_out, emit_out, mix_out, coarse_out) = rest[: g.n], rest[g.n :]
+    me = lax.axis_index("rad")
+    end_fine, end_emit, end_mix, _, _ = large_there(g)
+    h, ra, rows_a = g.h, g.ra, 2 * g.ra + 2
     for k in range(g.n):
-        out_refs[k][...] = stage[jnp.minimum(lax.rem(me + k, g.n), g.w - 1)]
-
-
-def weight_kernel(g, block, spread):
+        source = lax.rem(me + g.n - k, g.n)
+        got = in_refs[k]
+        for s in range(g.s):
+            sub = source * g.s + s
+            for x in range(4 * ra):
+                at = (x * g.s + s) * 16
+                fine_out[pl.ds(x * 16 * h + sub, 16, stride=h), :] = got[at : at + 16]
+            emit_out[pl.ds(sub, 64 * ra, stride=h), :] = got[end_fine:end_emit]
+            at = end_emit + s * 4 * rows_a
+            mix_out[pl.ds(sub, 4 * rows_a, stride=h), :] = got[at : at + 4 * rows_a]
+            at = end_mix + (ra + 4) * s
+            coarse_out[pl.ds(sub, ra + 4, stride=h), :] = got[at : at + ra + 4]
+
+
+def weight_kernel(g, block, own, spread, own_out, block_out):
+    own_out[...] = own[...]
+    block_out[...] = block[...]
     begins, _ = prepared_rows(g)
     for x in range(24):
         at = begins["stencil"] + x * g.h
@@ -291,9 +293,9 @@
 
 def main_kernel(g, block, spread, *rest):
     n, b, s_count, ra, h = g.n, g.b, g.s, g.ra, g.h
-    large_refs, small_refs, out_refs, rest = rest[:n], rest[n : 2 * n], rest[2 * n : 3 * n], rest[3 * n :]
-    parent, coarse_sum, edge_sum = rest[:3]
-    got, near, fine_in, emit_in, mix_in, coarse_in, coarse_ext, mid_ext, tall, cells, seen, joined, stage = rest[3:]
+    fine_in, emit_in, mixed, coarse, near = rest[:5]
+    out_refs, (resid_out, parent, coarse_sum, edge_sum), rest = rest[5 : 5 + n], rest[5 + n : 9 + n], rest[9 + n :]
+    mix_in, coarse_in, coarse_ext, mid_ext, tall, cells, seen, joined, stage = rest
     me, ang = lax.axis_index("rad"), lax.axis_index("ang")
     rows_a = 2 * ra + 2
     spacing = 1.0 / (4 * n)
@@ -303,19 +305,21 @@
     def weight_at(level, c, o):
         return spread[(level * 8 + c) * 27 + o]
 
-    for k in range(n):
-        source = lax.rem(me + n - k, n)
-        got[source] = large_refs[k][...]
-        near[source] = small_refs[k][...]
-    end_fine, end_emit = large_there(g)
-    end_mix, _ = small_there(g)
-    for r in range(n):
-        for s in range(s_count):
-            sub = r * s_count + s
-            at = s * 4 * rows_a
-            mix_in[pl.ds(sub, 4 * rows_a, stride=h), :] = near[r, at : at + 4 * rows_a]
-            at = end_mix + (ra + 4) * s
-            coarse_in[pl.ds(sub, ra + 4, stride=h), :] = near[r, at : at + ra + 4]
+    mix_in[...] = mixed[...]
+    coarse_in[...] = coarse[...]
+    live = jnp.where(worker < g.w // 2, ang > 0, ang < g.m - 1)
+    for q in range(g.w):
+        @pl.when(jnp.logical_and(worker == q, live))
+        def _(q=q):
+            if q == 0:
+                mix_in[: 4 * h] = near[: 4 * h]
+            if q == g.w - 1:
+                mix_in[4 * (rows_a - 1) * h :] = near[: 4 * h]
+            for a in range(ra + 4):
+                row = q * ra - 2 + a
+                if row < 0 or row >= g.la:
+                    at = (4 + (row + 2 if row < 0 else row - g.la)) * h
+                    coarse_in[a * h : (a + 1) * h] = near[at : at + h]
 
     first = ang * g.la + worker * ra
     top_in = jnp.where(first > 0, 1.0, 0.0).astype(F32)
@@ -346,14 +350,6 @@
                 for ri, step_r in ((1 + cr, 0), (3, -1) if cr == 0 else (0, 1)):
                     mid_ext[ri, row, bi] = along_rows(shifted, step_r * s_count)
 
-    for r in range(n):
-        for s in range(s_count):
-            sub = r * s_count + s
-            for x in range(4 * ra):
-                at = (x * s_count + s) * 16
-                fine_in[pl.ds(x * 16 * h + sub, 16, stride=h), :] = got[r, at : at + 16]
-            emit_in[pl.ds(sub, 64 * ra, stride=h), :] = got[r, end_fine:end_emit]
-
     def cell_rows(a, c, pr):
         return pl.ds(pl.multiple_of(((a * 8 + c) * 2 + pr) * h, 8), h)
 
@@ -390,42 +386,54 @@
             step *= 2
         return x
 
-    def position(at, carry):
-        a, pb = at // 4, lax.rem(at, 4)
-        half = pb // 2
-        rows = [cell_rows(a // 2, 4 * (f % 2) + 2 * lax.rem(a, 2) + lax.rem(pb, 2), f // 2) for f in range(4)]
-        density = [jnp.exp(cells[half, rows[f], :]) for f in range(4)]
-        layer = [spacing * d for d in density]
-        depth = sum_before(layer[0] + layer[1] + layer[2] + layer[3])
-        glow = []
-        for f in range(4):
-            where_emit = pl.multiple_of(((pb * 4 + f) * 4 * ra + a) * h, 8)
-            glow.append(spacing * emit_in[pl.ds(where_emit, h), :] * jnp.exp(-depth))
-            depth = depth + layer[f]
-        running = sum_before(glow[0] + glow[1] + glow[2] + glow[3])
+    def positions(at, carry):
+        a, half = at // 2, lax.rem(at, 2)
+        spots = []
+        for cb in range(2):
+            pb = 2 * half + cb
+            rows = [cell_rows(a // 2, 4 * (f % 2) + 2 * lax.rem(a, 2) + cb, f // 2) for f in range(4)]
+            emit = [pl.multiple_of(((pb * 4 + f) * 4 * ra + a) * h, 8) for f in range(4)]
+            stars = [(star * 4 * ra + a) * 4 + pb for star in range(g.stars)]
+            spots.append((pb, rows, emit, stars))
+        density = [[jnp.exp(cells[half, rows[f], :]) for f in range(4)] for _, rows, _, _ in spots]
+        glow = [[spacing * emit_in[pl.ds(emit[f], h), :] for f in range(4)] for _, _, emit, _ in spots]
+        bins = [[block[pl.ds(begins["bins"] + row, 1), :] for row in stars] for _, _, _, stars in spots]
+        data = [[block[pl.ds(begins["data"] + row, 1), :] for row in stars] for _, _, _, stars in spots]
         column = []
-        for f in range(4):
-            running = running + glow[f]
-            column.append(running)
-        total = [jnp.zeros((h, b), F32) for f in range(4)]
+        for d, light in zip(density, glow):
+            layer = [spacing * x for x in d]
+            depth = sum_before(layer[0] + layer[1] + layer[2] + layer[3])
+            for f in range(4):
+                light[f] = light[f] * jnp.exp(-depth)
+                depth = depth + layer[f]
+            running = sum_before(light[0] + light[1] + light[2] + light[3])
+            column.append([])
+            for f in range(4):
+                running = running + light[f]
+                column[-1].append(running)
+        total = [[jnp.zeros((h, b), F32) for f in range(4)] for _ in spots]
+        seen_at = []
         for star in range(g.stars):
-            row = (star * 4 * ra + a) * 4 + pb
-            bins = jnp.broadcast_to(block[pl.ds(begins["bins"] + row, 1), :], (h, b)) - radial
-            data = jnp.broadcast_to(block[pl.ds(begins["data"] + row, 1), :], (h, b))
-            mine = jnp.where(bins == 0, column[0], 0.0)
-            for f in range(1, 4):
-                mine = jnp.where(bins == f, column[f], mine)
-            predicted = sum_all(mine)
-            residual = data - predicted
+            for x, (pb, _, _, _) in enumerate(spots):
+                bin_here = jnp.broadcast_to(bins[x][star], (h, b)) - radial
+                mine = jnp.where(bin_here == 0, column[x][0], 0.0)
+                for f in range(1, 4):
+                    mine = jnp.where(bin_here == f, column[x][f], mine)
+                predicted = sum_all(mine)
+                residual = jnp.broadcast_to(data[x][star], (h, b)) - predicted
+                seen_at.append((pb, star, residual))
+                for f in range(4):
+                    term = residual * (predicted - column[x][f])
+                    total[x][f] = total[x][f] + jnp.where(bin_here > f, term, 0.0)
+        for pb, star, residual in seen_at:
             for s in range(s_count):
                 seen[pb, pl.ds((s * g.stars + star) * 4 * ra + a, 1), :] = residual[s : s + 1]
+        for x, (_, rows, _, _) in enumerate(spots):
             for f in range(4):
-                total[f] = total[f] + jnp.where(bins > f, residual * (predicted - column[f]), 0.0)
-        for f in range(4):
-            cells[half, rows[f], :] = -density[f] * total[f]
+                cells[half, rows[f], :] = -density[x][f] * total[x][f]
         return carry
 
-    lax.fori_loop(0, 16 * ra, position, 0)
+    lax.fori_loop(0, 8 * ra, positions, 0)
 
     parts = [thirds(cells[phase]) for phase in range(2)]
     order = [place_columns(b, 2, phase) for phase in range(2)]
@@ -436,8 +444,9 @@
     for phase in range(4):
         value = exact_dot(thirds(seen[phase]), place_columns(b, 4, phase))
         shown = value if shown is None else shown + value
-    end_field, _ = large_back(g)
-    per = 4 * g.stars * ra
+    per = 4 * g.stars * ra * s_count
+    for part in range(4):
+        resid_out[part * per : (part + 1) * per] = shown[:, part * b : (part + 1) * b]
     for r in range(n):
         for s in range(s_count):
             sub = r * s_count + s
@@ -445,9 +454,6 @@
                 for a in range(2 * ra):
                     at = ((half * 2 * ra + a) * s_count + s) * 16
                     stage[r, at : at + 16] = joined[half, pl.ds(a * 16 * h + sub, 16, stride=h), :]
-            for part in range(4):
-                at = end_field + (part * s_count + s) * per
-                stage[r, at : at + per] = shown[s * per : (s + 1) * per, part * b : (part + 1) * b]
     for k in range(n):
         out_refs[k][...] = stage[lax.rem(me + k, n)]
 
@@ -535,24 +541,18 @@
         out_refs[k][...] = stage[lax.rem(me + k, n)]
 
 
-def owner_kernel(g, block, *rest):
-    large_refs, small_refs, rest = rest[: g.n], rest[g.n : 2 * g.n], rest[2 * g.n :]
-    coarse_out, mid_out, fine_out, resid_out, got, near, fine, grad_mid, grad_coarse = rest
+def large_owner_kernel(g, block, *rest):
+    in_refs, shown_refs, rest = rest[: g.n], rest[g.n : 2 * g.n], rest[2 * g.n :]
+    fine_out, resid_out, mid_mix, got, shown, fine = rest
     me = lax.axis_index("rad")
     n, b, s_count, ra, la = g.n, g.b, g.s, g.ra, g.la
-    rows_a = 2 * ra + 2
     begins, _ = prepared_rows(g)
-    end_field, _ = large_back(g)
-    end_mid, end_coarse, _ = small_back(g)
     per = 4 * g.stars * ra
+    mid_mix[...] = block[begins["mid"] : begins["mid"] + 64]
     for k in range(n):
-        source = lax.rem(me + n - k, n)
-        got[source] = large_refs[k][...]
-        near[source] = small_refs[k][...]
-    grad_mid[...] = jnp.zeros(grad_mid.shape, F32)
-    grad_coarse[...] = jnp.zeros(grad_coarse.shape, F32)
+        got[lax.rem(me + n - k, n)] = in_refs[k][...]
+        shown[me ^ k] = shown_refs[k][...]
     for q in range(g.w):
-        low = q < g.w // 2
         for s in range(s_count):
             for half in range(2):
                 for a in range(2 * ra):
@@ -561,19 +561,9 @@
                     fine[half, rows, :] = got[q, at : at + 16]
             for part in range(4):
                 for star in range(g.stars):
-                    at = end_field + (part * s_count + s) * per + star * 4 * ra
+                    at = (part * s_count + s) * per + star * 4 * ra
                     rows = slice(4 * q * ra, 4 * (q + 1) * ra)
-                    resid_out[s, star, rows, part * b : (part + 1) * b] = got[q, at : at + 4 * ra]
-            edge = near[q, end_coarse + 6 * s : end_coarse + 6 * s + 6]
-            for x in range(4):
-                at = s * 4 * rows_a + x * rows_a
-                grad_mid[s, x, 2 * q * ra : 2 * q * ra + rows_a] += near[q, at : at + rows_a]
-                row = 2 * la if low else 1
-                grad_mid[s, x, row : row + 1] += edge[x : x + 1]
-            at = end_mid + (ra + 4) * s
-            grad_coarse[s, q * ra : q * ra + ra + 4] += near[q, at : at + ra + 4]
-            row = la if low else 2
-            grad_coarse[s, row : row + 2] += edge[4:6]
+                    resid_out[s, star, rows, part * b : (part + 1) * b] = shown[q, at : at + 4 * ra]
     for i in range(2):
         for j in range(8):
             rows = [begins["fine"] + 64 * i + 8 * c + j for c in range(8)]
@@ -586,6 +576,31 @@
                         term = weight[c] * fine[half, at : at + 2 * la]
                         total = term if total is None else total + term
                     fine_out[s, j, i, :, half * b : (half + 1) * b] = total
+
+
+def small_owner_kernel(g, mid_mix, *rest):
+    in_refs, (coarse_out, mid_out, near, grad_mid, grad_coarse) = rest[: g.n], rest[g.n :]
+    me = lax.axis_index("rad")
+    n, s_count, ra, la = g.n, g.s, g.ra, g.la
+    rows_a = 2 * ra + 2
+    end_mid, end_coarse, _ = small_back(g)
+    for k in range(n):
+        near[lax.rem(me + n - k, n)] = in_refs[k][...]
+    grad_mid[...] = jnp.zeros(grad_mid.shape, F32)
+    grad_coarse[...] = jnp.zeros(grad_coarse.shape, F32)
+    for q in range(g.w):
+        low = q < g.w // 2
+        for s in range(s_count):
+            edge = near[q, end_coarse + 6 * s : end_coarse + 6 * s + 6]
+            for x in range(4):
+                at = s * 4 * rows_a + x * rows_a
+                grad_mid[s, x, 2 * q * ra : 2 * q * ra + rows_a] += near[q, at : at + rows_a]
+                row = 2 * la if low else 1
+                grad_mid[s, x, row : row + 1] += edge[x : x + 1]
+            at = end_mid + (ra + 4) * s
+            grad_coarse[s, q * ra : q * ra + ra + 4] += near[q, at : at + ra + 4]
+            row = la if low else 2
+            grad_coarse[s, row : row + 2] += edge[4:6]
     for s in range(s_count):
         coarse_out[s, 0] = grad_coarse[s, 2 : 2 + la]
         cells = []
@@ -593,11 +608,14 @@
             cr, ca, cb = c // 4, c // 2 % 2, c % 2
             cells.append(grad_mid[s, 2 * cr + cb, pl.ds(1 + ca, la, stride=2), :])
         for j in range(8):
-            row = begins["mid"] + j
-            total = block[row : row + 1] * cells[0]
+            total = mid_mix[j : j + 1] * cells[0]
             for c in range(1, 8):
-                total = total + block[row + 8 * c : row + 8 * c + 1] * cells[c]
+                total = total + mid_mix[j + 8 * c : j + 8 * c + 1] * cells[c]
             mid_out[s, j, 0] = total
+
+
+def held(arrays):
+    return [(pltpu.SMEM if len(x.shape) == 1 else pltpu.VMEM)(x.shape, x.dtype) for x in arrays]
 
 
 def call(kernel, name, outs, operands, scratch, unmoved=0, written=0):
@@ -633,74 +651,72 @@
     n, m, s, la, b, stars, w, ra, h = g
     kernel = functools.partial
     rows_a = 2 * ra + 2
-    pairs = [(i, i ^ 1) for i in range(m)]
-    between = [(i, (i + 1) % m if i % 2 else (i - 1) % m) for i in range(m)]
     workers = [(r, a, 1 if min(r, w - 1) < w // 2 else -1) for r in range(n) for a in range(m)]
     sideways = [(r * m + a, r * m + (a - step) % m) for r, a, step in workers]
+    inward = [(to, at) for at, to in sideways]
 
     def exchange(blocks):
         return [blocks[0]] + [lax.ppermute(blocks[k], "rad", [(i, (i + k) % n) for i in range(n)]) for k in range(1, n)]
 
     noise_mid, noise_fine = noise_mid.transpose(1, 2, 0), noise_fine.transpose(1, 2, 0)
-    edge_rows = (eights(6 * s), b)
-    large, small = (large_there(g)[-1], b), (small_there(g)[-1], b)
+    large = (large_there(g)[-1], b)
+    operands = (emission, rows_mid, noise_mid, coarse_field, excite_mid, rows_fine, noise_fine, excite_fine)
     sent = call(
         kernel(scatter_kernel, g),
         "scatter",
         [(large, F32)] * n,
-        (rows_fine, noise_fine, excite_fine, emission),
+        operands,
         [
-            pltpu.SMEM(rows_fine.shape, jnp.int32),
-            noise_fine.shape,
-            excite_fine.shape,
-            emission.shape,
-            pltpu.SemaphoreType.DMA((4,)),
+            *held(operands),
+            pltpu.SemaphoreType.DMA((8,)),
             pltpu.SemaphoreType.DMA((n,)),
             (32 * s * la, 2 * b),
             (2, 32 * s * la, b),
             (4, 16 * la, b),
             (w, *large),
+            (s, 8, la, b),
+            (s, la + 4, b),
         ],
-        unmoved=4,
+        unmoved=8,
         written=n,
     )
     got = exchange(sent)
-    operands = (rows_mid, rows_fine, noise_mid, noise_fine, kernels_mid, kernels_fine)
-    operands += (coarse_field, excite_mid, star_bins, star_data)
-    one, two, block = call(
+    operands = (rows_mid, rows_fine, noise_mid, noise_fine, kernels_mid, kernels_fine, star_bins, star_data)
+    (block,) = call(
         kernel(prepare_kernel, g),
         "prepare",
-        [(edge_rows, F32), (edge_rows, F32), ((prepared_rows(g)[1], b), F32)],
+        [((prepared_rows(g)[1], b), F32)],
         (*operands, sent[0]),
-        [
-            *[(pltpu.SMEM if len(x.shape) == 1 else pltpu.VMEM)(x.shape, x.dtype) for x in operands],
-            pltpu.SemaphoreType.DMA((10,)),
-            (2, 4 * stars * ra, 4 * b),
-        ],
-        unmoved=11,
-    )
-    one, two = lax.ppermute(one, "ang", pairs), lax.ppermute(two, "ang", between)
-    got += exchange(
-        call(
-            kernel(halo_kernel, g),
-            "halos",
-            [(small, F32)] * n,
-            (block, one, two),
-            [(s, la + 4, b), (w, *small)],
-        )
-    )
-    (spread,) = call(kernel(weight_kernel, g), "weights", [((24 * 27, h, b), F32)], (block,), [])
-    large_out = (large_back(g)[-1], b)
-    *done, parent, coarse_sum, edge = call(
+        [*held(operands), pltpu.SemaphoreType.DMA((8,)), (2, 4 * stars * ra, 4 * b)],
+        unmoved=9,
+    )
+    spread, got[0], block = call(
+        kernel(weight_kernel, g),
+        "weights",
+        [((24 * 27, h, b), F32), (large, F32), (block.shape, F32)],
+        (block, sent[0]),
+        [],
+    )
+    (near,) = call(kernel(relay_kernel, g), "relay", [((6 * h, b), F32)], got, [])
+    near = lax.ppermute(near, ("rad", "ang"), inward)
+    parts = [(64 * ra * h, b), (64 * ra * h, b), (4 * rows_a * h, b), ((ra + 4) * h, b)]
+    unpacked = call(kernel(unpack_kernel, g), "unpack", [(part, F32) for part in parts], got, [])
+    def everywhere(block):
+        held, bit = {0: block}, n // 2
+        while bit:
+            swap = [(i, i ^ bit) for i in range(n)]
+            held |= {i ^ bit: lax.ppermute(x, "rad", swap) for i, x in held.items()}
+            bit //= 2
+        return [held[i] for i in range(n)]
+
+    field_out, resid_out = [(rows, b) for rows in large_back(g)]
+    *done, shown, parent, coarse_sum, edge = call(
         kernel(main_kernel, g),
         "main",
-        [(large_out, F32)] * n + [((4 * rows_a * h, b), F32), (((ra + 4) * h, b), F32), ((6 * h, b), F32)],
-        (block, spread, *got),
+        [(field_out, F32)] * n
+        + [(shape, F32) for shape in (resid_out, (4 * rows_a * h, b), ((ra + 4) * h, b), (6 * h, b))],
+        (block, spread, *unpacked, near),
         [
-            (n, *large),
-            (n, *small),
-            (64 * ra * h, b),
-            (64 * ra * h, b),
             (4 * rows_a * h, b),
             ((ra + 4) * h, b),
             (3, ra + 4, 3, h, b),
@@ -709,13 +725,14 @@
             (2, 32 * ra * h, b),
             (4, 4 * stars * ra * s, b),
             (2, 32 * ra * h, b),
-            (n, *large_out),
+            (n, *field_out),
         ],
     )
-    large, small = (large_back(g)[-1], b), (small_back(g)[-1], b)
+    small = (small_back(g)[-1], b)
+    shown = everywhere(shown)
     got = exchange(done)
     edge = lax.ppermute(edge, ("rad", "ang"), sideways)
-    got += exchange(
+    near = exchange(
         call(
             kernel(sums_kernel, g),
             "sums",
@@ -724,20 +741,21 @@
             [(n, *small)],
         )
     )
-    return tuple(
-        call(
-            kernel(owner_kernel, g),
-            "owner",
-            [
-                ((s, 1, la, b), F32),
-                ((s, 8, 1, la, b), F32),
-                ((s, 8, 2, 2 * la, 2 * b), F32),
-                ((s, stars, 4 * la, 4 * b), F32),
-            ],
-            (block, *got),
-            [(n, *large), (n, *small), (2, 32 * s * la, b), (s, 4, 2 * la + 2, b), (s, la + 4, b)],
-        )
-    )
+    grad_fine, residual, mid_mix = call(
+        kernel(large_owner_kernel, g),
+        "large_owner",
+        [((s, 8, 2, 2 * la, 2 * b), F32), ((s, stars, 4 * la, 4 * b), F32), ((64, b), F32)],
+        (block, *got, *shown),
+        [(n, *field_out), (n, *resid_out), (2, 32 * s * la, b)],
+    )
+    grad_coarse, grad_mid = call(
+        kernel(small_owner_kernel, g),
+        "small_owner",
+        [((s, 1, la, b), F32), ((s, 8, 1, la, b), F32)],
+        (mid_mix, *near),
+        [(n, *small), (s, 4, 2 * la + 2, b), (s, la + 4, b)],
+    )
+    return grad_coarse, grad_mid, grad_fine, residual
 
 
 def solution(mesh):

time: 48.6 us -> 44.6 us (0.918)
  waiting for transfers between devices: 13.4 us -> 7.93 us
  local copies, waits for them, and re-layouts: 0.97 us -> 1.85 us
    ppermute x12 -> x9, waiting for transfers between devices: 10.2 us -> 2.38 us  [exchange(): lax.ppermute(blocks[k], 'rad', [(i, (i + k) % n) for i in range(n)])]
    ppermute x2 -> x4, waiting for transfers between devices: 1.7 us -> 4.03 us  [the longest x1 4.03 us: per_device(): near = lax.ppermute(near, ('rad', 'ang'), inward)]
    ppermute x12 -> x9, starting transfers between devices: 19.3 us -> 17.3 us  [exchange(): lax.ppermute(blocks[k], 'rad', [(i, (i + k) % n) for i in range(n)])]
    ppermute x1, starting transfers between devices: 0.01 us -> 1.25 us  [per_device(): edge = lax.ppermute(edge, ('rad', 'ang'), sideways)]
    ppermute x2 -> x4, starting transfers between devices: 2.62 us -> 3.8 us  [the longest x3 3.75 us: everywhere(): held |= {i ^ bit: lax.ppermute(x, 'rad', swap) for i, x in held.items()}]
    unnamed x6 -> x4, local copies, waits for them, and re-layouts: 0.97 us -> 1.85 us
    pallas_call x7 -> x9, Pallas kernels: 11.4 us -> 11.5 us  [call(): pl.pallas_call(kernel, name=name, out_shape=[jax.ShapeDtypeStruct(shape,...]
  transfers between devices with their start and end apart: 15 -> 14, of which waited for: 7 -> 4; matrix products, arithmetic and copies ran while one was open for 0% -> 0% of each run, Pallas kernels for 8% -> 11%
where the time goes in v3:
time: 44.6 us; the launch traced here: 44.4 us
  starting transfers between devices  22.3 us (50%)
  Pallas kernels  11.5 us (26%)
  waiting for transfers between devices  7.93 us (18%)
  local copies, waits for them, and re-layouts  1.85 us (4%)
  between operations  0.71 us (2%)
    ppermute x9, starting transfers between devices, exchange(): lax.ppermute(blocks[k], 'rad', [(i, (i + k) % n) for i in range(n)])  17.3 us
    pallas_call x9, Pallas kernels, call(): pl.pallas_call(kernel, name=name, out_shape=[jax.ShapeDtypeStruct(shape,...  11.5 us
    ppermute x1, waiting for transfers between devices, per_device(): near = lax.ppermute(near, ('rad', 'ang'), inward)  4.03 us
    ppermute x3, starting transfers between devices, everywhere(): held |= {i ^ bit: lax.ppermute(x, 'rad', swap) for i, x in held.items()}  3.75 us
    ppermute x9, waiting for transfers between devices, exchange(): lax.ppermute(blocks[k], 'rad', [(i, (i + k) % n) for i in range(n)])  2.38 us
    unnamed x4, local copies, waits for them, and re-layouts  1.85 us
    ppermute x1, waiting for transfers between devices, per_device(): edge = lax.ppermute(edge, ('rad', 'ang'), sideways)  1.52 us
    ppermute x1, starting transfers between devices, per_device(): edge = lax.ppermute(edge, ('rad', 'ang'), sideways)  1.25 us
  transfers between devices with their start and end apart: 14, of which 4 were waited for; matrix products, arithmetic and copies ran while one was open for 0% of the time, Pallas kernels for 11%

profile of v3, /device:TPU:0, one launch (start us, length us, event | category | flops | bytes accessed | tf_op | source)
XLA Modules:
  0.0 44.4 jit_solution(11159692294249919472)
XLA Ops:
  0.6 3.0 %scatter.1 = (f32[248,128]{1,0:T(8,128)}, f32[248,128]{1,0:T(8,128)}, f32[248,128]{1,0:T(8,128)}, f32[248,128]{1,0:T(8,128)}) custom-call(f32[4,16,512]{2,1,0:T(8,128)} %rest_0_.2, s32[4]{0:T(128)} %rest_0_.3, f32[8,8,16]{2,1,0:T(8,128)} %bitcast.2, f32[2,1,4,128]{3,2,1,0:T(4,128)} %rest_3_.1, f32[2,8,1,4,128]{4,3,2,1,0:T(4,128)} %rest_4_.2, s32[8]{0:T(128)} %rest_1_.3, ...), custom_call_target="tpu_custom_call" | custom-call | tf_op jit(solution)/shard_map/scatter/pallas_call | solution.py:625
  3.6 3.1 %collective-permute-start = (f32[248,128]{1,0:T(8,128)}, f32[248,128]{1,0:T(8,128)S(1)}, u32[]{:S(2)}, u32[]{:S(2)}) collective-permute-start(f32[248,128]{1,0:T(8,128)} %get-tuple-element.36), channel_id=1, source_target_pairs={{0,8},{8,16},{16,24},{24,0},{1,9},{9,17},{17,25},{25,1},{2,10},{10... | collective-permute-start | bytes 380936 | tf_op jit(solution)/shard_map/ppermute | solution.py:659
  6.7 2.6 %collective-permute-start.1 = (f32[248,128]{1,0:T(8,128)}, f32[248,128]{1,0:T(8,128)S(1)}, u32[]{:S(2)}, u32[]{:S(2)}) collective-permute-start(f32[248,128]{1,0:T(8,128)} %get-tuple-element.37), channel_id=1, source_target_pairs={{0,16},{8,24},{16,0},{24,8},{1,17},{9,25},{17,1},{25,9},{2,18},{10... | collective-permute-start | bytes 380936 | tf_op jit(solution)/shard_map/ppermute | solution.py:659
  9.3 1.3 %collective-permute-start.2 = (f32[248,128]{1,0:T(8,128)}, f32[248,128]{1,0:T(8,128)S(1)}, u32[]{:S(2)}, u32[]{:S(2)}) collective-permute-start(f32[248,128]{1,0:T(8,128)} %get-tuple-element.38), channel_id=1, source_target_pairs={{0,24},{8,0},{16,8},{24,16},{1,25},{9,1},{17,9},{25,17},{2,26},{10... | collective-permute-start | bytes 380936 | tf_op jit(solution)/shard_map/ppermute | solution.py:659
  10.6 2.4 %prepare.1.block = f32[512,128]{1,0:T(8,128)} custom-call(s32[4]{0:T(128)} %rest_0_.3, s32[8]{0:T(128)} %rest_1_.3, f32[8,8,16]{2,1,0:T(8,128)} %bitcast.3, f32[8,8,16]{2,1,0:T(8,128)} %bitcast.5, f32[16,8,27]{2,1,0:T(8,128)} %rest_4_.3, f32[16,8,27]{2,1,0:T(8,128)} %rest_5_.3, s32[4,16,512]{2,1,0:T(8,128)} %rest_6_.1, f32[4,16,512]{2,1,0:T(8,128)} %rest_7_.3, ...), custom_call_target="tpu_custom_call" | custom-call | tf_op jit(solution)/shard_map/prepare/pallas_call | solution.py:625
  13.0 0.0 copy-start
  13.0 0.9 %copy-done = f32[512,128]{1,0:T(8,128)S(1)} copy-done((f32[512,128]{1,0:T(8,128)S(1)}, f32[512,128]{1,0:T(8,128)}, u32[]{:S(2)}) %copy-start) | copy-done | bytes 262168
  14.0 0.9 %copy-done.1 = f32[248,128]{1,0:T(8,128)S(1)} copy-done((f32[248,128]{1,0:T(8,128)S(1)}, f32[248,128]{1,0:T(8,128)}, u32[]{:S(2)}) %copy-start.1) | copy-done | bytes 127000
  14.9 1.2 %weights.1 = (f32[648,8,128]{2,1,0:T(8,128)S(1)}, f32[248,128]{1,0:T(8,128)S(1)}, f32[512,128]{1,0:T(8,128)S(1)}) custom-call(f32[512,128]{1,0:T(8,128)S(1)} %copy-done, f32[248,128]{1,0:T(8,128)S(1)} %copy-done.1), custom_call_target="tpu_custom_call" | custom-call | tf_op jit(solution)/shard_map/weights/pallas_call | solution.py:625
  16.1 0.0 collective-permute-done.rest_1_
  16.1 1.8 %collective-permute-done.1.rest_2_ = f32[248,128]{1,0:T(8,128)S(1)} collective-permute-done((f32[248,128]{1,0:T(8,128)}, f32[248,128]{1,0:T(8,128)S(1)}, u32[]{:S(2)}, u32[]{:S(2)}) %collective-permute-start.1) | collective-permute-done | bytes 127008 | tf_op jit(solution)/shard_map/ppermute | solution.py:659
  17.9 0.0 collective-permute-done.2.rest_3_
  17.9 0.1 collective-permute-start.3
  17.9 0.1 unpack.1
  18.0 4.0 %collective-permute-done.3.rest_4_ = f32[48,128]{1,0:T(8,128)S(1)} collective-permute-done((f32[48,128]{1,0:T(8,128)S(1)}, f32[48,128]{1,0:T(8,128)S(1)}, u32[]{:S(2)}, u32[]{:S(2)}) %collective-permute-start.3) | collective-permute-done | bytes 24608 | tf_op jit(solution)/shard_map/ppermute | solution.py:701
  22.1 3.1 %main.1 = (f32[128,128]{1,0:T(8,128)S(1)}, f32[128,128]{1,0:T(8,128)S(1)}, f32[128,128]{1,0:T(8,128)S(1)}, f32[128,128]{1,0:T(8,128)S(1)}, f32[128,128]{1,0:T(8,...) custom-call(f32[512,128]{1,0:T(8,128)S(1)} %get-tuple-element.33.block, ...), custom_call_target="tpu_custom_call" | custom-call | tf_op jit(solution)/shard_map/main/pallas_call | solution.py:625
  25.2 1.7 %collective-permute-start.8 = (f32[128,128]{1,0:T(8,128)S(1)}, f32[128,128]{1,0:T(8,128)S(1)}, u32[]{:S(2)}, u32[]{:S(2)}) collective-permute-start(f32[128,128]{1,0:T(8,128)S(1)} %get-tuple-element.47.rest_4_), channel_id=1, source_target_pairs={{0,16},{8,24},{16,0},{24,8},{1,17},{9,25},{17,1},{25,9},{2,18},{10... | collective-permute-start | bytes 196616 | tf_op jit(solution)/shard_map/ppermute | solution.py:708
  26.9 1.6 %collective-permute-start.4 = (f32[128,128]{1,0:T(8,128)S(1)}, f32[128,128]{1,0:T(8,128)S(1)}, u32[]{:S(2)}, u32[]{:S(2)}) collective-permute-start(f32[128,128]{1,0:T(8,128)S(1)} %get-tuple-element.44), channel_id=1, source_target_pairs={{0,8},{8,16},{16,24},{24,0},{1,9},{9,17},{17,25},{25,1},{2,10},{10... | collective-permute-start | bytes 196616 | tf_op jit(solution)/shard_map/ppermute | solution.py:659
  28.5 2.9 %collective-permute-start.5 = (f32[128,128]{1,0:T(8,128)S(1)}, f32[128,128]{1,0:T(8,128)S(1)}, u32[]{:S(2)}, u32[]{:S(2)}) collective-permute-start(f32[128,128]{1,0:T(8,128)S(1)} %get-tuple-element.45), channel_id=1, source_target_pairs={{0,16},{8,24},{16,0},{24,8},{1,17},{9,25},{17,1},{25,9},{2,18},{10... | collective-permute-start | bytes 196616 | tf_op jit(solution)/shard_map/ppermute | solution.py:659
  31.4 1.3 %collective-permute-start.10 = (f32[48,128]{1,0:T(8,128)S(1)}, f32[48,128]{1,0:T(8,128)S(1)}, u32[]{:S(2)}, u32[]{:S(2)}) collective-permute-start(f32[48,128]{1,0:T(8,128)S(1)} %get-tuple-element.51), channel_id=1, source_target_pairs={{0,7},{1,0},{2,1},{3,2},{4,3},{5,4},{6,5},{7,6},{8,15},{9,8},{10,9... | collective-permute-start | bytes 73736 | tf_op jit(solution)/shard_map/ppermute | solution.py:734
  32.6 1.5 %collective-permute-done.10.edge_ref = f32[48,128]{1,0:T(8,128)S(1)} collective-permute-done((f32[48,128]{1,0:T(8,128)S(1)}, f32[48,128]{1,0:T(8,128)S(1)}, u32[]{:S(2)}, u32[]{:S(2)}) %collective-permute-start.10) | collective-permute-done | bytes 24608 | tf_op jit(solution)/shard_map/ppermute | solution.py:734
  34.2 0.8 %collective-permute-start.7 = (f32[128,128]{1,0:T(8,128)S(1)}, f32[128,128]{1,0:T(8,128)S(1)}, u32[]{:S(2)}, u32[]{:S(2)}) collective-permute-start(f32[128,128]{1,0:T(8,128)S(1)} %get-tuple-element.47.rest_4_), channel_id=1, source_target_pairs={{0,8},{8,0},{16,24},{24,16},{1,9},{9,1},{17,25},{25,17},{2,10},{10... | collective-permute-start | bytes 196616 | tf_op jit(solution)/shard_map/ppermute | solution.py:708
  34.9 0.0 collective-permute-done.8.rest_6_
  34.9 1.3 %collective-permute-start.9 = (f32[128,128]{1,0:T(8,128)S(1)}, f32[128,128]{1,0:T(8,128)S(1)}, u32[]{:S(2)}, u32[]{:S(2)}) collective-permute-start(f32[128,128]{1,0:T(8,128)S(1)} %collective-permute-done.8.rest_6_), channel_id=1, source_target_pairs={{0,8},{8,0},{16,24},{24,16},{1,9},{9,1},{17,25},{25,17},{2,10},{10... | collective-permute-start | bytes 196616 | tf_op jit(solution)/shard_map/ppermute | solution.py:708
  36.2 0.0 collective-permute-done.4.rest_1_
  36.2 0.8 %collective-permute-start.11 = (f32[56,128]{1,0:T(8,128)S(1)}, f32[56,128]{1,0:T(8,128)S(1)}, u32[]{:S(2)}, u32[]{:S(2)}) collective-permute-start(f32[56,128]{1,0:T(8,128)S(1)} %get-tuple-element.53), channel_id=1, source_target_pairs={{0,8},{8,16},{16,24},{24,0},{1,9},{9,17},{17,25},{25,1},{2,10},{10... | collective-permute-start | bytes 86024 | tf_op jit(solution)/shard_map/ppermute | solution.py:659
  37.1 0.0 collective-permute-done.5.rest_2_
  37.1 2.7 %collective-permute-start.12 = (f32[56,128]{1,0:T(8,128)S(1)}, f32[56,128]{1,0:T(8,128)S(1)}, u32[]{:S(2)}, u32[]{:S(2)}) collective-permute-start(f32[56,128]{1,0:T(8,128)S(1)} %get-tuple-element.54), channel_id=1, source_target_pairs={{0,16},{8,24},{16,0},{24,8},{1,17},{9,25},{17,1},{25,9},{2,18},{10... | collective-permute-start | bytes 86024 | tf_op jit(solution)/shard_map/ppermute | solution.py:659
  39.8 2.3 %collective-permute-start.13 = (f32[56,128]{1,0:T(8,128)S(1)}, f32[56,128]{1,0:T(8,128)S(1)}, u32[]{:S(2)}, u32[]{:S(2)}) collective-permute-start(f32[56,128]{1,0:T(8,128)S(1)} %get-tuple-element.55), channel_id=1, source_target_pairs={{0,24},{8,0},{16,8},{24,16},{1,25},{9,1},{17,9},{25,17},{2,26},{10... | collective-permute-start | bytes 86024 | tf_op jit(solution)/shard_map/ppermute | solution.py:659
  42.1 1.0 %large_owner.1 = (f32[2,8,2,8,256]{4,3,2,1,0:T(8,128)}, f32[2,4,16,512]{3,2,1,0:T(8,128)}, f32[64,128]{1,0:T(8,128)S(1)}) custom-call(f32[512,128]{1,0:T(8,128)S(1)} %get-tuple-element.33.block, f32[128,128]{1,0:T(8,128)S(1)} %get-tuple-element.43.rest_0_, f32[128,128]{1,0:T(8,128)S(1)} %collective-permute-done.4.rest_1_, ...), custom_call_target="tpu_custom_call" | custom-call | tf_op jit(solution)/shard_map/large_owner/pallas_call | solution.py:625
  43.1 0.6 %collective-permute-done.13.rest_3_ = f32[56,128]{1,0:T(8,128)S(1)} collective-permute-done((f32[56,128]{1,0:T(8,128)S(1)}, f32[56,128]{1,0:T(8,128)S(1)}, u32[]{:S(2)}, u32[]{:S(2)}) %collective-permute-start.13) | collective-permute-done | bytes 28704 | tf_op jit(solution)/shard_map/ppermute | solution.py:659
  43.6 0.7 %small_owner.1 = (f32[2,1,4,128]{3,2,1,0:T(4,128)}, f32[2,8,1,4,128]{4,3,2,1,0:T(4,128)}) custom-call(f32[64,128]{1,0:T(8,128)S(1)} %get-tuple-element.48.mid_mix, f32[56,128]{1,0:T(8,128)S(1)} %get-tuple-element.52.rest_0_, f32[56,128]{1,0:T(8,128)S(1)} %collective-permute-done.11.rest_1_, f32[56,128]{1,0:T(8,128)S(1)} %collective-permute-done.12.rest_2_, ...), custom_call_target="tpu_custom_call" | custom-call | tf_op jit(solution)/shard_map/small_owner/pallas_call | solution.py:625
  (9 shorter events, 0.1 us)
Async XLA Ops:
  3.6 12.5 %collective-permute-start = (f32[248,128]{1,0:T(8,128)}, f32[248,128]{1,0:T(8,128)S(1)}, u32[]{:S(2)}, u32[]{:S(2)}) collective-permute-start(f32[248,128]{1,0:T(8,128)} %get-tuple-element.36), channel_id=1, source_target_pairs={{0,8},{8,16},{16,24},{24,0},{1,9},{9,17},{17,25},{25,1},{2,10},{10... | collective-permute-start | bytes 380936 | tf_op jit(solution)/shard_map/ppermute | solution.py:659
  6.7 11.2 %collective-permute-start.1 = (f32[248,128]{1,0:T(8,128)}, f32[248,128]{1,0:T(8,128)S(1)}, u32[]{:S(2)}, u32[]{:S(2)}) collective-permute-start(f32[248,128]{1,0:T(8,128)} %get-tuple-element.37), channel_id=1, source_target_pairs={{0,16},{8,24},{16,0},{24,8},{1,17},{9,25},{17,1},{25,9},{2,18},{10... | collective-permute-start | bytes 380936 | tf_op jit(solution)/shard_map/ppermute | solution.py:659
  9.3 8.6 %collective-permute-start.2 = (f32[248,128]{1,0:T(8,128)}, f32[248,128]{1,0:T(8,128)S(1)}, u32[]{:S(2)}, u32[]{:S(2)}) collective-permute-start(f32[248,128]{1,0:T(8,128)} %get-tuple-element.38), channel_id=1, source_target_pairs={{0,24},{8,0},{16,8},{24,16},{1,25},{9,1},{17,9},{25,17},{2,26},{10... | collective-permute-start | bytes 380936 | tf_op jit(solution)/shard_map/ppermute | solution.py:659
  13.0 1.0 %copy-start = (f32[512,128]{1,0:T(8,128)S(1)}, f32[512,128]{1,0:T(8,128)}, u32[]{:S(2)}) copy-start(f32[512,128]{1,0:T(8,128)} %prepare.1.block) | copy-start | bytes 786436
  14.0 0.9 %copy-start.1 = (f32[248,128]{1,0:T(8,128)S(1)}, f32[248,128]{1,0:T(8,128)}, u32[]{:S(2)}) copy-start(f32[248,128]{1,0:T(8,128)} %get-tuple-element.32.rest_8_.own) | copy-start | bytes 380932
  17.9 4.2 %collective-permute-start.3 = (f32[48,128]{1,0:T(8,128)S(1)}, f32[48,128]{1,0:T(8,128)S(1)}, u32[]{:S(2)}, u32[]{:S(2)}) collective-permute-start(f32[48,128]{1,0:T(8,128)S(1)} %relay.1), channel_id=1, source_target_pairs={{7,0},{0,1},{1,2},{2,3},{3,4},{4,5},{5,6},{6,7},{15,8},{8,9},{9,10... | collective-permute-start | bytes 73736 | tf_op jit(solution)/shard_map/ppermute | solution.py:701
  25.2 9.7 %collective-permute-start.8 = (f32[128,128]{1,0:T(8,128)S(1)}, f32[128,128]{1,0:T(8,128)S(1)}, u32[]{:S(2)}, u32[]{:S(2)}) collective-permute-start(f32[128,128]{1,0:T(8,128)S(1)} %get-tuple-element.47.rest_4_), channel_id=1, source_target_pairs={{0,16},{8,24},{16,0},{24,8},{1,17},{9,25},{17,1},{25,9},{2,18},{10... | collective-permute-start | bytes 196616 | tf_op jit(solution)/shard_map/ppermute | solution.py:708
  26.9 9.3 %collective-permute-start.4 = (f32[128,128]{1,0:T(8,128)S(1)}, f32[128,128]{1,0:T(8,128)S(1)}, u32[]{:S(2)}, u32[]{:S(2)}) collective-permute-start(f32[128,128]{1,0:T(8,128)S(1)} %get-tuple-element.44), channel_id=1, source_target_pairs={{0,8},{8,16},{16,24},{24,0},{1,9},{9,17},{17,25},{25,1},{2,10},{10... | collective-permute-start | bytes 196616 | tf_op jit(solution)/shard_map/ppermute | solution.py:659
  28.5 8.5 %collective-permute-start.5 = (f32[128,128]{1,0:T(8,128)S(1)}, f32[128,128]{1,0:T(8,128)S(1)}, u32[]{:S(2)}, u32[]{:S(2)}) collective-permute-start(f32[128,128]{1,0:T(8,128)S(1)} %get-tuple-element.45), channel_id=1, source_target_pairs={{0,16},{8,24},{16,0},{24,8},{1,17},{9,25},{17,1},{25,9},{2,18},{10... | collective-permute-start | bytes 196616 | tf_op jit(solution)/shard_map/ppermute | solution.py:659
  31.4 8.4 %collective-permute-start.6 = (f32[128,128]{1,0:T(8,128)S(1)}, f32[128,128]{1,0:T(8,128)S(1)}, u32[]{:S(2)}, u32[]{:S(2)}) collective-permute-start(f32[128,128]{1,0:T(8,128)S(1)} %get-tuple-element.46), channel_id=1, source_target_pairs={{0,24},{8,0},{16,8},{24,16},{1,25},{9,1},{17,9},{25,17},{2,26},{10... | collective-permute-start | bytes 196616 | tf_op jit(solution)/shard_map/ppermute | solution.py:659
  31.4 2.8 %collective-permute-start.10 = (f32[48,128]{1,0:T(8,128)S(1)}, f32[48,128]{1,0:T(8,128)S(1)}, u32[]{:S(2)}, u32[]{:S(2)}) collective-permute-start(f32[48,128]{1,0:T(8,128)S(1)} %get-tuple-element.51), channel_id=1, source_target_pairs={{0,7},{1,0},{2,1},{3,2},{4,3},{5,4},{6,5},{7,6},{8,15},{9,8},{10,9... | collective-permute-start | bytes 73736 | tf_op jit(solution)/shard_map/ppermute | solution.py:734
  34.2 7.9 %collective-permute-start.7 = (f32[128,128]{1,0:T(8,128)S(1)}, f32[128,128]{1,0:T(8,128)S(1)}, u32[]{:S(2)}, u32[]{:S(2)}) collective-permute-start(f32[128,128]{1,0:T(8,128)S(1)} %get-tuple-element.47.rest_4_), channel_id=1, source_target_pairs={{0,8},{8,0},{16,24},{24,16},{1,9},{9,1},{17,25},{25,17},{2,10},{10... | collective-permute-start | bytes 196616 | tf_op jit(solution)/shard_map/ppermute | solution.py:708
  34.9 7.1 %collective-permute-start.9 = (f32[128,128]{1,0:T(8,128)S(1)}, f32[128,128]{1,0:T(8,128)S(1)}, u32[]{:S(2)}, u32[]{:S(2)}) collective-permute-start(f32[128,128]{1,0:T(8,128)S(1)} %collective-permute-done.8.rest_6_), channel_id=1, source_target_pairs={{0,8},{8,0},{16,24},{24,16},{1,9},{9,1},{17,25},{25,17},{2,10},{10... | collective-permute-start | bytes 196616 | tf_op jit(solution)/shard_map/ppermute | solution.py:708
  36.2 6.8 %collective-permute-start.11 = (f32[56,128]{1,0:T(8,128)S(1)}, f32[56,128]{1,0:T(8,128)S(1)}, u32[]{:S(2)}, u32[]{:S(2)}) collective-permute-start(f32[56,128]{1,0:T(8,128)S(1)} %get-tuple-element.53), channel_id=1, source_target_pairs={{0,8},{8,16},{16,24},{24,0},{1,9},{9,17},{17,25},{25,1},{2,10},{10... | collective-permute-start | bytes 86024 | tf_op jit(solution)/shard_map/ppermute | solution.py:659
  37.1 6.0 %collective-permute-start.12 = (f32[56,128]{1,0:T(8,128)S(1)}, f32[56,128]{1,0:T(8,128)S(1)}, u32[]{:S(2)}, u32[]{:S(2)}) collective-permute-start(f32[56,128]{1,0:T(8,128)S(1)} %get-tuple-element.54), channel_id=1, source_target_pairs={{0,16},{8,24},{16,0},{24,8},{1,17},{9,25},{17,1},{25,9},{2,18},{10... | collective-permute-start | bytes 86024 | tf_op jit(solution)/shard_map/ppermute | solution.py:659
  39.8 3.9 %collective-permute-start.13 = (f32[56,128]{1,0:T(8,128)S(1)}, f32[56,128]{1,0:T(8,128)S(1)}, u32[]{:S(2)}, u32[]{:S(2)}) collective-permute-start(f32[56,128]{1,0:T(8,128)S(1)} %get-tuple-element.55), channel_id=1, source_target_pairs={{0,24},{8,0},{16,8},{24,16},{1,25},{9,1},{17,9},{25,17},{2,26},{10... | collective-permute-start | bytes 86024 | tf_op jit(solution)/shard_map/ppermute | solution.py:659

commit v4 on v3

--- a/solution.py
+++ b/solution.py
@@ -46,14 +46,11 @@
     return fine, emit, mix, coarse, eights(coarse + 6 * g.s)
 
 
-def large_back(g):
-    return 2 * 2 * g.ra * g.s * 16, 4 * g.s * 4 * g.stars * g.ra
-
-
-def small_back(g):
-    mid = g.s * 4 * (2 * g.ra + 2)
+def rows_back(g):
+    field = 2 * 2 * g.ra * g.s * 16
+    mid = field + g.s * 4 * (2 * g.ra + 2)
     coarse = mid + g.s * (g.ra + 4)
-    return mid, coarse, eights(coarse + 6 * g.s)
+    return field, mid, coarse, eights(coarse + 6 * g.s)
 
 
 def prepared_rows(g):
@@ -291,11 +288,21 @@
             spread[x * 27 + o] = jnp.broadcast_to(tile[:, o : o + 1], (g.h, g.b))
 
 
-def main_kernel(g, block, spread, *rest):
+def edges_inside(g, worker):
+    first = lax.axis_index("ang") * g.la + worker * g.ra
+    inside = jnp.where(first > 0, 1.0, 0.0), jnp.where(first + g.ra < g.m * g.la, 1.0, 0.0)
+    return [x.astype(F32) for x in inside]
+
+
+def cell_rows_of(g, a, c, pr):
+    return pl.ds(pl.multiple_of(((a * 8 + c) * 2 + pr) * g.h, 8), g.h)
+
+
+def forward_kernel(g, block, spread, *rest):
     n, b, s_count, ra, h = g.n, g.b, g.s, g.ra, g.h
     fine_in, emit_in, mixed, coarse, near = rest[:5]
-    out_refs, (resid_out, parent, coarse_sum, edge_sum), rest = rest[5 : 5 + n], rest[5 + n : 9 + n], rest[9 + n :]
-    mix_in, coarse_in, coarse_ext, mid_ext, tall, cells, seen, joined, stage = rest
+    cells, resid_out = rest[5:7]
+    mix_in, coarse_in, coarse_ext, mid_ext, seen = rest[7:]
     me, ang = lax.axis_index("rad"), lax.axis_index("ang")
     rows_a = 2 * ra + 2
     spacing = 1.0 / (4 * n)
@@ -321,9 +328,7 @@
                     at = (4 + (row + 2 if row < 0 else row - g.la)) * h
                     coarse_in[a * h : (a + 1) * h] = near[at : at + h]
 
-    first = ang * g.la + worker * ra
-    top_in = jnp.where(first > 0, 1.0, 0.0).astype(F32)
-    bottom_in = jnp.where(first + ra < g.m * g.la, 1.0, 0.0).astype(F32)
+    top_in, bottom_in = edges_inside(g, worker)
     for a in range(ra + 4):
         x = coarse_in[a * h : (a + 1) * h]
         for db in range(3):
@@ -350,8 +355,7 @@
                 for ri, step_r in ((1 + cr, 0), (3, -1) if cr == 0 else (0, 1)):
                     mid_ext[ri, row, bi] = along_rows(shifted, step_r * s_count)
 
-    def cell_rows(a, c, pr):
-        return pl.ds(pl.multiple_of(((a * 8 + c) * 2 + pr) * h, 8), h)
+    cell_rows = functools.partial(cell_rows_of, g)
 
     def fine_cells(c, carry):
         for pr in range(2):
@@ -435,11 +439,6 @@
 
     lax.fori_loop(0, 8 * ra, positions, 0)
 
-    parts = [thirds(cells[phase]) for phase in range(2)]
-    order = [place_columns(b, 2, phase) for phase in range(2)]
-    for half in range(2):
-        lanes = slice(half * b, (half + 1) * b)
-        joined[half] = exact_dot(parts[0], order[0][:, lanes]) + exact_dot(parts[1], order[1][:, lanes])
     shown = None
     for phase in range(4):
         value = exact_dot(thirds(seen[phase]), place_columns(b, 4, phase))
@@ -447,15 +446,17 @@
     per = 4 * g.stars * ra * s_count
     for part in range(4):
         resid_out[part * per : (part + 1) * per] = shown[:, part * b : (part + 1) * b]
-    for r in range(n):
-        for s in range(s_count):
-            sub = r * s_count + s
-            for half in range(2):
-                for a in range(2 * ra):
-                    at = ((half * 2 * ra + a) * s_count + s) * 16
-                    stage[r, at : at + 16] = joined[half, pl.ds(a * 16 * h + sub, 16, stride=h), :]
-    for k in range(n):
-        out_refs[k][...] = stage[lax.rem(me + k, n)]
+
+
+def backward_kernel(g, spread, cells, parent, coarse_sum, edge_sum, tall):
+    n, b, s_count, ra, h = g.n, g.b, g.s, g.ra, g.h
+    rows_a = 2 * ra + 2
+    worker = jnp.minimum(lax.axis_index("rad"), g.w - 1)
+    top_in, bottom_in = edges_inside(g, worker)
+    cell_rows = functools.partial(cell_rows_of, g)
+
+    def weight_at(level, c, o):
+        return spread[(level * 8 + c) * 27 + o]
 
     tall[...] = jnp.zeros(tall.shape, F32)
     for pr in range(2):
@@ -521,53 +522,100 @@
                     edge_sum[(4 + t) * h : (5 + t) * h] = coarse_sum[a * h : (a + 1) * h]
 
 
-def sums_kernel(g, parent, coarse_sum, edge_ref, *rest):
+def lanes_kernel(g, cells, out, joined):
+    n, b, s_count, ra, h = g.n, g.b, g.s, g.ra, g.h
+    parts = [thirds(cells[phase]) for phase in range(2)]
+    order = [place_columns(b, 2, phase) for phase in range(2)]
+    for half in range(2):
+        lanes = slice(half * b, (half + 1) * b)
+        joined[half] = exact_dot(parts[0], order[0][:, lanes]) + exact_dot(parts[1], order[1][:, lanes])
+    for r in range(n):
+        for s in range(s_count):
+            for half in range(2):
+                for a in range(2 * ra):
+                    at = ((half * 2 * ra + a) * s_count + s) * 16
+                    out[r, at : at + 16] = joined[half, pl.ds(a * 16 * h + r * s_count + s, 16, stride=h), :]
+
+
+def sums_kernel(g, field, parent, coarse_sum, edge_ref, *rest):
     out_refs, (stage,) = rest[: g.n], rest[g.n :]
     me, ang = lax.axis_index("rad"), lax.axis_index("ang")
     n, s_count, ra, h = g.n, g.s, g.ra, g.h
     rows_a = 2 * ra + 2
     live = jnp.where(jnp.minimum(me, g.w - 1) < g.w // 2, ang < g.m - 1, ang > 0)
-    end_mid, end_coarse, _ = small_back(g)
+    end_field, end_mid, end_coarse, end = rows_back(g)
     for r in range(n):
         for s in range(s_count):
             sub = r * s_count + s
             at = s * 4 * rows_a
             stage[r, at : at + 4 * rows_a] = parent[pl.ds(sub, 4 * rows_a, stride=h), :]
-            at = end_mid + (ra + 4) * s
+            at = end_mid - end_field + (ra + 4) * s
             stage[r, at : at + ra + 4] = coarse_sum[pl.ds(sub, ra + 4, stride=h), :]
-            at = end_coarse + 6 * s
+            at = end_coarse - end_field + 6 * s
             stage[r, at : at + 6] = jnp.where(live, edge_ref[pl.ds(sub, 6, stride=h), :], 0.0)
     for k in range(n):
-        out_refs[k][...] = stage[lax.rem(me + k, n)]
-
-
-def large_owner_kernel(g, block, *rest):
-    in_refs, shown_refs, rest = rest[: g.n], rest[g.n : 2 * g.n], rest[2 * g.n :]
-    fine_out, resid_out, mid_mix, got, shown, fine = rest
+        owner = lax.rem(me + k, n)
+        out_refs[k][:end_field] = field[owner]
+        out_refs[k][end_field:end] = stage[owner]
+
+
+def join_kernel(g, one, two, after, out):
+    rows = one.shape[0]
+    out[:rows] = one[...]
+    out[rows:] = two[...]
+
+
+def resid_owner_kernel(g, ids, block, *rest):
+    in_refs, (resid_out, mixes, shown) = rest[:-3], rest[-3:]
+    me = lax.axis_index("rad")
+    b, s_count, ra = g.b, g.s, g.ra
+    begins, end = prepared_rows(g)
+    per = 4 * g.stars * ra
+    mixes[...] = block[begins["mid"] : end]
+    for ref, held_ids in zip(in_refs, ids):
+        for at, i in enumerate(held_ids):
+            shown[me ^ i] = ref[at * 4 * s_count * per : (at + 1) * 4 * s_count * per]
+    for q in range(g.w):
+        for s in range(s_count):
+            for part in range(4):
+                for star in range(g.stars):
+                    at = (part * s_count + s) * per + star * 4 * ra
+                    rows = slice(4 * q * ra, 4 * (q + 1) * ra)
+                    resid_out[s, star, rows, part * b : (part + 1) * b] = shown[q, at : at + 4 * ra]
+
+
+def owner_kernel(g, mixes, *rest):
+    in_refs, (coarse_out, mid_out, fine_out, got, fine, grad_mid, grad_coarse) = rest[: g.n], rest[g.n :]
     me = lax.axis_index("rad")
     n, b, s_count, ra, la = g.n, g.b, g.s, g.ra, g.la
-    begins, _ = prepared_rows(g)
-    per = 4 * g.stars * ra
-    mid_mix[...] = block[begins["mid"] : begins["mid"] + 64]
+    rows_a = 2 * ra + 2
+    end_field, end_mid, end_coarse, _ = rows_back(g)
     for k in range(n):
         got[lax.rem(me + n - k, n)] = in_refs[k][...]
-        shown[me ^ k] = shown_refs[k][...]
+    grad_mid[...] = jnp.zeros(grad_mid.shape, F32)
+    grad_coarse[...] = jnp.zeros(grad_coarse.shape, F32)
     for q in range(g.w):
+        low = q < g.w // 2
         for s in range(s_count):
             for half in range(2):
                 for a in range(2 * ra):
                     at = ((half * 2 * ra + a) * s_count + s) * 16
                     rows = pl.ds(s * 32 * la + 2 * q * ra + a, 16, stride=2 * la)
                     fine[half, rows, :] = got[q, at : at + 16]
-            for part in range(4):
-                for star in range(g.stars):
-                    at = (part * s_count + s) * per + star * 4 * ra
-                    rows = slice(4 * q * ra, 4 * (q + 1) * ra)
-                    resid_out[s, star, rows, part * b : (part + 1) * b] = shown[q, at : at + 4 * ra]
+            edge = got[q, end_coarse + 6 * s : end_coarse + 6 * s + 6]
+            for x in range(4):
+                at = end_field + s * 4 * rows_a + x * rows_a
+                grad_mid[s, x, 2 * q * ra : 2 * q * ra + rows_a] += got[q, at : at + rows_a]
+                row = 2 * la if low else 1
+                grad_mid[s, x, row : row + 1] += edge[x : x + 1]
+            at = end_mid + (ra + 4) * s
+            grad_coarse[s, q * ra : q * ra + ra + 4] += got[q, at : at + ra + 4]
+            row = la if low else 2
+            grad_coarse[s, row : row + 2] += edge[4:6]
     for i in range(2):
         for j in range(8):
-            rows = [begins["fine"] + 64 * i + 8 * c + j for c in range(8)]
-            weight = [block[row : row + 1] for row in rows]
+            rows = [64 + 64 * i + 8 * c + j for c in range(8)]
+            weight = [mixes[row : row + 1] for row in rows]
             for s in range(s_count):
                 for half in range(2):
                     total = None
@@ -576,31 +624,6 @@
                         term = weight[c] * fine[half, at : at + 2 * la]
                         total = term if total is None else total + term
                     fine_out[s, j, i, :, half * b : (half + 1) * b] = total
-
-
-def small_owner_kernel(g, mid_mix, *rest):
-    in_refs, (coarse_out, mid_out, near, grad_mid, grad_coarse) = rest[: g.n], rest[g.n :]
-    me = lax.axis_index("rad")
-    n, s_count, ra, la = g.n, g.s, g.ra, g.la
-    rows_a = 2 * ra + 2
-    end_mid, end_coarse, _ = small_back(g)
-    for k in range(n):
-        near[lax.rem(me + n - k, n)] = in_refs[k][...]
-    grad_mid[...] = jnp.zeros(grad_mid.shape, F32)
-    grad_coarse[...] = jnp.zeros(grad_coarse.shape, F32)
-    for q in range(g.w):
-        low = q < g.w // 2
-        for s in range(s_count):
-            edge = near[q, end_coarse + 6 * s : end_coarse + 6 * s + 6]
-            for x in range(4):
-                at = s * 4 * rows_a + x * rows_a
-                grad_mid[s, x, 2 * q * ra : 2 * q * ra + rows_a] += near[q, at : at + rows_a]
-                row = 2 * la if low else 1
-                grad_mid[s, x, row : row + 1] += edge[x : x + 1]
-            at = end_mid + (ra + 4) * s
-            grad_coarse[s, q * ra : q * ra + ra + 4] += near[q, at : at + ra + 4]
-            row = la if low else 2
-            grad_coarse[s, row : row + 2] += edge[4:6]
     for s in range(s_count):
         coarse_out[s, 0] = grad_coarse[s, 2 : 2 + la]
         cells = []
@@ -608,9 +631,9 @@
             cr, ca, cb = c // 4, c // 2 % 2, c % 2
             cells.append(grad_mid[s, 2 * cr + cb, pl.ds(1 + ca, la, stride=2), :])
         for j in range(8):
-            total = mid_mix[j : j + 1] * cells[0]
+            total = mixes[j : j + 1] * cells[0]
             for c in range(1, 8):
-                total = total + mid_mix[j + 8 * c : j + 8 * c + 1] * cells[c]
+                total = total + mixes[j + 8 * c : j + 8 * c + 1] * cells[c]
             mid_out[s, j, 0] = total
 
 
@@ -701,59 +724,66 @@
     near = lax.ppermute(near, ("rad", "ang"), inward)
     parts = [(64 * ra * h, b), (64 * ra * h, b), (4 * rows_a * h, b), ((ra + 4) * h, b)]
     unpacked = call(kernel(unpack_kernel, g), "unpack", [(part, F32) for part in parts], got, [])
-    def everywhere(block):
-        held, bit = {0: block}, n // 2
-        while bit:
-            swap = [(i, i ^ bit) for i in range(n)]
-            held |= {i ^ bit: lax.ppermute(x, "rad", swap) for i, x in held.items()}
-            bit //= 2
-        return [held[i] for i in range(n)]
-
-    field_out, resid_out = [(rows, b) for rows in large_back(g)]
-    *done, shown, parent, coarse_sum, edge = call(
-        kernel(main_kernel, g),
-        "main",
-        [(field_out, F32)] * n
-        + [(shape, F32) for shape in (resid_out, (4 * rows_a * h, b), ((ra + 4) * h, b), (6 * h, b))],
+    def everywhere(block, after):
+        ids, bit = [0], n // 2
+        while True:
+            got = lax.ppermute(block, "rad", [(i, i ^ bit) for i in range(n)])
+            more = [i ^ bit for i in ids]
+            if bit == 1:
+                return (block, got), (ids, more)
+            shape = (2 * block.shape[0], b)
+            (block,) = call(kernel(join_kernel, g), "join", [(shape, F32)], (block, got, after), [])
+            ids, bit = ids + more, bit // 2
+
+    end_field, _, _, end = rows_back(g)
+    resid_rows = 16 * stars * ra * s
+    cells, shown = call(
+        kernel(forward_kernel, g),
+        "forward",
+        [((2, 32 * ra * h, b), F32), ((resid_rows, b), F32)],
         (block, spread, *unpacked, near),
         [
             (4 * rows_a * h, b),
             ((ra + 4) * h, b),
             (3, ra + 4, 3, h, b),
             (4, rows_a, 4, h, b),
-            (4, rows_a, 4, h, b),
-            (2, 32 * ra * h, b),
             (4, 4 * stars * ra * s, b),
-            (2, 32 * ra * h, b),
-            (n, *field_out),
         ],
     )
-    small = (small_back(g)[-1], b)
-    shown = everywhere(shown)
-    got = exchange(done)
+    parent, coarse_sum, edge = call(
+        kernel(backward_kernel, g),
+        "backward",
+        [((4 * rows_a * h, b), F32), (((ra + 4) * h, b), F32), ((6 * h, b), F32)],
+        (spread, cells),
+        [(4, rows_a, 4, h, b)],
+    )
     edge = lax.ppermute(edge, ("rad", "ang"), sideways)
-    near = exchange(
+    (field,) = call(
+        kernel(lanes_kernel, g), "lanes", [((n, end_field, b), F32)], (cells,), [(2, 32 * ra * h, b)]
+    )
+    got = exchange(
         call(
             kernel(sums_kernel, g),
             "sums",
-            [(small, F32)] * n,
-            (parent, coarse_sum, edge),
-            [(n, *small)],
+            [((end, b), F32)] * n,
+            (field, parent, coarse_sum, edge),
+            [(n, end - end_field, b)],
         )
     )
-    grad_fine, residual, mid_mix = call(
-        kernel(large_owner_kernel, g),
-        "large_owner",
-        [((s, 8, 2, 2 * la, 2 * b), F32), ((s, stars, 4 * la, 4 * b), F32), ((64, b), F32)],
-        (block, *got, *shown),
-        [(n, *field_out), (n, *resid_out), (2, 32 * s * la, b)],
-    )
-    grad_coarse, grad_mid = call(
-        kernel(small_owner_kernel, g),
-        "small_owner",
-        [((s, 1, la, b), F32), ((s, 8, 1, la, b), F32)],
-        (mid_mix, *near),
-        [(n, *small), (s, 4, 2 * la + 2, b), (s, la + 4, b)],
+    shown, ids = everywhere(shown, got[0])
+    residual, mixes = call(
+        kernel(resid_owner_kernel, g, ids),
+        "resid_owner",
+        [((s, stars, 4 * la, 4 * b), F32), ((192, b), F32)],
+        (block, *shown),
+        [(n, resid_rows, b)],
+    )
+    grad_coarse, grad_mid, grad_fine = call(
+        kernel(owner_kernel, g),
+        "owner",
+        [((s, 1, la, b), F32), ((s, 8, 1, la, b), F32), ((s, 8, 2, 2 * la, 2 * b), F32)],
+        (mixes, *got),
+        [(n, end, b), (2, 32 * s * la, b), (s, 4, 2 * la + 2, b), (s, la + 4, b)],
     )
     return grad_coarse, grad_mid, grad_fine, residual
 

time: 44.6 us -> 43.2 us (0.969)
  the two profiles are of different devices: /device:TPU:0 before, /device:TPU:11 now
where the time goes in v4:
time: 43.2 us; the launch traced here: 43 us
  waiting for transfers between devices  17.6 us (41%)
  Pallas kernels  11.8 us (27%)
  starting transfers between devices  11.1 us (26%)
  local copies, waits for them, and re-layouts  1.85 us (4%)
  between operations  0.71 us (2%)
    pallas_call x12, Pallas kernels, call(): pl.pallas_call(kernel, name=name, out_shape=[jax.ShapeDtypeStruct(shape,...  11.8 us
    ppermute x6, waiting for transfers between devices, exchange(): lax.ppermute(blocks[k], 'rad', [(i, (i + k) % n) for i in range(n)])  11 us
    ppermute x6, starting transfers between devices, exchange(): lax.ppermute(blocks[k], 'rad', [(i, (i + k) % n) for i in range(n)])  7.18 us
    ppermute x1, waiting for transfers between devices, per_device(): edge = lax.ppermute(edge, ('rad', 'ang'), sideways)  3.73 us
    ppermute x2, starting transfers between devices, everywhere(): got = lax.ppermute(block, 'rad', [(i, i ^ bit) for i in range(n)])  2.2 us
    ppermute x2, waiting for transfers between devices, everywhere(): got = lax.ppermute(block, 'rad', [(i, i ^ bit) for i in range(n)])  1.97 us
    unnamed x4, local copies, waits for them, and re-layouts  1.85 us
    ppermute x1, starting transfers between devices, per_device(): near = lax.ppermute(near, ('rad', 'ang'), inward)  1.64 us
  transfers between devices with their start and end apart: 10, of which 8 were waited for; matrix products, arithmetic and copies ran while one was open for 0% of the time, Pallas kernels for 13%

profile of v4, /device:TPU:11, one launch (start us, length us, event | category | flops | bytes accessed | tf_op | source)
XLA Modules:
  0.0 43.0 jit_solution(14197605431296999599)
XLA Ops:
  0.6 3.0 %scatter.1 = (f32[248,128]{1,0:T(8,128)}, f32[248,128]{1,0:T(8,128)}, f32[248,128]{1,0:T(8,128)}, f32[248,128]{1,0:T(8,128)}) custom-call(f32[4,16,512]{2,1,0:T(8,128)} %rest_0_.2, s32[4]{0:T(128)} %rest_0_.3, f32[8,8,16]{2,1,0:T(8,128)} %bitcast.2, f32[2,1,4,128]{3,2,1,0:T(4,128)} %rest_3_.1, f32[2,8,1,4,128]{4,3,2,1,0:T(4,128)} %rest_4_.2, s32[8]{0:T(128)} %rest_1_.3, ...), custom_call_target="tpu_custom_call" | custom-call | tf_op jit(solution)/shard_map/scatter/pallas_call | solution.py:648
  3.6 1.3 %collective-permute-start = (f32[248,128]{1,0:T(8,128)}, f32[248,128]{1,0:T(8,128)S(1)}, u32[]{:S(2)}, u32[]{:S(2)}) collective-permute-start(f32[248,128]{1,0:T(8,128)} %get-tuple-element.33), channel_id=1, source_target_pairs={{0,8},{8,16},{16,24},{24,0},{1,9},{9,17},{17,25},{25,1},{2,10},{10... | collective-permute-start | bytes 380936 | tf_op jit(solution)/shard_map/ppermute | solution.py:682
  4.9 1.1 %collective-permute-start.1 = (f32[248,128]{1,0:T(8,128)}, f32[248,128]{1,0:T(8,128)S(1)}, u32[]{:S(2)}, u32[]{:S(2)}) collective-permute-start(f32[248,128]{1,0:T(8,128)} %get-tuple-element.34), channel_id=1, source_target_pairs={{0,16},{8,24},{16,0},{24,8},{1,17},{9,25},{17,1},{25,9},{2,18},{10... | collective-permute-start | bytes 380936 | tf_op jit(solution)/shard_map/ppermute | solution.py:682
  6.0 1.4 %collective-permute-start.2 = (f32[248,128]{1,0:T(8,128)}, f32[248,128]{1,0:T(8,128)S(1)}, u32[]{:S(2)}, u32[]{:S(2)}) collective-permute-start(f32[248,128]{1,0:T(8,128)} %get-tuple-element.35), channel_id=1, source_target_pairs={{0,24},{8,0},{16,8},{24,16},{1,25},{9,1},{17,9},{25,17},{2,26},{10... | collective-permute-start | bytes 380936 | tf_op jit(solution)/shard_map/ppermute | solution.py:682
  7.4 2.4 %prepare.1.block = f32[512,128]{1,0:T(8,128)} custom-call(s32[4]{0:T(128)} %rest_0_.3, s32[8]{0:T(128)} %rest_1_.3, f32[8,8,16]{2,1,0:T(8,128)} %bitcast.3, f32[8,8,16]{2,1,0:T(8,128)} %bitcast.5, f32[16,8,27]{2,1,0:T(8,128)} %rest_4_.3, f32[16,8,27]{2,1,0:T(8,128)} %rest_5_.3, s32[4,16,512]{2,1,0:T(8,128)} %rest_6_.1, f32[4,16,512]{2,1,0:T(8,128)} %rest_7_.3, ...), custom_call_target="tpu_custom_call" | custom-call | tf_op jit(solution)/shard_map/prepare/pallas_call | solution.py:648
  9.8 0.0 copy-start
  9.8 0.9 %copy-done = f32[512,128]{1,0:T(8,128)S(1)} copy-done((f32[512,128]{1,0:T(8,128)S(1)}, f32[512,128]{1,0:T(8,128)}, u32[]{:S(2)}) %copy-start) | copy-done | bytes 262168
  10.8 0.9 %copy-done.1 = f32[248,128]{1,0:T(8,128)S(1)} copy-done((f32[248,128]{1,0:T(8,128)S(1)}, f32[248,128]{1,0:T(8,128)}, u32[]{:S(2)}) %copy-start.1) | copy-done | bytes 127000
  11.7 1.2 %weights.1 = (f32[648,8,128]{2,1,0:T(8,128)S(1)}, f32[248,128]{1,0:T(8,128)S(1)}, f32[512,128]{1,0:T(8,128)S(1)}) custom-call(f32[512,128]{1,0:T(8,128)S(1)} %copy-done, f32[248,128]{1,0:T(8,128)S(1)} %copy-done.1), custom_call_target="tpu_custom_call" | custom-call | tf_op jit(solution)/shard_map/weights/pallas_call | solution.py:648
  12.9 0.0 collective-permute-done.rest_1_
  12.9 2.6 %collective-permute-done.1.rest_2_ = f32[248,128]{1,0:T(8,128)S(1)} collective-permute-done((f32[248,128]{1,0:T(8,128)}, f32[248,128]{1,0:T(8,128)S(1)}, u32[]{:S(2)}, u32[]{:S(2)}) %collective-permute-start.1) | collective-permute-done | bytes 127008 | tf_op jit(solution)/shard_map/ppermute | solution.py:682
  15.5 2.7 %collective-permute-done.2.rest_3_ = f32[248,128]{1,0:T(8,128)S(1)} collective-permute-done((f32[248,128]{1,0:T(8,128)}, f32[248,128]{1,0:T(8,128)S(1)}, u32[]{:S(2)}, u32[]{:S(2)}) %collective-permute-start.2) | collective-permute-done | bytes 127008 | tf_op jit(solution)/shard_map/ppermute | solution.py:682
  18.2 1.6 %collective-permute-start.3 = (f32[48,128]{1,0:T(8,128)S(1)}, f32[48,128]{1,0:T(8,128)S(1)}, u32[]{:S(2)}, u32[]{:S(2)}) collective-permute-start(f32[48,128]{1,0:T(8,128)S(1)} %relay.1), channel_id=1, source_target_pairs={{7,0},{0,1},{1,2},{2,3},{3,4},{4,5},{5,6},{6,7},{15,8},{8,9},{9,10... | collective-permute-start | bytes 73736 | tf_op jit(solution)/shard_map/ppermute | solution.py:724
  19.8 0.1 unpack.1
  20.0 0.8 %collective-permute-done.3.rest_4_ = f32[48,128]{1,0:T(8,128)S(1)} collective-permute-done((f32[48,128]{1,0:T(8,128)S(1)}, f32[48,128]{1,0:T(8,128)S(1)}, u32[]{:S(2)}, u32[]{:S(2)}) %collective-permute-start.3) | collective-permute-done | bytes 24608 | tf_op jit(solution)/shard_map/ppermute | solution.py:724
  20.8 2.0 %forward.1 = (f32[2,256,128]{2,1,0:T(8,128)S(1)}, f32[128,128]{1,0:T(8,128)S(1)}) custom-call(f32[512,128]{1,0:T(8,128)S(1)} %get-tuple-element.30.block, f32[648,8,128]{2,1,0:T(8,128)S(1)} %get-tuple-element.31.spread, f32[512,128]{1,0:T(8,128)S(1)} %get-tuple-element.36.rest_0_, f32[512,128]{1,0:T(8,128)S(1)} %get-tuple-element.37.rest_1_, ...), custom_call_target="tpu_custom_call" | custom-call | tf_op jit(solution)/shard_map/forward/pallas_call | solution.py:648
  22.8 1.9 %collective-permute-start.4 = (f32[128,128]{1,0:T(8,128)S(1)}, f32[128,128]{1,0:T(8,128)S(1)}, u32[]{:S(2)}, u32[]{:S(2)}) collective-permute-start(f32[128,128]{1,0:T(8,128)S(1)} %get-tuple-element.40.one), channel_id=1, source_target_pairs={{0,16},{8,24},{16,0},{24,8},{1,17},{9,25},{17,1},{25,9},{2,18},{10... | collective-permute-start | bytes 196616 | tf_op jit(solution)/shard_map/ppermute | solution.py:730
  24.7 0.9 %backward.1 = (f32[128,128]{1,0:T(8,128)S(1)}, f32[40,128]{1,0:T(8,128)S(1)}, f32[48,128]{1,0:T(8,128)S(1)}) custom-call(f32[648,8,128]{2,1,0:T(8,128)S(1)} %get-tuple-element.31.spread, f32[2,256,128]{2,1,0:T(8,128)S(1)} %get-tuple-element.41.cells), custom_call_target="tpu_custom_call" | custom-call | tf_op jit(solution)/shard_map/backward/pallas_call | solution.py:648
  25.6 0.1 collective-permute-start.5
  25.6 0.4 lanes.1.field
  26.1 3.7 %collective-permute-done.5.edge_ref = f32[48,128]{1,0:T(8,128)S(1)} collective-permute-done((f32[48,128]{1,0:T(8,128)S(1)}, f32[48,128]{1,0:T(8,128)S(1)}, u32[]{:S(2)}, u32[]{:S(2)}) %collective-permute-start.5) | collective-permute-done | bytes 24608 | tf_op jit(solution)/shard_map/ppermute | solution.py:760
  29.8 0.1 sums.1
  29.8 0.0 collective-permute-done.4.two
  29.9 0.3 collective-permute-start.6
  30.1 0.8 %collective-permute-start.7 = (f32[184,128]{1,0:T(8,128)S(1)}, f32[184,128]{1,0:T(8,128)S(1)}, u32[]{:S(2)}, u32[]{:S(2)}) collective-permute-start(f32[184,128]{1,0:T(8,128)S(1)} %get-tuple-element.47), channel_id=1, source_target_pairs={{0,8},{8,16},{16,24},{24,0},{1,9},{9,17},{17,25},{25,1},{2,10},{10... | collective-permute-start | bytes 282632 | tf_op jit(solution)/shard_map/ppermute | solution.py:682
  31.0 2.5 %collective-permute-start.8 = (f32[184,128]{1,0:T(8,128)S(1)}, f32[184,128]{1,0:T(8,128)S(1)}, u32[]{:S(2)}, u32[]{:S(2)}) collective-permute-start(f32[184,128]{1,0:T(8,128)S(1)} %get-tuple-element.48), channel_id=1, source_target_pairs={{0,16},{8,24},{16,0},{24,8},{1,17},{9,25},{17,1},{25,9},{2,18},{10... | collective-permute-start | bytes 282632 | tf_op jit(solution)/shard_map/ppermute | solution.py:682
  33.5 2.0 %collective-permute-done.6.rest_1_ = f32[256,128]{1,0:T(8,128)S(1)} collective-permute-done((f32[256,128]{1,0:T(8,128)S(1)}, f32[256,128]{1,0:T(8,128)S(1)}, u32[]{:S(2)}, u32[]{:S(2)}) %collective-permute-start.6) | collective-permute-done | bytes 131104 | tf_op jit(solution)/shard_map/ppermute | solution.py:730
  35.5 0.8 %resid_owner.1 = (f32[2,4,16,512]{3,2,1,0:T(8,128)}, f32[192,128]{1,0:T(8,128)S(1)}) custom-call(f32[512,128]{1,0:T(8,128)S(1)} %get-tuple-element.30.block, f32[256,128]{1,0:T(8,128)S(1)} %join.1.rest_0_, f32[256,128]{1,0:T(8,128)S(1)} %collective-permute-done.6.rest_1_), custom_call_target="tpu_custom_call" | custom-call | tf_op jit(solution)/shard_map/resid_owner/pallas_call | solution.py:648
  36.2 1.2 %collective-permute-done.7.rest_1_ = f32[184,128]{1,0:T(8,128)S(1)} collective-permute-done((f32[184,128]{1,0:T(8,128)S(1)}, f32[184,128]{1,0:T(8,128)S(1)}, u32[]{:S(2)}, u32[]{:S(2)}) %collective-permute-start.7) | collective-permute-done | bytes 94240 | tf_op jit(solution)/shard_map/ppermute | solution.py:682
  37.5 1.3 %collective-permute-done.8.rest_2_ = f32[184,128]{1,0:T(8,128)S(1)} collective-permute-done((f32[184,128]{1,0:T(8,128)S(1)}, f32[184,128]{1,0:T(8,128)S(1)}, u32[]{:S(2)}, u32[]{:S(2)}) %collective-permute-start.8) | collective-permute-done | bytes 94240 | tf_op jit(solution)/shard_map/ppermute | solution.py:682
  38.8 3.2 %collective-permute-done.9.rest_3_ = f32[184,128]{1,0:T(8,128)S(1)} collective-permute-done((f32[184,128]{1,0:T(8,128)S(1)}, f32[184,128]{1,0:T(8,128)S(1)}, u32[]{:S(2)}, u32[]{:S(2)}) %collective-permute-start.9) | collective-permute-done | bytes 94240 | tf_op jit(solution)/shard_map/ppermute | solution.py:682
  42.0 1.0 %owner.1 = (f32[2,1,4,128]{3,2,1,0:T(4,128)}, f32[2,8,1,4,128]{4,3,2,1,0:T(4,128)}, f32[2,8,2,8,256]{4,3,2,1,0:T(8,128)}) custom-call(f32[192,128]{1,0:T(8,128)S(1)} %get-tuple-element.46.mixes, f32[184,128]{1,0:T(8,128)S(1)} %get-tuple-element.45.after.rest_0_, f32[184,128]{1,0:T(8,128)S(1)} %collective-permute-done.7.rest_1_, ...), custom_call_target="tpu_custom_call" | custom-call | tf_op jit(solution)/shard_map/owner/pallas_call | solution.py:648
  (4 shorter events, 0.0 us)
Async XLA Ops:
  3.6 9.3 %collective-permute-start = (f32[248,128]{1,0:T(8,128)}, f32[248,128]{1,0:T(8,128)S(1)}, u32[]{:S(2)}, u32[]{:S(2)}) collective-permute-start(f32[248,128]{1,0:T(8,128)} %get-tuple-element.33), channel_id=1, source_target_pairs={{0,8},{8,16},{16,24},{24,0},{1,9},{9,17},{17,25},{25,1},{2,10},{10... | collective-permute-start | bytes 380936 | tf_op jit(solution)/shard_map/ppermute | solution.py:682
  4.9 10.6 %collective-permute-start.1 = (f32[248,128]{1,0:T(8,128)}, f32[248,128]{1,0:T(8,128)S(1)}, u32[]{:S(2)}, u32[]{:S(2)}) collective-permute-start(f32[248,128]{1,0:T(8,128)} %get-tuple-element.34), channel_id=1, source_target_pairs={{0,16},{8,24},{16,0},{24,8},{1,17},{9,25},{17,1},{25,9},{2,18},{10... | collective-permute-start | bytes 380936 | tf_op jit(solution)/shard_map/ppermute | solution.py:682
  6.0 12.2 %collective-permute-start.2 = (f32[248,128]{1,0:T(8,128)}, f32[248,128]{1,0:T(8,128)S(1)}, u32[]{:S(2)}, u32[]{:S(2)}) collective-permute-start(f32[248,128]{1,0:T(8,128)} %get-tuple-element.35), channel_id=1, source_target_pairs={{0,24},{8,0},{16,8},{24,16},{1,25},{9,1},{17,9},{25,17},{2,26},{10... | collective-permute-start | bytes 380936 | tf_op jit(solution)/shard_map/ppermute | solution.py:682
  9.8 1.0 %copy-start = (f32[512,128]{1,0:T(8,128)S(1)}, f32[512,128]{1,0:T(8,128)}, u32[]{:S(2)}) copy-start(f32[512,128]{1,0:T(8,128)} %prepare.1.block) | copy-start | bytes 786436
  10.8 0.9 %copy-start.1 = (f32[248,128]{1,0:T(8,128)S(1)}, f32[248,128]{1,0:T(8,128)}, u32[]{:S(2)}) copy-start(f32[248,128]{1,0:T(8,128)} %get-tuple-element.29.rest_8_.own) | copy-start | bytes 380932
  18.2 2.6 %collective-permute-start.3 = (f32[48,128]{1,0:T(8,128)S(1)}, f32[48,128]{1,0:T(8,128)S(1)}, u32[]{:S(2)}, u32[]{:S(2)}) collective-permute-start(f32[48,128]{1,0:T(8,128)S(1)} %relay.1), channel_id=1, source_target_pairs={{7,0},{0,1},{1,2},{2,3},{3,4},{4,5},{5,6},{6,7},{15,8},{8,9},{9,10... | collective-permute-start | bytes 73736 | tf_op jit(solution)/shard_map/ppermute | solution.py:724
  22.8 7.1 %collective-permute-start.4 = (f32[128,128]{1,0:T(8,128)S(1)}, f32[128,128]{1,0:T(8,128)S(1)}, u32[]{:S(2)}, u32[]{:S(2)}) collective-permute-start(f32[128,128]{1,0:T(8,128)S(1)} %get-tuple-element.40.one), channel_id=1, source_target_pairs={{0,16},{8,24},{16,0},{24,8},{1,17},{9,25},{17,1},{25,9},{2,18},{10... | collective-permute-start | bytes 196616 | tf_op jit(solution)/shard_map/ppermute | solution.py:730
  25.6 4.2 %collective-permute-start.5 = (f32[48,128]{1,0:T(8,128)S(1)}, f32[48,128]{1,0:T(8,128)S(1)}, u32[]{:S(2)}, u32[]{:S(2)}) collective-permute-start(f32[48,128]{1,0:T(8,128)S(1)} %get-tuple-element.44), channel_id=1, source_target_pairs={{0,7},{1,0},{2,1},{3,2},{4,3},{5,4},{6,5},{7,6},{8,15},{9,8},{10,9... | collective-permute-start | bytes 73736 | tf_op jit(solution)/shard_map/ppermute | solution.py:760
  29.9 5.6 %collective-permute-start.6 = (f32[256,128]{1,0:T(8,128)S(1)}, f32[256,128]{1,0:T(8,128)S(1)}, u32[]{:S(2)}, u32[]{:S(2)}) collective-permute-start(f32[256,128]{1,0:T(8,128)S(1)} %join.1.rest_0_), channel_id=1, source_target_pairs={{0,8},{8,0},{16,24},{24,16},{1,9},{9,1},{17,25},{25,17},{2,10},{10... | collective-permute-start | bytes 393224 | tf_op jit(solution)/shard_map/ppermute | solution.py:730
  30.1 7.3 %collective-permute-start.7 = (f32[184,128]{1,0:T(8,128)S(1)}, f32[184,128]{1,0:T(8,128)S(1)}, u32[]{:S(2)}, u32[]{:S(2)}) collective-permute-start(f32[184,128]{1,0:T(8,128)S(1)} %get-tuple-element.47), channel_id=1, source_target_pairs={{0,8},{8,16},{16,24},{24,0},{1,9},{9,17},{17,25},{25,1},{2,10},{10... | collective-permute-start | bytes 282632 | tf_op jit(solution)/shard_map/ppermute | solution.py:682
  31.0 7.8 %collective-permute-start.8 = (f32[184,128]{1,0:T(8,128)S(1)}, f32[184,128]{1,0:T(8,128)S(1)}, u32[]{:S(2)}, u32[]{:S(2)}) collective-permute-start(f32[184,128]{1,0:T(8,128)S(1)} %get-tuple-element.48), channel_id=1, source_target_pairs={{0,16},{8,24},{16,0},{24,8},{1,17},{9,25},{17,1},{25,9},{2,18},{10... | collective-permute-start | bytes 282632 | tf_op jit(solution)/shard_map/ppermute | solution.py:682
  33.5 8.5 %collective-permute-start.9 = (f32[184,128]{1,0:T(8,128)S(1)}, f32[184,128]{1,0:T(8,128)S(1)}, u32[]{:S(2)}, u32[]{:S(2)}) collective-permute-start(f32[184,128]{1,0:T(8,128)S(1)} %get-tuple-element.49), channel_id=1, source_target_pairs={{0,24},{8,0},{16,8},{24,16},{1,25},{9,1},{17,9},{25,17},{2,26},{10... | collective-permute-start | bytes 282632 | tf_op jit(solution)/shard_map/ppermute | solution.py:682

commit v5 on v4

--- a/solution.py
+++ b/solution.py
@@ -42,15 +42,13 @@
     fine = 2 * 2 * g.ra * g.s * 16
     emit = fine + 16 * 4 * g.ra
     mix = emit + g.s * 4 * (2 * g.ra + 2)
-    coarse = mix + g.s * (g.ra + 4)
-    return fine, emit, mix, coarse, eights(coarse + 6 * g.s)
+    return fine, emit, mix, eights(mix + g.s * (g.ra + 4))
 
 
 def rows_back(g):
     field = 2 * 2 * g.ra * g.s * 16
     mid = field + g.s * 4 * (2 * g.ra + 2)
-    coarse = mid + g.s * (g.ra + 4)
-    return field, mid, coarse, eights(coarse + 6 * g.s)
+    return field, mid, eights(mid + g.s * (g.ra + 4))
 
 
 def prepared_rows(g):
@@ -104,12 +102,13 @@
     high = x.astype(BF16)
     rest = x - high.astype(F32)
     middle = rest.astype(BF16)
-    return high, middle, (rest - middle.astype(F32)).astype(BF16)
+    return jnp.concatenate([high, middle, (rest - middle.astype(F32)).astype(BF16)], axis=0)
 
 
 def exact_dot(parts, choice):
-    high, middle, low = [jnp.dot(part, choice, preferred_element_type=F32) for part in parts]
-    return high + (middle + low)
+    sums = jnp.dot(parts, choice, preferred_element_type=F32)
+    rows = sums.shape[0] // 3
+    return sums[:rows] + (sums[rows : 2 * rows] + sums[2 * rows :])
 
 
 def along_lanes(x, step):
@@ -172,13 +171,17 @@
 def scatter_kernel(g, *rest):
     sources, out_refs, rest = rest[:8], rest[8 : 8 + g.n], rest[8 + g.n :]
     held, (sems, out_sems, raw, split, lit, stage, mixed, wide) = rest[:8], rest[8:]
-    copies = start_all(list(zip(sources, held)), sems)
+    light = start_all([(sources[0].at[f], held[0].at[f]) for f in range(4)], sems)
+    copies = start_all(list(zip(sources[1:7], held[1:7])), sems, 4)
+    spots = [(s, slice(4 * part, 4 * part + 4)) for s in range(g.s) for part in range(2)]
+    copies += start_all([(sources[7].at[spot], held[7].at[spot]) for spot in spots], sems, 10)
     emission_ref, rows_mid, noise_mid, coarse_ref, excite_ref, rows_ref, noise_ref, fine_ref = held
     me = lax.axis_index("rad")
     b, s_count, la = g.b, g.s, g.la
-    end_fine, end_emit, end_mix, end_coarse, _ = large_there(g)
+    end_fine, end_emit, end_mix, _ = large_there(g)
     choices = [pick_columns(b, 4, phase) for phase in range(4)]
-    copies[0].wait()
+    halves = [pick_columns(b, 2, phase) for phase in range(2)]
+    wait_all(light)
     parts = thirds(emission_ref[...].reshape(16 * la, 4 * b))
     for phase in range(4):
         lit[phase] = exact_dot(parts, choices[phase])
@@ -188,7 +191,7 @@
                 at = end_fine + (phase * 4 + f) * 4 * g.ra
                 rows = slice(f * 4 * la + 4 * q * g.ra, f * 4 * la + 4 * (q + 1) * g.ra)
                 stage[q, at : at + 4 * g.ra] = lit[phase, rows]
-    wait_all(copies[1:5])
+    wait_all(copies[:4])
     weight = table_weights(noise_mid, rows_mid[me])
     for c in range(8):
         for s in range(s_count):
@@ -196,32 +199,24 @@
             for j in range(1, 8):
                 total = total + weight(c, j) * excite_ref[s, j, 0]
             mixed[s, c] = total
-    wide[...] = jnp.zeros(wide.shape, F32)
     for s in range(s_count):
+        wide[s, :2] = coarse_ref[s, 0, la - 2 :]
         wide[s, 2 : 2 + la] = coarse_ref[s, 0]
+        wide[s, 2 + la :] = coarse_ref[s, 0, :2]
     for q in range(g.w):
-        low = q < g.w // 2
         for s in range(s_count):
             for row in range(2 * g.ra + 2):
-                a, ca = divmod(2 * q * g.ra - 1 + row, 2)
+                a, ca = divmod((2 * q * g.ra - 1 + row) % (2 * la), 2)
                 for cr in range(2):
                     for cb in range(2):
                         at = end_emit + ((s * (2 * g.ra + 2) + row) * 2 + cr) * 2 + cb
-                        if 0 <= a < la:
-                            stage[q, at : at + 1] = mixed[s, 4 * cr + 2 * ca + cb, a : a + 1]
-                        else:
-                            stage[q, at : at + 1] = jnp.zeros((1, b), F32)
+                        stage[q, at : at + 1] = mixed[s, 4 * cr + 2 * ca + cb, a : a + 1]
             at = end_mix + (g.ra + 4) * s
             stage[q, at : at + g.ra + 4] = wide[s, q * g.ra : q * g.ra + g.ra + 4]
-            at = end_coarse + 6 * s
-            row = la - 1 if low else 0
-            for cr in range(2):
-                for cb in range(2):
-                    c = 4 * cr + (2 if low else 0) + cb
-                    stage[q, at + 2 * cr + cb : at + 2 * cr + cb + 1] = mixed[s, c, row : row + 1]
-            row = la - 2 if low else 0
-            stage[q, at + 4 : at + 6] = coarse_ref[s, 0, row : row + 2]
-    wait_all(copies[5:])
+    workers = [jnp.minimum(lax.rem(me + k, g.n), g.w - 1) for k in range(g.n)]
+    done = [(stage.at[worker, end_fine:], out.at[end_fine:]) for worker, out in zip(workers, out_refs)]
+    done = start_all(done, out_sems)
+    wait_all(copies[4:])
     for i in range(2):
         weight = table_weights(noise_ref, rows_ref[2 * me + i])
         for c in range(8):
@@ -234,7 +229,7 @@
                 raw[at : at + 2 * la] = total
     parts = thirds(raw[...])
     for phase in range(2):
-        split[phase] = exact_dot(parts, pick_columns(b, 2, phase))
+        split[phase] = exact_dot(parts, halves[phase])
     for q in range(g.w):
         for phase in range(2):
             for a in range(2 * g.ra):
@@ -242,25 +237,39 @@
                     at = ((phase * 2 * g.ra + a) * s_count + s) * 16
                     rows = pl.ds(s * 32 * la + 2 * q * g.ra + a, 16, stride=2 * la)
                     stage[q, at : at + 16] = split[phase, rows, :]
-    workers = [jnp.minimum(lax.rem(me + k, g.n), g.w - 1) for k in range(g.n)]
-    wait_all(start_all([(stage.at[worker], out) for worker, out in zip(workers, out_refs)], out_sems))
+    last = [(stage.at[worker, :end_fine], out.at[:end_fine]) for worker, out in zip(workers, out_refs)]
+    wait_all(done + start_all(last, out_sems, g.n))
 
 
 def relay_kernel(g, *rest):
     in_refs, (edge_out,) = rest[: g.n], rest[g.n :]
     me = lax.axis_index("rad")
-    _, _, _, end_coarse, _ = large_there(g)
+    low = jnp.minimum(me, g.w - 1) < g.w // 2
+    _, end_emit, end_mix, _ = large_there(g)
+    rows_a = 2 * g.ra + 2
     for k in range(g.n):
         source = lax.rem(me + g.n - k, g.n)
         for s in range(g.s):
-            rows = pl.ds(source * g.s + s, 6, stride=g.h)
-            edge_out[rows, :] = in_refs[k][end_coarse + 6 * s : end_coarse + 6 * s + 6]
+            sub = source * g.s + s
+            mid = end_emit + s * 4 * rows_a
+            coarse = end_mix + (g.ra + 4) * s
+            end_mid, end_coarse = mid + 4 * rows_a, coarse + g.ra + 4
+            value = jnp.where(low, in_refs[k][mid : mid + 4], in_refs[k][end_mid - 4 : end_mid])
+            edge_out[pl.ds(sub, 4, stride=g.h), :] = value
+            value = jnp.where(low, in_refs[k][coarse : coarse + 2], in_refs[k][end_coarse - 2 : end_coarse])
+            edge_out[pl.ds(4 * g.h + sub, 2, stride=g.h), :] = value
+
+
+def outside(g, q):
+    low = q < g.w // 2
+    rows = [(a, q * g.ra - 2 + a) for a in range(g.ra + 4)]
+    return [(a, a if low else a - g.ra - 2) for a, row in rows if row < 0 or row >= g.la]
 
 
 def unpack_kernel(g, *rest):
     in_refs, (fine_out, emit_out, mix_out, coarse_out) = rest[: g.n], rest[g.n :]
     me = lax.axis_index("rad")
-    end_fine, end_emit, end_mix, _, _ = large_there(g)
+    end_fine, end_emit, end_mix, _ = large_there(g)
     h, ra, rows_a = g.h, g.ra, 2 * g.ra + 2
     for k in range(g.n):
         source = lax.rem(me + g.n - k, g.n)
@@ -316,17 +325,15 @@
     coarse_in[...] = coarse[...]
     live = jnp.where(worker < g.w // 2, ang > 0, ang < g.m - 1)
     for q in range(g.w):
-        @pl.when(jnp.logical_and(worker == q, live))
+        @pl.when(worker == q)
         def _(q=q):
             if q == 0:
-                mix_in[: 4 * h] = near[: 4 * h]
+                mix_in[: 4 * h] = jnp.where(live, near[: 4 * h], 0.0)
             if q == g.w - 1:
-                mix_in[4 * (rows_a - 1) * h :] = near[: 4 * h]
-            for a in range(ra + 4):
-                row = q * ra - 2 + a
-                if row < 0 or row >= g.la:
-                    at = (4 + (row + 2 if row < 0 else row - g.la)) * h
-                    coarse_in[a * h : (a + 1) * h] = near[at : at + h]
+                mix_in[4 * (rows_a - 1) * h :] = jnp.where(live, near[: 4 * h], 0.0)
+            for a, place in outside(g, q):
+                at = (4 + place) * h
+                coarse_in[a * h : (a + 1) * h] = jnp.where(live, near[at : at + h], 0.0)
 
     top_in, bottom_in = edges_inside(g, worker)
     for a in range(ra + 4):
@@ -507,19 +514,11 @@
             for a, value in sums.items():
                 coarse_sum[a * h : (a + 1) * h] += along_lanes(along_rows(value, (dr - 1) * s_count), db - 1)
 
-    edge_sum[...] = jnp.zeros(edge_sum.shape, F32)
-    for q in range(g.w):
-        @pl.when(worker == q)
-        def _(q=q):
-            low = q < g.w // 2
-            if q == 0 or q == g.w - 1:
-                for x in range(4):
-                    at = (x * rows_a + (0 if low else rows_a - 1)) * h
-                    edge_sum[x * h : (x + 1) * h] = parent[at : at + h]
-            for t in range(2):
-                a = (t - 2 if low else g.la + t) - q * ra + 2
-                if 0 <= a < ra + 4:
-                    edge_sum[(4 + t) * h : (5 + t) * h] = coarse_sum[a * h : (a + 1) * h]
+    low = worker < g.w // 2
+    for x in range(4):
+        at, end = x * rows_a * h, (x + 1) * rows_a * h
+        edge_sum[x * h : (x + 1) * h] = jnp.where(low, parent[at : at + h], parent[end - h : end])
+    edge_sum[4 * h :] = jnp.where(low, coarse_sum[: 2 * h], coarse_sum[(ra + 2) * h :])
 
 
 def lanes_kernel(g, cells, out, joined):
@@ -537,13 +536,26 @@
                     out[r, at : at + 16] = joined[half, pl.ds(a * 16 * h + r * s_count + s, 16, stride=h), :]
 
 
-def sums_kernel(g, field, parent, coarse_sum, edge_ref, *rest):
-    out_refs, (stage,) = rest[: g.n], rest[g.n :]
+def sums_kernel(g, field, parent_ref, coarse_ref, edge_ref, *rest):
+    out_refs, (stage, parent, coarse_sum) = rest[: g.n], rest[g.n :]
     me, ang = lax.axis_index("rad"), lax.axis_index("ang")
     n, s_count, ra, h = g.n, g.s, g.ra, g.h
     rows_a = 2 * ra + 2
-    live = jnp.where(jnp.minimum(me, g.w - 1) < g.w // 2, ang < g.m - 1, ang > 0)
-    end_field, end_mid, end_coarse, end = rows_back(g)
+    worker = jnp.minimum(me, g.w - 1)
+    live = jnp.where(worker < g.w // 2, ang < g.m - 1, ang > 0)
+    end_field, end_mid, end = rows_back(g)
+    parent[...] = parent_ref[...]
+    coarse_sum[...] = coarse_ref[...]
+    for q in range(g.w):
+        @pl.when(worker == q)
+        def _(q=q):
+            if q == 0 or q == g.w - 1:
+                for x in range(4):
+                    at = (x * rows_a + (0 if q == 0 else rows_a - 1)) * h
+                    parent[at : at + h] = jnp.where(live, edge_ref[x * h : (x + 1) * h], 0.0)
+            for a, place in outside(g, q):
+                at = (4 + place) * h
+                coarse_sum[a * h : (a + 1) * h] = jnp.where(live, edge_ref[at : at + h], 0.0)
     for r in range(n):
         for s in range(s_count):
             sub = r * s_count + s
@@ -551,8 +563,6 @@
             stage[r, at : at + 4 * rows_a] = parent[pl.ds(sub, 4 * rows_a, stride=h), :]
             at = end_mid - end_field + (ra + 4) * s
             stage[r, at : at + ra + 4] = coarse_sum[pl.ds(sub, ra + 4, stride=h), :]
-            at = end_coarse - end_field + 6 * s
-            stage[r, at : at + 6] = jnp.where(live, edge_ref[pl.ds(sub, 6, stride=h), :], 0.0)
     for k in range(n):
         owner = lax.rem(me + k, n)
         out_refs[k][:end_field] = field[owner]
@@ -589,29 +599,29 @@
     me = lax.axis_index("rad")
     n, b, s_count, ra, la = g.n, g.b, g.s, g.ra, g.la
     rows_a = 2 * ra + 2
-    end_field, end_mid, end_coarse, _ = rows_back(g)
+    end_field, end_mid, _ = rows_back(g)
     for k in range(n):
         got[lax.rem(me + n - k, n)] = in_refs[k][...]
     grad_mid[...] = jnp.zeros(grad_mid.shape, F32)
     grad_coarse[...] = jnp.zeros(grad_coarse.shape, F32)
     for q in range(g.w):
-        low = q < g.w // 2
         for s in range(s_count):
             for half in range(2):
                 for a in range(2 * ra):
                     at = ((half * 2 * ra + a) * s_count + s) * 16
                     rows = pl.ds(s * 32 * la + 2 * q * ra + a, 16, stride=2 * la)
                     fine[half, rows, :] = got[q, at : at + 16]
-            edge = got[q, end_coarse + 6 * s : end_coarse + 6 * s + 6]
             for x in range(4):
                 at = end_field + s * 4 * rows_a + x * rows_a
                 grad_mid[s, x, 2 * q * ra : 2 * q * ra + rows_a] += got[q, at : at + rows_a]
-                row = 2 * la if low else 1
-                grad_mid[s, x, row : row + 1] += edge[x : x + 1]
             at = end_mid + (ra + 4) * s
             grad_coarse[s, q * ra : q * ra + ra + 4] += got[q, at : at + ra + 4]
-            row = la if low else 2
-            grad_coarse[s, row : row + 2] += edge[4:6]
+    for s in range(s_count):
+        for x in range(4):
+            grad_mid[s, x, 1:2] += grad_mid[s, x, 2 * la + 1 :]
+            grad_mid[s, x, 2 * la : 2 * la + 1] += grad_mid[s, x, :1]
+        grad_coarse[s, 2:4] += grad_coarse[s, la + 2 :]
+        grad_coarse[s, la : la + 2] += grad_coarse[s, :2]
     for i in range(2):
         for j in range(8):
             rows = [64 + 64 * i + 8 * c + j for c in range(8)]
@@ -691,8 +701,8 @@
         operands,
         [
             *held(operands),
-            pltpu.SemaphoreType.DMA((8,)),
-            pltpu.SemaphoreType.DMA((n,)),
+            pltpu.SemaphoreType.DMA((10 + 2 * s,)),
+            pltpu.SemaphoreType.DMA((2 * n,)),
             (32 * s * la, 2 * b),
             (2, 32 * s * la, b),
             (4, 16 * la, b),
@@ -735,7 +745,7 @@
             (block,) = call(kernel(join_kernel, g), "join", [(shape, F32)], (block, got, after), [])
             ids, bit = ids + more, bit // 2
 
-    end_field, _, _, end = rows_back(g)
+    end_field, _, end = rows_back(g)
     resid_rows = 16 * stars * ra * s
     cells, shown = call(
         kernel(forward_kernel, g),
@@ -767,7 +777,7 @@
             "sums",
             [((end, b), F32)] * n,
             (field, parent, coarse_sum, edge),
-            [(n, end - end_field, b)],
+            [(n, end - end_field, b), parent.shape, coarse_sum.shape],
         )
     )
     shown, ids = everywhere(shown, got[0])

time: 43.2 us -> 42.3 us (0.979)
  waiting for transfers between devices: 17.6 us -> 17 us
    ppermute x6, waiting for transfers between devices: 11 us -> 10.4 us  [exchange(): lax.ppermute(blocks[k], 'rad', [(i, (i + k) % n) for i in range(n)])]
where the time goes in v5:
time: 42.3 us; the launch traced here: 42 us
  waiting for transfers between devices  17 us (40%)
  Pallas kernels  11.4 us (27%)
  starting transfers between devices  11.1 us (26%)
  local copies, waits for them, and re-layouts  1.85 us (4%)
  between operations  0.72 us (2%)
    pallas_call x12, Pallas kernels, call(): pl.pallas_call(kernel, name=name, out_shape=[jax.ShapeDtypeStruct(shape,...  11.4 us
    ppermute x6, waiting for transfers between devices, exchange(): lax.ppermute(blocks[k], 'rad', [(i, (i + k) % n) for i in range(n)])  10.4 us
    ppermute x6, starting transfers between devices, exchange(): lax.ppermute(blocks[k], 'rad', [(i, (i + k) % n) for i in range(n)])  7.13 us
    ppermute x1, waiting for transfers between devices, per_device(): edge = lax.ppermute(edge, ('rad', 'ang'), sideways)  3.74 us
    ppermute x2, starting transfers between devices, everywhere(): got = lax.ppermute(block, 'rad', [(i, i ^ bit) for i in range(n)])  2.26 us
    ppermute x2, waiting for transfers between devices, everywhere(): got = lax.ppermute(block, 'rad', [(i, i ^ bit) for i in range(n)])  1.96 us
    unnamed x4, local copies, waits for them, and re-layouts  1.85 us
    ppermute x1, starting transfers between devices, per_device(): near = lax.ppermute(near, ('rad', 'ang'), inward)  1.64 us
  transfers between devices with their start and end apart: 10, of which 8 were waited for; matrix products, arithmetic and copies ran while one was open for 0% of the time, Pallas kernels for 13%

profile of v5, /device:TPU:11, one launch (start us, length us, event | category | flops | bytes accessed | tf_op | source)
XLA Modules:
  0.0 42.0 jit_solution(16913695870443805740)
XLA Ops:
  0.6 2.8 %scatter.1 = (f32[240,128]{1,0:T(8,128)}, f32[240,128]{1,0:T(8,128)}, f32[240,128]{1,0:T(8,128)}, f32[240,128]{1,0:T(8,128)}) custom-call(f32[4,16,512]{2,1,0:T(8,128)} %rest_0_.2, s32[4]{0:T(128)} %rest_0_.3, f32[8,8,16]{2,1,0:T(8,128)} %bitcast.2, f32[2,1,4,128]{3,2,1,0:T(4,128)} %rest_3_.1, f32[2,8,1,4,128]{4,3,2,1,0:T(4,128)} %rest_4_.2, s32[8]{0:T(128)} %rest_1_.3, ...), custom_call_target="tpu_custom_call" | custom-call | tf_op jit(solution)/shard_map/scatter/pallas_call | solution.py:658
  3.4 1.4 %collective-permute-start = (f32[240,128]{1,0:T(8,128)}, f32[240,128]{1,0:T(8,128)S(1)}, u32[]{:S(2)}, u32[]{:S(2)}) collective-permute-start(f32[240,128]{1,0:T(8,128)} %get-tuple-element.33), channel_id=1, source_target_pairs={{0,8},{8,16},{16,24},{24,0},{1,9},{9,17},{17,25},{25,1},{2,10},{10... | collective-permute-start | bytes 368648 | tf_op jit(solution)/shard_map/ppermute | solution.py:692
  4.8 1.1 %collective-permute-start.1 = (f32[240,128]{1,0:T(8,128)}, f32[240,128]{1,0:T(8,128)S(1)}, u32[]{:S(2)}, u32[]{:S(2)}) collective-permute-start(f32[240,128]{1,0:T(8,128)} %get-tuple-element.34), channel_id=1, source_target_pairs={{0,16},{8,24},{16,0},{24,8},{1,17},{9,25},{17,1},{25,9},{2,18},{10... | collective-permute-start | bytes 368648 | tf_op jit(solution)/shard_map/ppermute | solution.py:692
  5.9 1.4 %collective-permute-start.2 = (f32[240,128]{1,0:T(8,128)}, f32[240,128]{1,0:T(8,128)S(1)}, u32[]{:S(2)}, u32[]{:S(2)}) collective-permute-start(f32[240,128]{1,0:T(8,128)} %get-tuple-element.35), channel_id=1, source_target_pairs={{0,24},{8,0},{16,8},{24,16},{1,25},{9,1},{17,9},{25,17},{2,26},{10... | collective-permute-start | bytes 368648 | tf_op jit(solution)/shard_map/ppermute | solution.py:692
  7.3 2.3 %prepare.1.block = f32[512,128]{1,0:T(8,128)} custom-call(s32[4]{0:T(128)} %rest_0_.3, s32[8]{0:T(128)} %rest_1_.3, f32[8,8,16]{2,1,0:T(8,128)} %bitcast.3, f32[8,8,16]{2,1,0:T(8,128)} %bitcast.5, f32[16,8,27]{2,1,0:T(8,128)} %rest_4_.3, f32[16,8,27]{2,1,0:T(8,128)} %rest_5_.3, s32[4,16,512]{2,1,0:T(8,128)} %rest_6_.1, f32[4,16,512]{2,1,0:T(8,128)} %rest_7_.3, ...), custom_call_target="tpu_custom_call" | custom-call | tf_op jit(solution)/shard_map/prepare/pallas_call | solution.py:658
  9.6 0.0 copy-start
  9.6 0.9 %copy-done = f32[512,128]{1,0:T(8,128)S(1)} copy-done((f32[512,128]{1,0:T(8,128)S(1)}, f32[512,128]{1,0:T(8,128)}, u32[]{:S(2)}) %copy-start) | copy-done | bytes 262168
  10.5 0.9 %copy-done.1 = f32[240,128]{1,0:T(8,128)S(1)} copy-done((f32[240,128]{1,0:T(8,128)S(1)}, f32[240,128]{1,0:T(8,128)}, u32[]{:S(2)}) %copy-start.1) | copy-done | bytes 122904
  11.4 1.2 %weights.1 = (f32[648,8,128]{2,1,0:T(8,128)S(1)}, f32[240,128]{1,0:T(8,128)S(1)}, f32[512,128]{1,0:T(8,128)S(1)}) custom-call(f32[512,128]{1,0:T(8,128)S(1)} %copy-done, f32[240,128]{1,0:T(8,128)S(1)} %copy-done.1), custom_call_target="tpu_custom_call" | custom-call | tf_op jit(solution)/shard_map/weights/pallas_call | solution.py:658
  12.6 0.0 collective-permute-done.rest_1_
  12.6 2.4 %collective-permute-done.1.rest_2_ = f32[240,128]{1,0:T(8,128)S(1)} collective-permute-done((f32[240,128]{1,0:T(8,128)}, f32[240,128]{1,0:T(8,128)S(1)}, u32[]{:S(2)}, u32[]{:S(2)}) %collective-permute-start.1) | collective-permute-done | bytes 122912 | tf_op jit(solution)/shard_map/ppermute | solution.py:692
  15.0 2.7 %collective-permute-done.2.rest_3_ = f32[240,128]{1,0:T(8,128)S(1)} collective-permute-done((f32[240,128]{1,0:T(8,128)}, f32[240,128]{1,0:T(8,128)S(1)}, u32[]{:S(2)}, u32[]{:S(2)}) %collective-permute-start.2) | collective-permute-done | bytes 122912 | tf_op jit(solution)/shard_map/ppermute | solution.py:692
  17.7 1.6 %collective-permute-start.3 = (f32[48,128]{1,0:T(8,128)S(1)}, f32[48,128]{1,0:T(8,128)S(1)}, u32[]{:S(2)}, u32[]{:S(2)}) collective-permute-start(f32[48,128]{1,0:T(8,128)S(1)} %relay.1), channel_id=1, source_target_pairs={{7,0},{0,1},{1,2},{2,3},{3,4},{4,5},{5,6},{6,7},{15,8},{8,9},{9,10... | collective-permute-start | bytes 73736 | tf_op jit(solution)/shard_map/ppermute | solution.py:734
  19.4 0.1 unpack.1
  19.5 0.8 %collective-permute-done.3.rest_4_ = f32[48,128]{1,0:T(8,128)S(1)} collective-permute-done((f32[48,128]{1,0:T(8,128)S(1)}, f32[48,128]{1,0:T(8,128)S(1)}, u32[]{:S(2)}, u32[]{:S(2)}) %collective-permute-start.3) | collective-permute-done | bytes 24608 | tf_op jit(solution)/shard_map/ppermute | solution.py:734
  20.3 1.9 %forward.1 = (f32[2,256,128]{2,1,0:T(8,128)S(1)}, f32[128,128]{1,0:T(8,128)S(1)}) custom-call(f32[512,128]{1,0:T(8,128)S(1)} %get-tuple-element.30.block, f32[648,8,128]{2,1,0:T(8,128)S(1)} %get-tuple-element.31.spread, f32[512,128]{1,0:T(8,128)S(1)} %get-tuple-element.36.rest_0_, f32[512,128]{1,0:T(8,128)S(1)} %get-tuple-element.37.rest_1_, ...), custom_call_target="tpu_custom_call" | custom-call | tf_op jit(solution)/shard_map/forward/pallas_call | solution.py:658
  22.2 1.9 %collective-permute-start.4 = (f32[128,128]{1,0:T(8,128)S(1)}, f32[128,128]{1,0:T(8,128)S(1)}, u32[]{:S(2)}, u32[]{:S(2)}) collective-permute-start(f32[128,128]{1,0:T(8,128)S(1)} %get-tuple-element.40.one), channel_id=1, source_target_pairs={{0,16},{8,24},{16,0},{24,8},{1,17},{9,25},{17,1},{25,9},{2,18},{10... | collective-permute-start | bytes 196616 | tf_op jit(solution)/shard_map/ppermute | solution.py:740
  24.2 0.8 %backward.1 = (f32[128,128]{1,0:T(8,128)S(1)}, f32[40,128]{1,0:T(8,128)S(1)}, f32[48,128]{1,0:T(8,128)S(1)}) custom-call(f32[648,8,128]{2,1,0:T(8,128)S(1)} %get-tuple-element.31.spread, f32[2,256,128]{2,1,0:T(8,128)S(1)} %get-tuple-element.41.cells), custom_call_target="tpu_custom_call" | custom-call | tf_op jit(solution)/shard_map/backward/pallas_call | solution.py:658
  25.0 0.1 collective-permute-start.5
  25.1 0.4 lanes.1.field
  25.5 3.7 %collective-permute-done.5.edge_ref = f32[48,128]{1,0:T(8,128)S(1)} collective-permute-done((f32[48,128]{1,0:T(8,128)S(1)}, f32[48,128]{1,0:T(8,128)S(1)}, u32[]{:S(2)}, u32[]{:S(2)}) %collective-permute-start.5) | collective-permute-done | bytes 24608 | tf_op jit(solution)/shard_map/ppermute | solution.py:770
  29.2 0.1 sums.1
  29.3 0.0 collective-permute-done.4.two
  29.3 0.3 collective-permute-start.6
  29.6 0.8 %collective-permute-start.7 = (f32[176,128]{1,0:T(8,128)S(1)}, f32[176,128]{1,0:T(8,128)S(1)}, u32[]{:S(2)}, u32[]{:S(2)}) collective-permute-start(f32[176,128]{1,0:T(8,128)S(1)} %get-tuple-element.47), channel_id=1, source_target_pairs={{0,8},{8,16},{16,24},{24,0},{1,9},{9,17},{17,25},{25,1},{2,10},{10... | collective-permute-start | bytes 270344 | tf_op jit(solution)/shard_map/ppermute | solution.py:692
  30.4 2.5 %collective-permute-start.8 = (f32[176,128]{1,0:T(8,128)S(1)}, f32[176,128]{1,0:T(8,128)S(1)}, u32[]{:S(2)}, u32[]{:S(2)}) collective-permute-start(f32[176,128]{1,0:T(8,128)S(1)} %get-tuple-element.48), channel_id=1, source_target_pairs={{0,16},{8,24},{16,0},{24,8},{1,17},{9,25},{17,1},{25,9},{2,18},{10... | collective-permute-start | bytes 270344 | tf_op jit(solution)/shard_map/ppermute | solution.py:692
  32.9 2.0 %collective-permute-done.6.rest_1_ = f32[256,128]{1,0:T(8,128)S(1)} collective-permute-done((f32[256,128]{1,0:T(8,128)S(1)}, f32[256,128]{1,0:T(8,128)S(1)}, u32[]{:S(2)}, u32[]{:S(2)}) %collective-permute-start.6) | collective-permute-done | bytes 131104 | tf_op jit(solution)/shard_map/ppermute | solution.py:740
  34.9 0.8 %resid_owner.1 = (f32[2,4,16,512]{3,2,1,0:T(8,128)}, f32[192,128]{1,0:T(8,128)S(1)}) custom-call(f32[512,128]{1,0:T(8,128)S(1)} %get-tuple-element.30.block, f32[256,128]{1,0:T(8,128)S(1)} %join.1.rest_0_, f32[256,128]{1,0:T(8,128)S(1)} %collective-permute-done.6.rest_1_), custom_call_target="tpu_custom_call" | custom-call | tf_op jit(solution)/shard_map/resid_owner/pallas_call | solution.py:658
  35.7 1.1 %collective-permute-done.7.rest_1_ = f32[176,128]{1,0:T(8,128)S(1)} collective-permute-done((f32[176,128]{1,0:T(8,128)S(1)}, f32[176,128]{1,0:T(8,128)S(1)}, u32[]{:S(2)}, u32[]{:S(2)}) %collective-permute-start.7) | collective-permute-done | bytes 90144 | tf_op jit(solution)/shard_map/ppermute | solution.py:692
  36.8 1.2 %collective-permute-done.8.rest_2_ = f32[176,128]{1,0:T(8,128)S(1)} collective-permute-done((f32[176,128]{1,0:T(8,128)S(1)}, f32[176,128]{1,0:T(8,128)S(1)}, u32[]{:S(2)}, u32[]{:S(2)}) %collective-permute-start.8) | collective-permute-done | bytes 90144 | tf_op jit(solution)/shard_map/ppermute | solution.py:692
  38.0 3.0 %collective-permute-done.9.rest_3_ = f32[176,128]{1,0:T(8,128)S(1)} collective-permute-done((f32[176,128]{1,0:T(8,128)S(1)}, f32[176,128]{1,0:T(8,128)S(1)}, u32[]{:S(2)}, u32[]{:S(2)}) %collective-permute-start.9) | collective-permute-done | bytes 90144 | tf_op jit(solution)/shard_map/ppermute | solution.py:692
  41.0 1.0 %owner.1 = (f32[2,1,4,128]{3,2,1,0:T(4,128)}, f32[2,8,1,4,128]{4,3,2,1,0:T(4,128)}, f32[2,8,2,8,256]{4,3,2,1,0:T(8,128)}) custom-call(f32[192,128]{1,0:T(8,128)S(1)} %get-tuple-element.46.mixes, f32[176,128]{1,0:T(8,128)S(1)} %get-tuple-element.45.after.rest_0_, f32[176,128]{1,0:T(8,128)S(1)} %collective-permute-done.7.rest_1_, ...), custom_call_target="tpu_custom_call" | custom-call | tf_op jit(solution)/shard_map/owner/pallas_call | solution.py:658
  (4 shorter events, 0.0 us)
Async XLA Ops:
  3.4 9.2 %collective-permute-start = (f32[240,128]{1,0:T(8,128)}, f32[240,128]{1,0:T(8,128)S(1)}, u32[]{:S(2)}, u32[]{:S(2)}) collective-permute-start(f32[240,128]{1,0:T(8,128)} %get-tuple-element.33), channel_id=1, source_target_pairs={{0,8},{8,16},{16,24},{24,0},{1,9},{9,17},{17,25},{25,1},{2,10},{10... | collective-permute-start | bytes 368648 | tf_op jit(solution)/shard_map/ppermute | solution.py:692
  4.8 10.2 %collective-permute-start.1 = (f32[240,128]{1,0:T(8,128)}, f32[240,128]{1,0:T(8,128)S(1)}, u32[]{:S(2)}, u32[]{:S(2)}) collective-permute-start(f32[240,128]{1,0:T(8,128)} %get-tuple-element.34), channel_id=1, source_target_pairs={{0,16},{8,24},{16,0},{24,8},{1,17},{9,25},{17,1},{25,9},{2,18},{10... | collective-permute-start | bytes 368648 | tf_op jit(solution)/shard_map/ppermute | solution.py:692
  5.9 11.8 %collective-permute-start.2 = (f32[240,128]{1,0:T(8,128)}, f32[240,128]{1,0:T(8,128)S(1)}, u32[]{:S(2)}, u32[]{:S(2)}) collective-permute-start(f32[240,128]{1,0:T(8,128)} %get-tuple-element.35), channel_id=1, source_target_pairs={{0,24},{8,0},{16,8},{24,16},{1,25},{9,1},{17,9},{25,17},{2,26},{10... | collective-permute-start | bytes 368648 | tf_op jit(solution)/shard_map/ppermute | solution.py:692
  9.6 1.0 %copy-start = (f32[512,128]{1,0:T(8,128)S(1)}, f32[512,128]{1,0:T(8,128)}, u32[]{:S(2)}) copy-start(f32[512,128]{1,0:T(8,128)} %prepare.1.block) | copy-start | bytes 786436
  10.5 0.9 %copy-start.1 = (f32[240,128]{1,0:T(8,128)S(1)}, f32[240,128]{1,0:T(8,128)}, u32[]{:S(2)}) copy-start(f32[240,128]{1,0:T(8,128)} %get-tuple-element.29.rest_8_.own) | copy-start | bytes 368644
  17.7 2.6 %collective-permute-start.3 = (f32[48,128]{1,0:T(8,128)S(1)}, f32[48,128]{1,0:T(8,128)S(1)}, u32[]{:S(2)}, u32[]{:S(2)}) collective-permute-start(f32[48,128]{1,0:T(8,128)S(1)} %relay.1), channel_id=1, source_target_pairs={{7,0},{0,1},{1,2},{2,3},{3,4},{4,5},{5,6},{6,7},{15,8},{8,9},{9,10... | collective-permute-start | bytes 73736 | tf_op jit(solution)/shard_map/ppermute | solution.py:734
  22.2 7.1 %collective-permute-start.4 = (f32[128,128]{1,0:T(8,128)S(1)}, f32[128,128]{1,0:T(8,128)S(1)}, u32[]{:S(2)}, u32[]{:S(2)}) collective-permute-start(f32[128,128]{1,0:T(8,128)S(1)} %get-tuple-element.40.one), channel_id=1, source_target_pairs={{0,16},{8,24},{16,0},{24,8},{1,17},{9,25},{17,1},{25,9},{2,18},{10... | collective-permute-start | bytes 196616 | tf_op jit(solution)/shard_map/ppermute | solution.py:740
  25.0 4.2 %collective-permute-start.5 = (f32[48,128]{1,0:T(8,128)S(1)}, f32[48,128]{1,0:T(8,128)S(1)}, u32[]{:S(2)}, u32[]{:S(2)}) collective-permute-start(f32[48,128]{1,0:T(8,128)S(1)} %get-tuple-element.44), channel_id=1, source_target_pairs={{0,7},{1,0},{2,1},{3,2},{4,3},{5,4},{6,5},{7,6},{8,15},{9,8},{10,9... | collective-permute-start | bytes 73736 | tf_op jit(solution)/shard_map/ppermute | solution.py:770
  29.3 5.6 %collective-permute-start.6 = (f32[256,128]{1,0:T(8,128)S(1)}, f32[256,128]{1,0:T(8,128)S(1)}, u32[]{:S(2)}, u32[]{:S(2)}) collective-permute-start(f32[256,128]{1,0:T(8,128)S(1)} %join.1.rest_0_), channel_id=1, source_target_pairs={{0,8},{8,0},{16,24},{24,16},{1,9},{9,1},{17,25},{25,17},{2,10},{10... | collective-permute-start | bytes 393224 | tf_op jit(solution)/shard_map/ppermute | solution.py:740
  29.6 7.2 %collective-permute-start.7 = (f32[176,128]{1,0:T(8,128)S(1)}, f32[176,128]{1,0:T(8,128)S(1)}, u32[]{:S(2)}, u32[]{:S(2)}) collective-permute-start(f32[176,128]{1,0:T(8,128)S(1)} %get-tuple-element.47), channel_id=1, source_target_pairs={{0,8},{8,16},{16,24},{24,0},{1,9},{9,17},{17,25},{25,1},{2,10},{10... | collective-permute-start | bytes 270344 | tf_op jit(solution)/shard_map/ppermute | solution.py:692
  30.4 7.7 %collective-permute-start.8 = (f32[176,128]{1,0:T(8,128)S(1)}, f32[176,128]{1,0:T(8,128)S(1)}, u32[]{:S(2)}, u32[]{:S(2)}) collective-permute-start(f32[176,128]{1,0:T(8,128)S(1)} %get-tuple-element.48), channel_id=1, source_target_pairs={{0,16},{8,24},{16,0},{24,8},{1,17},{9,25},{17,1},{25,9},{2,18},{10... | collective-permute-start | bytes 270344 | tf_op jit(solution)/shard_map/ppermute | solution.py:692
  32.9 8.1 %collective-permute-start.9 = (f32[176,128]{1,0:T(8,128)S(1)}, f32[176,128]{1,0:T(8,128)S(1)}, u32[]{:S(2)}, u32[]{:S(2)}) collective-permute-start(f32[176,128]{1,0:T(8,128)S(1)} %get-tuple-element.49), channel_id=1, source_target_pairs={{0,24},{8,0},{16,8},{24,16},{1,25},{9,1},{17,9},{25,17},{2,26},{10... | collective-permute-start | bytes 270344 | tf_op jit(solution)/shard_map/ppermute | solution.py:692

commit v6 on v5

--- a/solution.py
+++ b/solution.py
@@ -379,7 +379,7 @@
                     cells[pb, cell_rows(a, c, pr), :] = total
         return carry
 
-    lax.fori_loop(0, 8, fine_cells, 0)
+    lax.fori_loop(0, 4, lambda i, carry: fine_cells(2 * i + 1, fine_cells(2 * i, carry)), 0)
 
     radial = (4 * (lax.broadcasted_iota(jnp.int32, (h, b), 0) // s_count)).astype(F32)
 
@@ -398,15 +398,15 @@
         return x
 
     def positions(at, carry):
-        a, half = at // 2, lax.rem(at, 2)
+        a = at
         spots = []
-        for cb in range(2):
-            pb = 2 * half + cb
+        for pb in range(4):
+            cb = pb % 2
             rows = [cell_rows(a // 2, 4 * (f % 2) + 2 * lax.rem(a, 2) + cb, f // 2) for f in range(4)]
             emit = [pl.multiple_of(((pb * 4 + f) * 4 * ra + a) * h, 8) for f in range(4)]
             stars = [(star * 4 * ra + a) * 4 + pb for star in range(g.stars)]
             spots.append((pb, rows, emit, stars))
-        density = [[jnp.exp(cells[half, rows[f], :]) for f in range(4)] for _, rows, _, _ in spots]
+        density = [[jnp.exp(cells[pb // 2, rows[f], :]) for f in range(4)] for pb, rows, _, _ in spots]
         glow = [[spacing * emit_in[pl.ds(emit[f], h), :] for f in range(4)] for _, _, emit, _ in spots]
         bins = [[block[pl.ds(begins["bins"] + row, 1), :] for row in stars] for _, _, _, stars in spots]
         data = [[block[pl.ds(begins["data"] + row, 1), :] for row in stars] for _, _, _, stars in spots]
@@ -439,12 +439,12 @@
         for pb, star, residual in seen_at:
             for s in range(s_count):
                 seen[pb, pl.ds((s * g.stars + star) * 4 * ra + a, 1), :] = residual[s : s + 1]
-        for x, (_, rows, _, _) in enumerate(spots):
+        for x, (pb, rows, _, _) in enumerate(spots):
             for f in range(4):
-                cells[half, rows[f], :] = -density[x][f] * total[x][f]
+                cells[pb // 2, rows[f], :] = -density[x][f] * total[x][f]
         return carry
 
-    lax.fori_loop(0, 8 * ra, positions, 0)
+    lax.fori_loop(0, 4 * ra, positions, 0)
 
     shown = None
     for phase in range(4):
@@ -482,7 +482,7 @@
                     tall[pr + dr, row, bi] += value
             return carry
 
-        lax.fori_loop(0, 8, gather, 0)
+        lax.fori_loop(0, 4, lambda i, carry: gather(2 * i + 1, gather(2 * i, carry)), 0)
     for row in range(rows_a):
         for pr in range(2):
             for pb in range(2):

time: 42.3 us -> 42 us (level)
  no operation moved by 1% of the time
where the time goes in v6:
time: 42 us; the launch traced here: 41.8 us
  waiting for transfers between devices  17.1 us (41%)
  Pallas kernels  11.1 us (26%)
  starting transfers between devices  11.1 us (26%)
  local copies, waits for them, and re-layouts  1.85 us (4%)
  between operations  0.72 us (2%)
    pallas_call x12, Pallas kernels, call(): pl.pallas_call(kernel, name=name, out_shape=[jax.ShapeDtypeStruct(shape,...  11.1 us
    ppermute x6, waiting for transfers between devices, exchange(): lax.ppermute(blocks[k], 'rad', [(i, (i + k) % n) for i in range(n)])  10.5 us
    ppermute x6, starting transfers between devices, exchange(): lax.ppermute(blocks[k], 'rad', [(i, (i + k) % n) for i in range(n)])  7.13 us
    ppermute x1, waiting for transfers between devices, per_device(): edge = lax.ppermute(edge, ('rad', 'ang'), sideways)  3.74 us
    ppermute x2, starting transfers between devices, everywhere(): got = lax.ppermute(block, 'rad', [(i, i ^ bit) for i in range(n)])  2.26 us
    ppermute x2, waiting for transfers between devices, everywhere(): got = lax.ppermute(block, 'rad', [(i, i ^ bit) for i in range(n)])  1.97 us
    unnamed x4, local copies, waits for them, and re-layouts  1.85 us
    ppermute x1, starting transfers between devices, per_device(): near = lax.ppermute(near, ('rad', 'ang'), inward)  1.64 us
  transfers between devices with their start and end apart: 10, of which 8 were waited for; matrix products, arithmetic and copies ran while one was open for 0% of the time, Pallas kernels for 13%

profile of v6, /device:TPU:11, one launch (start us, length us, event | category | flops | bytes accessed | tf_op | source)
XLA Modules:
  0.0 41.8 jit_solution(8215166785524395695)
XLA Ops:
  0.6 2.8 %scatter.1 = (f32[240,128]{1,0:T(8,128)}, f32[240,128]{1,0:T(8,128)}, f32[240,128]{1,0:T(8,128)}, f32[240,128]{1,0:T(8,128)}) custom-call(f32[4,16,512]{2,1,0:T(8,128)} %rest_0_.2, s32[4]{0:T(128)} %rest_0_.3, f32[8,8,16]{2,1,0:T(8,128)} %bitcast.2, f32[2,1,4,128]{3,2,1,0:T(4,128)} %rest_3_.1, f32[2,8,1,4,128]{4,3,2,1,0:T(4,128)} %rest_4_.2, s32[8]{0:T(128)} %rest_1_.3, ...), custom_call_target="tpu_custom_call" | custom-call | tf_op jit(solution)/shard_map/scatter/pallas_call | solution.py:658
  3.4 1.4 %collective-permute-start = (f32[240,128]{1,0:T(8,128)}, f32[240,128]{1,0:T(8,128)S(1)}, u32[]{:S(2)}, u32[]{:S(2)}) collective-permute-start(f32[240,128]{1,0:T(8,128)} %get-tuple-element.33), channel_id=1, source_target_pairs={{0,8},{8,16},{16,24},{24,0},{1,9},{9,17},{17,25},{25,1},{2,10},{10... | collective-permute-start | bytes 368648 | tf_op jit(solution)/shard_map/ppermute | solution.py:692
  4.8 1.1 %collective-permute-start.1 = (f32[240,128]{1,0:T(8,128)}, f32[240,128]{1,0:T(8,128)S(1)}, u32[]{:S(2)}, u32[]{:S(2)}) collective-permute-start(f32[240,128]{1,0:T(8,128)} %get-tuple-element.34), channel_id=1, source_target_pairs={{0,16},{8,24},{16,0},{24,8},{1,17},{9,25},{17,1},{25,9},{2,18},{10... | collective-permute-start | bytes 368648 | tf_op jit(solution)/shard_map/ppermute | solution.py:692
  5.9 1.4 %collective-permute-start.2 = (f32[240,128]{1,0:T(8,128)}, f32[240,128]{1,0:T(8,128)S(1)}, u32[]{:S(2)}, u32[]{:S(2)}) collective-permute-start(f32[240,128]{1,0:T(8,128)} %get-tuple-element.35), channel_id=1, source_target_pairs={{0,24},{8,0},{16,8},{24,16},{1,25},{9,1},{17,9},{25,17},{2,26},{10... | collective-permute-start | bytes 368648 | tf_op jit(solution)/shard_map/ppermute | solution.py:692
  7.3 2.3 %prepare.1.block = f32[512,128]{1,0:T(8,128)} custom-call(s32[4]{0:T(128)} %rest_0_.3, s32[8]{0:T(128)} %rest_1_.3, f32[8,8,16]{2,1,0:T(8,128)} %bitcast.3, f32[8,8,16]{2,1,0:T(8,128)} %bitcast.5, f32[16,8,27]{2,1,0:T(8,128)} %rest_4_.3, f32[16,8,27]{2,1,0:T(8,128)} %rest_5_.3, s32[4,16,512]{2,1,0:T(8,128)} %rest_6_.1, f32[4,16,512]{2,1,0:T(8,128)} %rest_7_.3, ...), custom_call_target="tpu_custom_call" | custom-call | tf_op jit(solution)/shard_map/prepare/pallas_call | solution.py:658
  9.6 0.0 copy-start
  9.6 0.9 %copy-done = f32[512,128]{1,0:T(8,128)S(1)} copy-done((f32[512,128]{1,0:T(8,128)S(1)}, f32[512,128]{1,0:T(8,128)}, u32[]{:S(2)}) %copy-start) | copy-done | bytes 262168
  10.5 0.9 %copy-done.1 = f32[240,128]{1,0:T(8,128)S(1)} copy-done((f32[240,128]{1,0:T(8,128)S(1)}, f32[240,128]{1,0:T(8,128)}, u32[]{:S(2)}) %copy-start.1) | copy-done | bytes 122904
  11.4 1.2 %weights.1 = (f32[648,8,128]{2,1,0:T(8,128)S(1)}, f32[240,128]{1,0:T(8,128)S(1)}, f32[512,128]{1,0:T(8,128)S(1)}) custom-call(f32[512,128]{1,0:T(8,128)S(1)} %copy-done, f32[240,128]{1,0:T(8,128)S(1)} %copy-done.1), custom_call_target="tpu_custom_call" | custom-call | tf_op jit(solution)/shard_map/weights/pallas_call | solution.py:658
  12.6 0.0 collective-permute-done.rest_1_
  12.6 2.4 %collective-permute-done.1.rest_2_ = f32[240,128]{1,0:T(8,128)S(1)} collective-permute-done((f32[240,128]{1,0:T(8,128)}, f32[240,128]{1,0:T(8,128)S(1)}, u32[]{:S(2)}, u32[]{:S(2)}) %collective-permute-start.1) | collective-permute-done | bytes 122912 | tf_op jit(solution)/shard_map/ppermute | solution.py:692
  15.0 2.7 %collective-permute-done.2.rest_3_ = f32[240,128]{1,0:T(8,128)S(1)} collective-permute-done((f32[240,128]{1,0:T(8,128)}, f32[240,128]{1,0:T(8,128)S(1)}, u32[]{:S(2)}, u32[]{:S(2)}) %collective-permute-start.2) | collective-permute-done | bytes 122912 | tf_op jit(solution)/shard_map/ppermute | solution.py:692
  17.7 1.6 %collective-permute-start.3 = (f32[48,128]{1,0:T(8,128)S(1)}, f32[48,128]{1,0:T(8,128)S(1)}, u32[]{:S(2)}, u32[]{:S(2)}) collective-permute-start(f32[48,128]{1,0:T(8,128)S(1)} %relay.1), channel_id=1, source_target_pairs={{7,0},{0,1},{1,2},{2,3},{3,4},{4,5},{5,6},{6,7},{15,8},{8,9},{9,10... | collective-permute-start | bytes 73736 | tf_op jit(solution)/shard_map/ppermute | solution.py:734
  19.4 0.1 unpack.1
  19.5 0.8 %collective-permute-done.3.rest_4_ = f32[48,128]{1,0:T(8,128)S(1)} collective-permute-done((f32[48,128]{1,0:T(8,128)S(1)}, f32[48,128]{1,0:T(8,128)S(1)}, u32[]{:S(2)}, u32[]{:S(2)}) %collective-permute-start.3) | collective-permute-done | bytes 24608 | tf_op jit(solution)/shard_map/ppermute | solution.py:734
  20.3 1.6 %forward.1 = (f32[2,256,128]{2,1,0:T(8,128)S(1)}, f32[128,128]{1,0:T(8,128)S(1)}) custom-call(f32[512,128]{1,0:T(8,128)S(1)} %get-tuple-element.30.block, f32[648,8,128]{2,1,0:T(8,128)S(1)} %get-tuple-element.31.spread, f32[512,128]{1,0:T(8,128)S(1)} %get-tuple-element.36.rest_0_, f32[512,128]{1,0:T(8,128)S(1)} %get-tuple-element.37.rest_1_, ...), custom_call_target="tpu_custom_call" | custom-call | tf_op jit(solution)/shard_map/forward/pallas_call | solution.py:658
  21.9 1.9 %collective-permute-start.4 = (f32[128,128]{1,0:T(8,128)S(1)}, f32[128,128]{1,0:T(8,128)S(1)}, u32[]{:S(2)}, u32[]{:S(2)}) collective-permute-start(f32[128,128]{1,0:T(8,128)S(1)} %get-tuple-element.40.one), channel_id=1, source_target_pairs={{0,16},{8,24},{16,0},{24,8},{1,17},{9,25},{17,1},{25,9},{2,18},{10... | collective-permute-start | bytes 196616 | tf_op jit(solution)/shard_map/ppermute | solution.py:740
  23.9 0.8 %backward.1 = (f32[128,128]{1,0:T(8,128)S(1)}, f32[40,128]{1,0:T(8,128)S(1)}, f32[48,128]{1,0:T(8,128)S(1)}) custom-call(f32[648,8,128]{2,1,0:T(8,128)S(1)} %get-tuple-element.31.spread, f32[2,256,128]{2,1,0:T(8,128)S(1)} %get-tuple-element.41.cells), custom_call_target="tpu_custom_call" | custom-call | tf_op jit(solution)/shard_map/backward/pallas_call | solution.py:658
  24.7 0.1 collective-permute-start.5
  24.8 0.4 lanes.1.field
  25.2 3.7 %collective-permute-done.5.edge_ref = f32[48,128]{1,0:T(8,128)S(1)} collective-permute-done((f32[48,128]{1,0:T(8,128)S(1)}, f32[48,128]{1,0:T(8,128)S(1)}, u32[]{:S(2)}, u32[]{:S(2)}) %collective-permute-start.5) | collective-permute-done | bytes 24608 | tf_op jit(solution)/shard_map/ppermute | solution.py:770
  28.9 0.1 sums.1
  29.0 0.3 collective-permute-start.6
  29.3 0.8 %collective-permute-start.7 = (f32[176,128]{1,0:T(8,128)S(1)}, f32[176,128]{1,0:T(8,128)S(1)}, u32[]{:S(2)}, u32[]{:S(2)}) collective-permute-start(f32[176,128]{1,0:T(8,128)S(1)} %get-tuple-element.47), channel_id=1, source_target_pairs={{0,8},{8,16},{16,24},{24,0},{1,9},{9,17},{17,25},{25,1},{2,10},{10... | collective-permute-start | bytes 270344 | tf_op jit(solution)/shard_map/ppermute | solution.py:692
  30.1 2.5 %collective-permute-start.8 = (f32[176,128]{1,0:T(8,128)S(1)}, f32[176,128]{1,0:T(8,128)S(1)}, u32[]{:S(2)}, u32[]{:S(2)}) collective-permute-start(f32[176,128]{1,0:T(8,128)S(1)} %get-tuple-element.48), channel_id=1, source_target_pairs={{0,16},{8,24},{16,0},{24,8},{1,17},{9,25},{17,1},{25,9},{2,18},{10... | collective-permute-start | bytes 270344 | tf_op jit(solution)/shard_map/ppermute | solution.py:692
  32.6 0.0 collective-permute-start.9
  32.6 2.0 %collective-permute-done.6.rest_1_ = f32[256,128]{1,0:T(8,128)S(1)} collective-permute-done((f32[256,128]{1,0:T(8,128)S(1)}, f32[256,128]{1,0:T(8,128)S(1)}, u32[]{:S(2)}, u32[]{:S(2)}) %collective-permute-start.6) | collective-permute-done | bytes 131104 | tf_op jit(solution)/shard_map/ppermute | solution.py:740
  34.6 0.8 %resid_owner.1 = (f32[2,4,16,512]{3,2,1,0:T(8,128)}, f32[192,128]{1,0:T(8,128)S(1)}) custom-call(f32[512,128]{1,0:T(8,128)S(1)} %get-tuple-element.30.block, f32[256,128]{1,0:T(8,128)S(1)} %join.1.rest_0_, f32[256,128]{1,0:T(8,128)S(1)} %collective-permute-done.6.rest_1_), custom_call_target="tpu_custom_call" | custom-call | tf_op jit(solution)/shard_map/resid_owner/pallas_call | solution.py:658
  35.4 1.1 %collective-permute-done.7.rest_1_ = f32[176,128]{1,0:T(8,128)S(1)} collective-permute-done((f32[176,128]{1,0:T(8,128)S(1)}, f32[176,128]{1,0:T(8,128)S(1)}, u32[]{:S(2)}, u32[]{:S(2)}) %collective-permute-start.7) | collective-permute-done | bytes 90144 | tf_op jit(solution)/shard_map/ppermute | solution.py:692
  36.5 1.2 %collective-permute-done.8.rest_2_ = f32[176,128]{1,0:T(8,128)S(1)} collective-permute-done((f32[176,128]{1,0:T(8,128)S(1)}, f32[176,128]{1,0:T(8,128)S(1)}, u32[]{:S(2)}, u32[]{:S(2)}) %collective-permute-start.8) | collective-permute-done | bytes 90144 | tf_op jit(solution)/shard_map/ppermute | solution.py:692
  37.7 3.1 %collective-permute-done.9.rest_3_ = f32[176,128]{1,0:T(8,128)S(1)} collective-permute-done((f32[176,128]{1,0:T(8,128)S(1)}, f32[176,128]{1,0:T(8,128)S(1)}, u32[]{:S(2)}, u32[]{:S(2)}) %collective-permute-start.9) | collective-permute-done | bytes 90144 | tf_op jit(solution)/shard_map/ppermute | solution.py:692
  40.8 1.0 %owner.1 = (f32[2,1,4,128]{3,2,1,0:T(4,128)}, f32[2,8,1,4,128]{4,3,2,1,0:T(4,128)}, f32[2,8,2,8,256]{4,3,2,1,0:T(8,128)}) custom-call(f32[192,128]{1,0:T(8,128)S(1)} %get-tuple-element.46.mixes, f32[176,128]{1,0:T(8,128)S(1)} %get-tuple-element.45.after.rest_0_, f32[176,128]{1,0:T(8,128)S(1)} %collective-permute-done.7.rest_1_, ...), custom_call_target="tpu_custom_call" | custom-call | tf_op jit(solution)/shard_map/owner/pallas_call | solution.py:658
  (4 shorter events, 0.0 us)
Async XLA Ops:
  3.4 9.2 %collective-permute-start = (f32[240,128]{1,0:T(8,128)}, f32[240,128]{1,0:T(8,128)S(1)}, u32[]{:S(2)}, u32[]{:S(2)}) collective-permute-start(f32[240,128]{1,0:T(8,128)} %get-tuple-element.33), channel_id=1, source_target_pairs={{0,8},{8,16},{16,24},{24,0},{1,9},{9,17},{17,25},{25,1},{2,10},{10... | collective-permute-start | bytes 368648 | tf_op jit(solution)/shard_map/ppermute | solution.py:692
  4.8 10.2 %collective-permute-start.1 = (f32[240,128]{1,0:T(8,128)}, f32[240,128]{1,0:T(8,128)S(1)}, u32[]{:S(2)}, u32[]{:S(2)}) collective-permute-start(f32[240,128]{1,0:T(8,128)} %get-tuple-element.34), channel_id=1, source_target_pairs={{0,16},{8,24},{16,0},{24,8},{1,17},{9,25},{17,1},{25,9},{2,18},{10... | collective-permute-start | bytes 368648 | tf_op jit(solution)/shard_map/ppermute | solution.py:692
  5.9 11.8 %collective-permute-start.2 = (f32[240,128]{1,0:T(8,128)}, f32[240,128]{1,0:T(8,128)S(1)}, u32[]{:S(2)}, u32[]{:S(2)}) collective-permute-start(f32[240,128]{1,0:T(8,128)} %get-tuple-element.35), channel_id=1, source_target_pairs={{0,24},{8,0},{16,8},{24,16},{1,25},{9,1},{17,9},{25,17},{2,26},{10... | collective-permute-start | bytes 368648 | tf_op jit(solution)/shard_map/ppermute | solution.py:692
  9.6 1.0 %copy-start = (f32[512,128]{1,0:T(8,128)S(1)}, f32[512,128]{1,0:T(8,128)}, u32[]{:S(2)}) copy-start(f32[512,128]{1,0:T(8,128)} %prepare.1.block) | copy-start | bytes 786436
  10.5 0.9 %copy-start.1 = (f32[240,128]{1,0:T(8,128)S(1)}, f32[240,128]{1,0:T(8,128)}, u32[]{:S(2)}) copy-start(f32[240,128]{1,0:T(8,128)} %get-tuple-element.29.rest_8_.own) | copy-start | bytes 368644
  17.7 2.6 %collective-permute-start.3 = (f32[48,128]{1,0:T(8,128)S(1)}, f32[48,128]{1,0:T(8,128)S(1)}, u32[]{:S(2)}, u32[]{:S(2)}) collective-permute-start(f32[48,128]{1,0:T(8,128)S(1)} %relay.1), channel_id=1, source_target_pairs={{7,0},{0,1},{1,2},{2,3},{3,4},{4,5},{5,6},{6,7},{15,8},{8,9},{9,10... | collective-permute-start | bytes 73736 | tf_op jit(solution)/shard_map/ppermute | solution.py:734
  21.9 7.0 %collective-permute-start.4 = (f32[128,128]{1,0:T(8,128)S(1)}, f32[128,128]{1,0:T(8,128)S(1)}, u32[]{:S(2)}, u32[]{:S(2)}) collective-permute-start(f32[128,128]{1,0:T(8,128)S(1)} %get-tuple-element.40.one), channel_id=1, source_target_pairs={{0,16},{8,24},{16,0},{24,8},{1,17},{9,25},{17,1},{25,9},{2,18},{10... | collective-permute-start | bytes 196616 | tf_op jit(solution)/shard_map/ppermute | solution.py:740
  24.7 4.2 %collective-permute-start.5 = (f32[48,128]{1,0:T(8,128)S(1)}, f32[48,128]{1,0:T(8,128)S(1)}, u32[]{:S(2)}, u32[]{:S(2)}) collective-permute-start(f32[48,128]{1,0:T(8,128)S(1)} %get-tuple-element.44), channel_id=1, source_target_pairs={{0,7},{1,0},{2,1},{3,2},{4,3},{5,4},{6,5},{7,6},{8,15},{9,8},{10,9... | collective-permute-start | bytes 73736 | tf_op jit(solution)/shard_map/ppermute | solution.py:770
  29.0 5.6 %collective-permute-start.6 = (f32[256,128]{1,0:T(8,128)S(1)}, f32[256,128]{1,0:T(8,128)S(1)}, u32[]{:S(2)}, u32[]{:S(2)}) collective-permute-start(f32[256,128]{1,0:T(8,128)S(1)} %join.1.rest_0_), channel_id=1, source_target_pairs={{0,8},{8,0},{16,24},{24,16},{1,9},{9,1},{17,25},{25,17},{2,10},{10... | collective-permute-start | bytes 393224 | tf_op jit(solution)/shard_map/ppermute | solution.py:740
  29.3 7.2 %collective-permute-start.7 = (f32[176,128]{1,0:T(8,128)S(1)}, f32[176,128]{1,0:T(8,128)S(1)}, u32[]{:S(2)}, u32[]{:S(2)}) collective-permute-start(f32[176,128]{1,0:T(8,128)S(1)} %get-tuple-element.47), channel_id=1, source_target_pairs={{0,8},{8,16},{16,24},{24,0},{1,9},{9,17},{17,25},{25,1},{2,10},{10... | collective-permute-start | bytes 270344 | tf_op jit(solution)/shard_map/ppermute | solution.py:692
  30.1 7.6 %collective-permute-start.8 = (f32[176,128]{1,0:T(8,128)S(1)}, f32[176,128]{1,0:T(8,128)S(1)}, u32[]{:S(2)}, u32[]{:S(2)}) collective-permute-start(f32[176,128]{1,0:T(8,128)S(1)} %get-tuple-element.48), channel_id=1, source_target_pairs={{0,16},{8,24},{16,0},{24,8},{1,17},{9,25},{17,1},{25,9},{2,18},{10... | collective-permute-start | bytes 270344 | tf_op jit(solution)/shard_map/ppermute | solution.py:692
  32.6 8.2 %collective-permute-start.9 = (f32[176,128]{1,0:T(8,128)S(1)}, f32[176,128]{1,0:T(8,128)S(1)}, u32[]{:S(2)}, u32[]{:S(2)}) collective-permute-start(f32[176,128]{1,0:T(8,128)S(1)} %get-tuple-element.49), channel_id=1, source_target_pairs={{0,24},{8,0},{16,8},{24,16},{1,25},{9,1},{17,9},{25,17},{2,26},{10... | collective-permute-start | bytes 270344 | tf_op jit(solution)/shard_map/ppermute | solution.py:692

commit v7 on v6

--- a/solution.py
+++ b/solution.py
@@ -321,8 +321,8 @@
     def weight_at(level, c, o):
         return spread[(level * 8 + c) * 27 + o]
 
-    mix_in[...] = mixed[...]
-    coarse_in[...] = coarse[...]
+    mix_in[...] = mixed[: 4 * rows_a * h]
+    coarse_in[...] = coarse[: (ra + 4) * h]
     live = jnp.where(worker < g.w // 2, ang > 0, ang < g.m - 1)
     for q in range(g.w):
         @pl.when(worker == q)
@@ -730,9 +730,9 @@
         (block, sent[0]),
         [],
     )
-    (near,) = call(kernel(relay_kernel, g), "relay", [((6 * h, b), F32)], got, [])
+    (near,) = call(kernel(relay_kernel, g), "relay", [((7 * h, b), F32)], got, [])
     near = lax.ppermute(near, ("rad", "ang"), inward)
-    parts = [(64 * ra * h, b), (64 * ra * h, b), (4 * rows_a * h, b), ((ra + 4) * h, b)]
+    parts = [((x + 1) * h, b) for x in (64 * ra, 64 * ra, 4 * rows_a, ra + 4)]
     unpacked = call(kernel(unpack_kernel, g), "unpack", [(part, F32) for part in parts], got, [])
     def everywhere(block, after):
         ids, bit = [0], n // 2

time: 42 us -> 42 us (level)
  no operation moved by 1% of the time
where the time goes in v7:
time: 42 us; the launch traced here: 41.8 us
  waiting for transfers between devices  17.1 us (41%)
  starting transfers between devices  11.1 us (26%)
  Pallas kernels  11 us (26%)
  local copies, waits for them, and re-layouts  1.85 us (4%)
  between operations  0.72 us (2%)
    pallas_call x12, Pallas kernels, call(): pl.pallas_call(kernel, name=name, out_shape=[jax.ShapeDtypeStruct(shape,...  11 us
    ppermute x6, waiting for transfers between devices, exchange(): lax.ppermute(blocks[k], 'rad', [(i, (i + k) % n) for i in range(n)])  10.5 us
    ppermute x6, starting transfers between devices, exchange(): lax.ppermute(blocks[k], 'rad', [(i, (i + k) % n) for i in range(n)])  7.13 us
    ppermute x1, waiting for transfers between devices, per_device(): edge = lax.ppermute(edge, ('rad', 'ang'), sideways)  3.74 us
    ppermute x2, starting transfers between devices, everywhere(): got = lax.ppermute(block, 'rad', [(i, i ^ bit) for i in range(n)])  2.27 us
    ppermute x2, waiting for transfers between devices, everywhere(): got = lax.ppermute(block, 'rad', [(i, i ^ bit) for i in range(n)])  1.97 us
    unnamed x4, local copies, waits for them, and re-layouts  1.85 us
    ppermute x1, starting transfers between devices, per_device(): near = lax.ppermute(near, ('rad', 'ang'), inward)  1.64 us
  transfers between devices with their start and end apart: 10, of which 8 were waited for; matrix products, arithmetic and copies ran while one was open for 0% of the time, Pallas kernels for 13%

profile of v7, /device:TPU:11, one launch (start us, length us, event | category | flops | bytes accessed | tf_op | source)
XLA Modules:
  0.0 41.8 jit_solution(4629913125481083000)
XLA Ops:
  0.6 2.8 %scatter.1 = (f32[240,128]{1,0:T(8,128)}, f32[240,128]{1,0:T(8,128)}, f32[240,128]{1,0:T(8,128)}, f32[240,128]{1,0:T(8,128)}) custom-call(f32[4,16,512]{2,1,0:T(8,128)} %rest_0_.2, s32[4]{0:T(128)} %rest_0_.3, f32[8,8,16]{2,1,0:T(8,128)} %bitcast.2, f32[2,1,4,128]{3,2,1,0:T(4,128)} %rest_3_.1, f32[2,8,1,4,128]{4,3,2,1,0:T(4,128)} %rest_4_.2, s32[8]{0:T(128)} %rest_1_.3, ...), custom_call_target="tpu_custom_call" | custom-call | tf_op jit(solution)/shard_map/scatter/pallas_call | solution.py:658
  3.4 1.4 %collective-permute-start = (f32[240,128]{1,0:T(8,128)}, f32[240,128]{1,0:T(8,128)S(1)}, u32[]{:S(2)}, u32[]{:S(2)}) collective-permute-start(f32[240,128]{1,0:T(8,128)} %get-tuple-element.33), channel_id=1, source_target_pairs={{0,8},{8,16},{16,24},{24,0},{1,9},{9,17},{17,25},{25,1},{2,10},{10... | collective-permute-start | bytes 368648 | tf_op jit(solution)/shard_map/ppermute | solution.py:692
  4.8 1.1 %collective-permute-start.1 = (f32[240,128]{1,0:T(8,128)}, f32[240,128]{1,0:T(8,128)S(1)}, u32[]{:S(2)}, u32[]{:S(2)}) collective-permute-start(f32[240,128]{1,0:T(8,128)} %get-tuple-element.34), channel_id=1, source_target_pairs={{0,16},{8,24},{16,0},{24,8},{1,17},{9,25},{17,1},{25,9},{2,18},{10... | collective-permute-start | bytes 368648 | tf_op jit(solution)/shard_map/ppermute | solution.py:692
  5.9 1.4 %collective-permute-start.2 = (f32[240,128]{1,0:T(8,128)}, f32[240,128]{1,0:T(8,128)S(1)}, u32[]{:S(2)}, u32[]{:S(2)}) collective-permute-start(f32[240,128]{1,0:T(8,128)} %get-tuple-element.35), channel_id=1, source_target_pairs={{0,24},{8,0},{16,8},{24,16},{1,25},{9,1},{17,9},{25,17},{2,26},{10... | collective-permute-start | bytes 368648 | tf_op jit(solution)/shard_map/ppermute | solution.py:692
  7.3 2.3 %prepare.1.block = f32[512,128]{1,0:T(8,128)} custom-call(s32[4]{0:T(128)} %rest_0_.3, s32[8]{0:T(128)} %rest_1_.3, f32[8,8,16]{2,1,0:T(8,128)} %bitcast.3, f32[8,8,16]{2,1,0:T(8,128)} %bitcast.5, f32[16,8,27]{2,1,0:T(8,128)} %rest_4_.3, f32[16,8,27]{2,1,0:T(8,128)} %rest_5_.3, s32[4,16,512]{2,1,0:T(8,128)} %rest_6_.1, f32[4,16,512]{2,1,0:T(8,128)} %rest_7_.3, ...), custom_call_target="tpu_custom_call" | custom-call | tf_op jit(solution)/shard_map/prepare/pallas_call | solution.py:658
  9.6 0.0 copy-start
  9.6 0.9 %copy-done = f32[512,128]{1,0:T(8,128)S(1)} copy-done((f32[512,128]{1,0:T(8,128)S(1)}, f32[512,128]{1,0:T(8,128)}, u32[]{:S(2)}) %copy-start) | copy-done | bytes 262168
  10.5 0.9 %copy-done.1 = f32[240,128]{1,0:T(8,128)S(1)} copy-done((f32[240,128]{1,0:T(8,128)S(1)}, f32[240,128]{1,0:T(8,128)}, u32[]{:S(2)}) %copy-start.1) | copy-done | bytes 122904
  11.4 1.2 %weights.1 = (f32[648,8,128]{2,1,0:T(8,128)S(1)}, f32[240,128]{1,0:T(8,128)S(1)}, f32[512,128]{1,0:T(8,128)S(1)}) custom-call(f32[512,128]{1,0:T(8,128)S(1)} %copy-done, f32[240,128]{1,0:T(8,128)S(1)} %copy-done.1), custom_call_target="tpu_custom_call" | custom-call | tf_op jit(solution)/shard_map/weights/pallas_call | solution.py:658
  12.6 2.4 %collective-permute-done.1.rest_2_ = f32[240,128]{1,0:T(8,128)S(1)} collective-permute-done((f32[240,128]{1,0:T(8,128)}, f32[240,128]{1,0:T(8,128)S(1)}, u32[]{:S(2)}, u32[]{:S(2)}) %collective-permute-start.1) | collective-permute-done | bytes 122912 | tf_op jit(solution)/shard_map/ppermute | solution.py:692
  15.0 2.7 %collective-permute-done.2.rest_3_ = f32[240,128]{1,0:T(8,128)S(1)} collective-permute-done((f32[240,128]{1,0:T(8,128)}, f32[240,128]{1,0:T(8,128)S(1)}, u32[]{:S(2)}, u32[]{:S(2)}) %collective-permute-start.2) | collective-permute-done | bytes 122912 | tf_op jit(solution)/shard_map/ppermute | solution.py:692
  17.7 1.6 %collective-permute-start.3 = (f32[56,128]{1,0:T(8,128)S(1)}, f32[56,128]{1,0:T(8,128)S(1)}, u32[]{:S(2)}, u32[]{:S(2)}) collective-permute-start(f32[56,128]{1,0:T(8,128)S(1)} %relay.1), channel_id=1, source_target_pairs={{7,0},{0,1},{1,2},{2,3},{3,4},{4,5},{5,6},{6,7},{15,8},{8,9},{9,10... | collective-permute-start | bytes 86024 | tf_op jit(solution)/shard_map/ppermute | solution.py:734
  19.4 0.1 unpack.1
  19.5 0.9 %collective-permute-done.3.rest_4_ = f32[56,128]{1,0:T(8,128)S(1)} collective-permute-done((f32[56,128]{1,0:T(8,128)S(1)}, f32[56,128]{1,0:T(8,128)S(1)}, u32[]{:S(2)}, u32[]{:S(2)}) %collective-permute-start.3) | collective-permute-done | bytes 28704 | tf_op jit(solution)/shard_map/ppermute | solution.py:734
  20.4 1.6 %forward.1 = (f32[2,256,128]{2,1,0:T(8,128)S(1)}, f32[128,128]{1,0:T(8,128)S(1)}) custom-call(f32[512,128]{1,0:T(8,128)S(1)} %get-tuple-element.30.block, f32[648,8,128]{2,1,0:T(8,128)S(1)} %get-tuple-element.31.spread, f32[520,128]{1,0:T(8,128)S(1)} %get-tuple-element.36.rest_0_, f32[520,128]{1,0:T(8,128)S(1)} %get-tuple-element.37.rest_1_, ...), custom_call_target="tpu_custom_call" | custom-call | tf_op jit(solution)/shard_map/forward/pallas_call | solution.py:658
  21.9 2.0 %collective-permute-start.4 = (f32[128,128]{1,0:T(8,128)S(1)}, f32[128,128]{1,0:T(8,128)S(1)}, u32[]{:S(2)}, u32[]{:S(2)}) collective-permute-start(f32[128,128]{1,0:T(8,128)S(1)} %get-tuple-element.40.one), channel_id=1, source_target_pairs={{0,16},{8,24},{16,0},{24,8},{1,17},{9,25},{17,1},{25,9},{2,18},{10... | collective-permute-start | bytes 196616 | tf_op jit(solution)/shard_map/ppermute | solution.py:740
  23.9 0.8 %backward.1 = (f32[128,128]{1,0:T(8,128)S(1)}, f32[40,128]{1,0:T(8,128)S(1)}, f32[48,128]{1,0:T(8,128)S(1)}) custom-call(f32[648,8,128]{2,1,0:T(8,128)S(1)} %get-tuple-element.31.spread, f32[2,256,128]{2,1,0:T(8,128)S(1)} %get-tuple-element.41.cells), custom_call_target="tpu_custom_call" | custom-call | tf_op jit(solution)/shard_map/backward/pallas_call | solution.py:658
  24.7 0.1 collective-permute-start.5
  24.8 0.4 lanes.1.field
  25.1 3.7 %collective-permute-done.5.edge_ref = f32[48,128]{1,0:T(8,128)S(1)} collective-permute-done((f32[48,128]{1,0:T(8,128)S(1)}, f32[48,128]{1,0:T(8,128)S(1)}, u32[]{:S(2)}, u32[]{:S(2)}) %collective-permute-start.5) | collective-permute-done | bytes 24608 | tf_op jit(solution)/shard_map/ppermute | solution.py:770
  28.9 0.1 sums.1
  29.0 0.0 collective-permute-done.4.two
  29.0 0.3 collective-permute-start.6
  29.3 0.8 %collective-permute-start.7 = (f32[176,128]{1,0:T(8,128)S(1)}, f32[176,128]{1,0:T(8,128)S(1)}, u32[]{:S(2)}, u32[]{:S(2)}) collective-permute-start(f32[176,128]{1,0:T(8,128)S(1)} %get-tuple-element.47), channel_id=1, source_target_pairs={{0,8},{8,16},{16,24},{24,0},{1,9},{9,17},{17,25},{25,1},{2,10},{10... | collective-permute-start | bytes 270344 | tf_op jit(solution)/shard_map/ppermute | solution.py:692
  30.1 2.5 %collective-permute-start.8 = (f32[176,128]{1,0:T(8,128)S(1)}, f32[176,128]{1,0:T(8,128)S(1)}, u32[]{:S(2)}, u32[]{:S(2)}) collective-permute-start(f32[176,128]{1,0:T(8,128)S(1)} %get-tuple-element.48), channel_id=1, source_target_pairs={{0,16},{8,24},{16,0},{24,8},{1,17},{9,25},{17,1},{25,9},{2,18},{10... | collective-permute-start | bytes 270344 | tf_op jit(solution)/shard_map/ppermute | solution.py:692
  32.6 0.0 collective-permute-start.9
  32.6 2.0 %collective-permute-done.6.rest_1_ = f32[256,128]{1,0:T(8,128)S(1)} collective-permute-done((f32[256,128]{1,0:T(8,128)S(1)}, f32[256,128]{1,0:T(8,128)S(1)}, u32[]{:S(2)}, u32[]{:S(2)}) %collective-permute-start.6) | collective-permute-done | bytes 131104 | tf_op jit(solution)/shard_map/ppermute | solution.py:740
  34.6 0.8 %resid_owner.1 = (f32[2,4,16,512]{3,2,1,0:T(8,128)}, f32[192,128]{1,0:T(8,128)S(1)}) custom-call(f32[512,128]{1,0:T(8,128)S(1)} %get-tuple-element.30.block, f32[256,128]{1,0:T(8,128)S(1)} %join.1.rest_0_, f32[256,128]{1,0:T(8,128)S(1)} %collective-permute-done.6.rest_1_), custom_call_target="tpu_custom_call" | custom-call | tf_op jit(solution)/shard_map/resid_owner/pallas_call | solution.py:658
  35.4 1.1 %collective-permute-done.7.rest_1_ = f32[176,128]{1,0:T(8,128)S(1)} collective-permute-done((f32[176,128]{1,0:T(8,128)S(1)}, f32[176,128]{1,0:T(8,128)S(1)}, u32[]{:S(2)}, u32[]{:S(2)}) %collective-permute-start.7) | collective-permute-done | bytes 90144 | tf_op jit(solution)/shard_map/ppermute | solution.py:692
  36.5 1.1 %collective-permute-done.8.rest_2_ = f32[176,128]{1,0:T(8,128)S(1)} collective-permute-done((f32[176,128]{1,0:T(8,128)S(1)}, f32[176,128]{1,0:T(8,128)S(1)}, u32[]{:S(2)}, u32[]{:S(2)}) %collective-permute-start.8) | collective-permute-done | bytes 90144 | tf_op jit(solution)/shard_map/ppermute | solution.py:692
  37.6 3.1 %collective-permute-done.9.rest_3_ = f32[176,128]{1,0:T(8,128)S(1)} collective-permute-done((f32[176,128]{1,0:T(8,128)S(1)}, f32[176,128]{1,0:T(8,128)S(1)}, u32[]{:S(2)}, u32[]{:S(2)}) %collective-permute-start.9) | collective-permute-done | bytes 90144 | tf_op jit(solution)/shard_map/ppermute | solution.py:692
  40.8 1.0 %owner.1 = (f32[2,1,4,128]{3,2,1,0:T(4,128)}, f32[2,8,1,4,128]{4,3,2,1,0:T(4,128)}, f32[2,8,2,8,256]{4,3,2,1,0:T(8,128)}) custom-call(f32[192,128]{1,0:T(8,128)S(1)} %get-tuple-element.46.mixes, f32[176,128]{1,0:T(8,128)S(1)} %get-tuple-element.45.after.rest_0_, f32[176,128]{1,0:T(8,128)S(1)} %collective-permute-done.7.rest_1_, ...), custom_call_target="tpu_custom_call" | custom-call | tf_op jit(solution)/shard_map/owner/pallas_call | solution.py:658
  (4 shorter events, 0.0 us)
Async XLA Ops:
  3.4 9.2 %collective-permute-start = (f32[240,128]{1,0:T(8,128)}, f32[240,128]{1,0:T(8,128)S(1)}, u32[]{:S(2)}, u32[]{:S(2)}) collective-permute-start(f32[240,128]{1,0:T(8,128)} %get-tuple-element.33), channel_id=1, source_target_pairs={{0,8},{8,16},{16,24},{24,0},{1,9},{9,17},{17,25},{25,1},{2,10},{10... | collective-permute-start | bytes 368648 | tf_op jit(solution)/shard_map/ppermute | solution.py:692
  4.8 10.2 %collective-permute-start.1 = (f32[240,128]{1,0:T(8,128)}, f32[240,128]{1,0:T(8,128)S(1)}, u32[]{:S(2)}, u32[]{:S(2)}) collective-permute-start(f32[240,128]{1,0:T(8,128)} %get-tuple-element.34), channel_id=1, source_target_pairs={{0,16},{8,24},{16,0},{24,8},{1,17},{9,25},{17,1},{25,9},{2,18},{10... | collective-permute-start | bytes 368648 | tf_op jit(solution)/shard_map/ppermute | solution.py:692
  5.9 11.8 %collective-permute-start.2 = (f32[240,128]{1,0:T(8,128)}, f32[240,128]{1,0:T(8,128)S(1)}, u32[]{:S(2)}, u32[]{:S(2)}) collective-permute-start(f32[240,128]{1,0:T(8,128)} %get-tuple-element.35), channel_id=1, source_target_pairs={{0,24},{8,0},{16,8},{24,16},{1,25},{9,1},{17,9},{25,17},{2,26},{10... | collective-permute-start | bytes 368648 | tf_op jit(solution)/shard_map/ppermute | solution.py:692
  9.6 1.0 %copy-start = (f32[512,128]{1,0:T(8,128)S(1)}, f32[512,128]{1,0:T(8,128)}, u32[]{:S(2)}) copy-start(f32[512,128]{1,0:T(8,128)} %prepare.1.block) | copy-start | bytes 786436
  10.5 0.9 %copy-start.1 = (f32[240,128]{1,0:T(8,128)S(1)}, f32[240,128]{1,0:T(8,128)}, u32[]{:S(2)}) copy-start(f32[240,128]{1,0:T(8,128)} %get-tuple-element.29.rest_8_.own) | copy-start | bytes 368644
  17.7 2.6 %collective-permute-start.3 = (f32[56,128]{1,0:T(8,128)S(1)}, f32[56,128]{1,0:T(8,128)S(1)}, u32[]{:S(2)}, u32[]{:S(2)}) collective-permute-start(f32[56,128]{1,0:T(8,128)S(1)} %relay.1), channel_id=1, source_target_pairs={{7,0},{0,1},{1,2},{2,3},{3,4},{4,5},{5,6},{6,7},{15,8},{8,9},{9,10... | collective-permute-start | bytes 86024 | tf_op jit(solution)/shard_map/ppermute | solution.py:734
  21.9 7.0 %collective-permute-start.4 = (f32[128,128]{1,0:T(8,128)S(1)}, f32[128,128]{1,0:T(8,128)S(1)}, u32[]{:S(2)}, u32[]{:S(2)}) collective-permute-start(f32[128,128]{1,0:T(8,128)S(1)} %get-tuple-element.40.one), channel_id=1, source_target_pairs={{0,16},{8,24},{16,0},{24,8},{1,17},{9,25},{17,1},{25,9},{2,18},{10... | collective-permute-start | bytes 196616 | tf_op jit(solution)/shard_map/ppermute | solution.py:740
  24.7 4.2 %collective-permute-start.5 = (f32[48,128]{1,0:T(8,128)S(1)}, f32[48,128]{1,0:T(8,128)S(1)}, u32[]{:S(2)}, u32[]{:S(2)}) collective-permute-start(f32[48,128]{1,0:T(8,128)S(1)} %get-tuple-element.44), channel_id=1, source_target_pairs={{0,7},{1,0},{2,1},{3,2},{4,3},{5,4},{6,5},{7,6},{8,15},{9,8},{10,9... | collective-permute-start | bytes 73736 | tf_op jit(solution)/shard_map/ppermute | solution.py:770
  29.0 5.6 %collective-permute-start.6 = (f32[256,128]{1,0:T(8,128)S(1)}, f32[256,128]{1,0:T(8,128)S(1)}, u32[]{:S(2)}, u32[]{:S(2)}) collective-permute-start(f32[256,128]{1,0:T(8,128)S(1)} %join.1.rest_0_), channel_id=1, source_target_pairs={{0,8},{8,0},{16,24},{24,16},{1,9},{9,1},{17,25},{25,17},{2,10},{10... | collective-permute-start | bytes 393224 | tf_op jit(solution)/shard_map/ppermute | solution.py:740
  29.3 7.2 %collective-permute-start.7 = (f32[176,128]{1,0:T(8,128)S(1)}, f32[176,128]{1,0:T(8,128)S(1)}, u32[]{:S(2)}, u32[]{:S(2)}) collective-permute-start(f32[176,128]{1,0:T(8,128)S(1)} %get-tuple-element.47), channel_id=1, source_target_pairs={{0,8},{8,16},{16,24},{24,0},{1,9},{9,17},{17,25},{25,1},{2,10},{10... | collective-permute-start | bytes 270344 | tf_op jit(solution)/shard_map/ppermute | solution.py:692
  30.1 7.6 %collective-permute-start.8 = (f32[176,128]{1,0:T(8,128)S(1)}, f32[176,128]{1,0:T(8,128)S(1)}, u32[]{:S(2)}, u32[]{:S(2)}) collective-permute-start(f32[176,128]{1,0:T(8,128)S(1)} %get-tuple-element.48), channel_id=1, source_target_pairs={{0,16},{8,24},{16,0},{24,8},{1,17},{9,25},{17,1},{25,9},{2,18},{10... | collective-permute-start | bytes 270344 | tf_op jit(solution)/shard_map/ppermute | solution.py:692
  32.6 8.2 %collective-permute-start.9 = (f32[176,128]{1,0:T(8,128)S(1)}, f32[176,128]{1,0:T(8,128)S(1)}, u32[]{:S(2)}, u32[]{:S(2)}) collective-permute-start(f32[176,128]{1,0:T(8,128)S(1)} %get-tuple-element.49), channel_id=1, source_target_pairs={{0,24},{8,0},{16,8},{24,16},{1,25},{9,1},{17,9},{25,17},{2,26},{10... | collective-permute-start | bytes 270344 | tf_op jit(solution)/shard_map/ppermute | solution.py:692
